TPU v7x, 512 devices: a whole 4x8x8 slice. The times are simulated.
512 devices in a mesh: dp: 16 (over z, x_hi), wide: 32 (over y, x_lo, core).
Axes of the slice: x: 4 (x_hi: 2, x_lo: 2; x = x_hi * 2 + x_lo), y: 8, z: 8, core: 2. Of those that a mesh axis runs over, the one named last changes fastest.
Arguments:
- activations: bfloat16 [65536, 16384], P(('dp', 'wide')), may hold values from -24 to 24
- output_gradients: bfloat16 [65536, 256], P(('dp', 'wide')), may hold values from -0.0234375 to 0.0234375
- frozen_span_rows: bfloat16 [4, 2, 64, 16384], P(None, None, 'wide'), may hold values from -0.046875 to 0.046875
- span_owner_slab: int32 [4], replicated, may hold values from 0 to 3, each once
- adapter_down_factor: bfloat16 [16384, 64], P('wide'), may hold values from -0.046875 to 0.046875
- adapter_up_factor: bfloat16 [64, 256], replicated, may hold values from -0.75 to 0.75
- completion_token_counts: int32 [1024], P(('dp', 'wide')), may hold values from 1 to 64
- balance_slot_plan: int32 [16, 4096], P('dp'), may hold values from 0 to 4095, as said below
Outputs:
- adapter_down_gradient: float32 [16384, 64], P('wide')
- adapter_up_gradient: float32 [64, 256], replicated
Inputs may be any that keep to these rules, and one draw needn't show every extreme that they name: `balance_slot_plan`: for each replica, a permutation of the 4096 slots; slot s lies on device s // 128 of wide, and every device of wide sends exactly 4 of its rows to every device of wide.
All inputs are finite; a program needn't handle non-finite values.
Results may differ from a plain program's by a relative error of at most 0.0095.
Values may be sent and summed in bfloat16 or wider, within the bound.
No kernel may reach another device: no remote copies, remote signals or barrier semaphores. Data moves between devices by JAX's collectives and lax.ppermute only.
A program may use at most 128 MiB of HBM per device.

v0:
```python
import jax
import jax.numpy as jnp
from jax import lax
from jax.sharding import PartitionSpec as P


def slot_orders(plan_row, device_index, rows, lanes):
    mine = lax.dynamic_slice_in_dim(plan_row, device_index * rows, rows, 0)
    send_order = jnp.argsort(mine)
    everyone = jnp.arange(lanes * rows, dtype=jnp.int32)
    source_of = jnp.zeros_like(plan_row).at[plan_row].set(everyone)
    my_sources = lax.dynamic_slice_in_dim(source_of, device_index * rows, rows, 0)
    local_slots = jnp.arange(rows, dtype=jnp.int32)
    recv_order = jnp.argsort(my_sources // rows * rows + local_slots)
    return (send_order, recv_order)


def shards(
    activations,
    output_gradients,
    frozen_span_rows,
    span_owner_slab,
    adapter_down_factor,
    adapter_up_factor,
    completion_token_counts,
    balance_slot_plan,
):
    rows, width = activations.shape
    rank_index = adapter_down_factor.shape[1]
    lanes = lax.axis_size("wide")
    device_index = lax.axis_index("wide")
    seg_rows = rows // completion_token_counts.shape[0]
    position = jnp.arange(rows, dtype=jnp.int32)
    live_rows = position % seg_rows < jnp.repeat(
        completion_token_counts, seg_rows, total_repeat_length=rows
    )
    masked_rows = jnp.where(live_rows[:, None], activations, jnp.zeros_like(activations))
    send_order, recv_order = slot_orders(balance_slot_plan[0], device_index, rows, lanes)
    returned = lax.all_to_all(
        output_gradients[recv_order], "wide", split_axis=0, concat_axis=0, tiled=True
    )
    cotangent = returned[jnp.argsort(send_order)]
    span_count = frozen_span_rows.shape[0]
    unit_share = frozen_span_rows.shape[2]
    all_units = unit_share * lanes
    empty = jnp.zeros((2, rows, span_count, all_units), jnp.float32)
    products = jnp.einsum(
        "sd,cjkd->jsck",
        masked_rows,
        lax.all_gather(frozen_span_rows, "wide", axis=2, tiled=True),
        preferred_element_type=jnp.float32,
    )
    stored = lax.dynamic_update_slice_in_dim(empty, products, jnp.int32(0), 3)
    ordered_rows = jnp.take(stored, span_owner_slab, axis=2).reshape(
        2, rows, span_count * all_units
    )
    span_piece = lax.all_gather(adapter_down_factor, "wide", axis=0, tiled=True)
    columns = lax.slice_in_dim(masked_rows, 0, span_piece.shape[0], axis=1)
    adapter_product = (
        jnp.zeros((rows, rank_index), jnp.float32)
        + jnp.dot(columns, span_piece, preferred_element_type=jnp.float32)
    ).astype(jnp.bfloat16)
    gate_preactivation = ordered_rows[0] + jnp.dot(
        adapter_product, adapter_up_factor, preferred_element_type=jnp.float32
    )
    up_preactivation = ordered_rows[1]
    sigmoid_gate = jax.nn.sigmoid(gate_preactivation)
    gate_gradient = (
        cotangent.astype(jnp.float32)
        * up_preactivation
        * sigmoid_gate
        * (1.0 + gate_preactivation * (1.0 - sigmoid_gate))
    ).astype(jnp.bfloat16)
    contract_rows = (((0,), (0,)), ((), ()))
    up_partial = lax.dot_general(
        adapter_product, gate_gradient, contract_rows, preferred_element_type=jnp.float32
    )
    adapter_product_gradient = jnp.dot(
        gate_gradient, adapter_up_factor.T, preferred_element_type=jnp.float32
    ).astype(jnp.bfloat16)
    down_partial = lax.dot_general(
        masked_rows, adapter_product_gradient, contract_rows, preferred_element_type=jnp.float32
    )
    rounded = lax.optimization_barrier(down_partial.astype(jnp.bfloat16)).astype(jnp.float32)
    row_share = lax.psum_scatter(rounded, "wide", scatter_dimension=0, tiled=True)
    down_grad = lax.psum(row_share, "dp")
    up_grad = lax.psum(up_partial, ("dp", "wide"))
    return (down_grad, up_grad)


def solution(mesh):
    placed = (
        P(("dp", "wide"), None),
        P(("dp", "wide"), None),
        P(None, None, "wide", None),
        P(),
        P("wide", None),
        P(),
        P(("dp", "wide")),
        P("dp", None),
    )
    return jax.shard_map(
        shards, mesh=mesh, in_specs=placed, out_specs=(P("wide", None), P()), check_vma=False
    )
```

profile of v0, /device:TPU:6, one launch (start us, length us, event | category | flops | bytes accessed | tf_op | source)
XLA Modules:
  0.0 777.8 jit_solution(8432636298132844008)
XLA Ops:
  7.2 0.0 copy-start
  7.2 0.0 all-gather.5.cloned.1.call-start
  7.2 0.7 all-gather.5.cloned.1.call-update
  7.9 0.0 all-gather.3.cloned.1.call-start
  8.0 2.2 copy.14
  10.2 0.0 all-gather.3.cloned.1.call-update
  10.2 0.7 compare_select_fusion
  11.0 15.5 %scatter_custom_fusion = s32[4096]{0:T(1024)S(1)} fusion(s32[4096]{0:T(1024)S(1)} %bitcast.29, s32[4096]{0:T(1024)S(1)} %iota.22, s32[]{:T(128)} %constant.123.clone.1), kind=kCustom, calls=%fused_computation.16 | custom fusion | bytes 16388 | tf_op jit(solution)/shard_map/scatter | solution.py:11
  26.5 0.1 iota_add_fusion
  26.6 2.5 sort.45
  29.2 0.0 copy-done
  29.2 0.8 gather_fusion
  30.0 0.7 all_to_all.8
  30.7 8.7 %all-to-all-start = ((bf16[32,4,256]{2,1,0:T(4,128)(2,1)}), bf16[32,4,256]{2,1,0:T(4,128)(2,1)S(1)}, u32[]{:S(2)}, u32[]{:S(2)}) async-start(bf16[32,4,256]{2,1,0:T(4,128)(2,1)} %all_to_all.8), calls=%async_computation | async-start | bytes 131072 | tf_op jit(solution)/shard_map/all_to_all | solution.py:39
  39.4 0.0 reduce-scatter.2.cloned.1.call-start
  39.4 0.7 dynamic-slice_bitcast_fusion
  40.1 2.5 sort.46
  42.6 2.5 sort.47
  45.2 1.3 fusion.12
  46.5 0.7 compare_select_fusion.1
  47.2 0.7 compare_and_fusion
  47.8 1.9 fusion.10
  49.8 0.0 all-to-all-done
  49.8 0.8 gather_fusion.1
  50.7 32.5 %all-gather.5.cloned.1.call-done = bf16[16384,64]{0,1:T(8,128)(2,1)} async-done(((bf16[512,64]{0,1:T(8,128)(2,1)}), bf16[16384,64]{0,1:T(8,128)(2,1)}) %all-gather.5.cloned.1.call-update) | async-done | bytes 2097168 | tf_op jit(solution)/shard_map/all_gather | solution.py:57
  83.1 4.5 convolution_convert_fusion.2
  87.6 0.0 copy-start.1
  87.6 99.3 %all-gather.3.cloned.1.call-done = bf16[4,2,64,16384]{3,0,1,2:T(4,128)(2,1)} async-done(((bf16[4,2,2,16384]{3,0,1,2:T(4,128)(2,1)}), bf16[4,2,64,16384]{3,0,1,2:T(4,128)(2,1)}) %all-gather.3.cloned.1.call-update) | async-done | bytes 16777232 | tf_op jit(solution)/shard_map/all_gather | solution.py:50
  187.0 28.6 %fusion.3 = f32[2,128,4,64]{1,3,0,2:T(8,128)S(1)} fusion(bf16[4,2,64,16384]{3,0,1,2:T(4,128)(2,1)} %all-gather.3.cloned.1.call-done, bf16[128,16384]{1,0:T(8,128)(2,1)} %param.10, pred[128]{0:T(512)(128)(4,1)S(1)} %fusion.10), kind=kOutput, calls=%fused_computation.9 | convolution fusion | flops 2149580800 | bytes 21233792 | tf_op jit(solution)/shard_map/sd,cjkd->jsck/dot_general | solution.py:47
  215.6 0.6 gather_fusion.2
  216.2 0.1 select_bitcast_fusion
  216.3 0.1 copy.17
  216.4 0.1 copy.16
  216.5 0.0 copy-done.1
  216.5 0.2 multiply_convert_fusion
  216.8 3.0 convolution_convert_fusion
  219.8 2.2 convert_element_type.23
  222.0 0.0 reduce-scatter.2.cloned.1.call-update
  222.0 0.0 all-reduce.5.cloned.1.call-start
  222.1 0.8 fusion.13
  222.9 0.0 all-reduce.5.cloned.1.call-update
  222.9 0.0 all-reduce.3.cloned.1.call-start
  222.9 120.9 %reduce-scatter.2.cloned.1.call-done = f32[512,64]{0,1:T(8,128)} async-done(((f32[16384,64]{0,1:T(8,128)}), f32[512,64]{0,1:T(8,128)}) %reduce-scatter.2.cloned.1.call-update) | async-done | bytes 131088 | tf_op jit(solution)/shard_map/reduce_scatter | solution.py:85
  343.8 0.0 all-reduce.3.cloned.1.call-update
  343.8 263.4 %all-reduce.5.cloned.1.call-done = f32[64,256]{1,0:T(8,128)} async-done(((f32[64,256]{1,0:T(8,128)}), f32[64,256]{1,0:T(8,128)}) %all-reduce.5.cloned.1.call-update) | async-done | bytes 65552 | tf_op jit(solution)/shard_map/psum | solution.py:87
  607.2 161.0 %all-reduce.3.cloned.1.call-done = f32[512,64]{0,1:T(8,128)} async-done(((f32[512,64]{0,1:T(8,128)}), f32[512,64]{0,1:T(8,128)}) %all-reduce.3.cloned.1.call-update) | async-done | bytes 131088 | tf_op jit(solution)/shard_map/psum | solution.py:86
  768.2 1.6 copy.25
  769.8 1.5 copy.26
  (11 shorter events, 0.1 us)
Async XLA Ops:
  7.2 22.0 %copy-start = (bf16[128,256]{1,0:T(8,128)(2,1)S(1)}, bf16[128,256]{1,0:T(8,128)(2,1)}, u32[]{:S(2)}) copy-start(bf16[128,256]{1,0:T(8,128)(2,1)} %param.11) | copy-start | bytes 196612
  7.2 75.9 %all-gather.5.cloned.1.call-start = ((), (), s32[]{:S(2)}) async-start(), calls=%async_computation.3 | async-start | bytes 2162688 | tf_op jit(solution)/shard_map/all_gather | solution.py:57
  7.9 179.1 %all-gather.3.cloned.1.call-start = ((), (), s32[]{:S(2)}) async-start(), calls=%async_computation.2 | async-start | bytes 17301504 | tf_op jit(solution)/shard_map/all_gather | solution.py:50
  30.7 19.1 %all-to-all-start = ((bf16[32,4,256]{2,1,0:T(4,128)(2,1)}), bf16[32,4,256]{2,1,0:T(4,128)(2,1)S(1)}, u32[]{:S(2)}, u32[]{:S(2)}) async-start(bf16[32,4,256]{2,1,0:T(4,128)(2,1)} %all_to_all.8), calls=%async_computation | async-start | bytes 131072 | tf_op jit(solution)/shard_map/all_to_all | solution.py:39
  39.4 304.4 %reduce-scatter.2.cloned.1.call-start = ((), (), s32[]{:S(2)}) async-start(), calls=%async_computation.4 | async-start | bytes 4325376 | tf_op jit(solution)/shard_map/reduce_scatter | solution.py:85
  87.6 128.9 %copy-start.1 = (bf16[64,256]{1,0:T(8,128)(2,1)S(1)}, bf16[64,256]{1,0:T(8,128)(2,1)}, u32[]{:S(2)}) copy-start(bf16[64,256]{1,0:T(8,128)(2,1)} %param.15) | copy-start | bytes 98308
  222.0 385.2 %all-reduce.5.cloned.1.call-start = ((), (), s32[]{:S(2)}) async-start(), calls=%async_computation.6 | async-start | bytes 131072 | tf_op jit(solution)/shard_map/psum | solution.py:87
  222.9 545.3 %all-reduce.3.cloned.1.call-start = ((), (), s32[]{:S(2)}) async-start(), calls=%async_computation.5 | async-start | bytes 262144 | tf_op jit(solution)/shard_map/psum | solution.py:86
Sparse Core Ops, SparseCore 0:
  10.2 72.9 all-gather.4
  85.3 101.6 all-gather.2
  222.2 121.5 reduce-scatter.1
  349.2 257.9 all-reduce.4
  610.2 157.9 all-reduce.2
where the time goes:
time: 778 us
  waiting for transfers between devices  678 us (87%)
  matrix products  37.2 us (5%)
  local copies, waits for them, and re-layouts  25.9 us (3%)
  other arithmetic  14 us (2%)
  between operations  13.9 us (2%)
  starting transfers between devices  8.92 us (1%)
    psum x1, waiting for transfers between devices, shards(): up_grad = lax.psum(up_partial, ('dp', 'wide'))  263 us
    psum x1, waiting for transfers between devices, shards(): down_grad = lax.psum(row_share, 'dp')  161 us
    reduce_scatter x1, waiting for transfers between devices, shards(): lax.psum_scatter(rounded, 'wide', scatter_dimension=0, tiled=True)  121 us
    all_gather x1, waiting for transfers between devices, shards(): lax.all_gather(frozen_span_rows, 'wide', axis=2, tiled=True)  99.3 us
    all_gather x1, waiting for transfers between devices, shards(): span_piece = lax.all_gather(adapter_down_factor, 'wide', axis=0, tiled=True)  32.5 us
    dot_general x1, matrix products, shards(): jnp.einsum('sd,cjkd->jsck', masked_rows, lax.all_gather(frozen_span_rows,...  28.6 us
  transfers between devices with their start and end apart: 6, of which 5 were waited for; matrix products, arithmetic and copies ran while one was open for 5% of the time, Pallas kernels for 0%

commit v1 on v0

v1 whole, which is shorter than its diff:
```python
import functools

import jax
import jax.numpy as jnp
from jax import lax
from jax.experimental import pallas as pl
from jax.experimental.pallas import tpu as pltpu
from jax.sharding import Mesh
from jax.sharding import PartitionSpec as P

F32 = jnp.float32
BF16 = jnp.bfloat16
DP = ("z", "xh")
WIDE = ("y", "xl", "core")
RING = ("xh", "xl")
REPLICAS = ("z", "xh", "y")
EVERY = ("z", "xh", "y", "xl", "core")
VMEM_LIMIT = 40 * 1024 * 1024
NT = (((1,), (1,)), ((), ()))
TN = (((0,), (0,)), ((), ()))


def shift(array, axes, step):
    size = lax.axis_size(axes)
    return lax.ppermute(array, axes, [(i, (i + step) % size) for i in range(size)])


def exchange(array, axes):
    return lax.all_to_all(array, axes, split_axis=0, concat_axis=0, tiled=True)


def params():
    return pltpu.CompilerParams(vmem_limit_bytes=VMEM_LIMIT)


def split_rows_kernel(core_ref, x_ref, own_a, own_b, other_a, other_b, *, block):
    core = core_ref[0]
    half = x_ref.shape[0] // 2
    for xl in range(2):
        mine = pl.multiple_of(xl * 2 * block + core * block, block)
        his = pl.multiple_of(xl * 2 * block + (1 - core) * block, block)
        own_a[xl, 0] = x_ref[:half, pl.ds(mine, block)]
        own_b[xl, 0] = x_ref[half:, pl.ds(mine, block)]
        other_a[xl, 0] = x_ref[:half, pl.ds(his, block)]
        other_b[xl, 0] = x_ref[half:, pl.ds(his, block)]


def split_rows(x, core, ys, block):
    rows, width = x.shape
    half = rows // 2
    shape = jax.ShapeDtypeStruct((2, ys // 4, half, 4 * block), BF16)
    spec = pl.BlockSpec((2, 1, half, block), lambda y, c: (0, y // 4, 0, y % 4))
    parts = pl.pallas_call(
        functools.partial(split_rows_kernel, block=block),
        grid_spec=pltpu.PrefetchScalarGridSpec(
            num_scalar_prefetch=1,
            grid=(ys,),
            in_specs=[pl.BlockSpec((rows, 4 * block), lambda y, c: (0, y))],
            out_specs=[spec] * 4,
        ),
        out_shape=[shape] * 4,
        compiler_params=params(),
        cost_estimate=pl.CostEstimate(flops=0, bytes_accessed=rows * width * 4, transcendentals=0),
        name="split_rows",
    )(core, x)
    return [part.reshape(2 * (ys // 4), half, 4 * block) for part in parts]


def split_weights_kernel(w_ref, out_ref, *, block):
    spans, _, units, _ = w_ref.shape
    rows = jnp.concatenate(
        [w_ref[s, j].astype(F32) for j in range(2) for s in range(spans)], axis=0
    ).astype(BF16)
    for parity in range(2):
        for xl in range(2):
            at = (xl * 2 + parity) * block
            out_ref[parity, xl, 0] = rows[:, at : at + block]


def split_weights(w, ys, block):
    spans, _, units, width = w.shape
    n = 2 * spans * units
    out = pl.pallas_call(
        functools.partial(split_weights_kernel, block=block),
        grid=(ys,),
        in_specs=[pl.BlockSpec((spans, 2, units, 4 * block), lambda y: (0, 0, 0, y))],
        out_specs=pl.BlockSpec((2, 2, 1, n, block), lambda y: (0, 0, y // 4, 0, y % 4)),
        out_shape=jax.ShapeDtypeStruct((2, 2, ys // 4, n, 4 * block), BF16),
        compiler_params=params(),
        cost_estimate=pl.CostEstimate(flops=0, bytes_accessed=w.size * 4, transcendentals=0),
        name="split_weights",
    )(w)
    return out.reshape(2, 2 * (ys // 4), n, 4 * block)


def products_kernel(*refs, block):
    x_refs, (w_ref, down_ref, out_ref) = refs[:8], refs[8:]
    x = jnp.concatenate([r[0] for r in x_refs], axis=0)
    w = w_ref[...].reshape(-1, w_ref.shape[-1])
    down = jnp.concatenate(
        [
            jnp.concatenate(
                [down_ref[y, :, t * block : (t + 1) * block] for t in range(4)], axis=0
            )
            for y in range(4)
        ],
        axis=1,
    )
    units = w.shape[0]
    wide = lax.dot_general(x, w, NT, preferred_element_type=F32)
    low = lax.dot_general(x, down, NT, preferred_element_type=F32)

    @pl.when(pl.program_id(0) == 0)
    def _():
        out_ref[:, :units] = wide
        out_ref[:, units:] = low

    @pl.when(pl.program_id(0) > 0)
    def _():
        out_ref[:, :units] += wide
        out_ref[:, units:] += low


def products(xs, gathered, n, rank, block):
    chunks, part, lanes = xs[0].shape
    ys = gathered.shape[0]
    units = ys * 2 * n
    x_spec = pl.BlockSpec((1, part, lanes), lambda k: (k, 0, 0))
    per = chunks // 2
    return pl.pallas_call(
        functools.partial(products_kernel, block=block),
        grid=(chunks,),
        in_specs=[x_spec] * 8
        + [
            pl.BlockSpec((ys, 2 * n, lanes), lambda k: (0, k, 0)),
            pl.BlockSpec((4, rank // 4, lanes), lambda k: (k % per, 2 * chunks + k // per, 0)),
        ],
        out_specs=pl.BlockSpec((8 * part, units + rank), lambda k: (0, 0)),
        out_shape=jax.ShapeDtypeStruct((8 * part, units + rank), F32),
        compiler_params=params(),
        cost_estimate=pl.CostEstimate(
            flops=2 * 8 * part * chunks * lanes * (units + rank),
            bytes_accessed=(8 * part + units + rank) * chunks * lanes * 2,
            transcendentals=0,
        ),
        name="products",
    )(*xs, gathered, gathered)


def swap_pairs(ref, part):
    return jnp.concatenate(
        [ref[(i ^ 1) * part : ((i ^ 1) + 1) * part] for i in range(8)], axis=0
    )


def gate_kernel(mine_ref, his_ref, cot_ref, pick_ref, up_ref, low_ref, up_grad_ref, *, n, part):
    units = pick_ref.shape[1]
    total = mine_ref[...] + swap_pairs(his_ref, part)
    low = total[:, units:].astype(BF16)
    pick = pick_ref[...]
    up = jnp.dot(up_ref[...], pick, preferred_element_type=F32).astype(BF16)
    cot = jnp.dot(cot_ref[...], pick, preferred_element_type=F32)
    both = total[:, :units]
    gate = both + jnp.dot(low, up, preferred_element_type=F32)
    upper = pltpu.roll(both, units - n // 2, 1)
    s = jax.nn.sigmoid(gate)
    grad = (cot * upper * s * (1.0 + gate * (1.0 - s))).astype(BF16)
    low_ref[...] = lax.dot_general(grad, up, NT, preferred_element_type=F32)
    ordered = lax.dot_general(grad, pick, NT, preferred_element_type=F32).astype(BF16)
    first = [i for i in range(8) if i % 2 == 0]
    low_m = jnp.concatenate([low[i * part : (i + 1) * part] for i in first], axis=0)
    ordered_m = jnp.concatenate([ordered[i * part : (i + 1) * part] for i in first], axis=0)
    up_grad_ref[...] = lax.dot_general(low_m, ordered_m, TN, preferred_element_type=F32)


def gate_stage(mine, his, cot, pick, up, n):
    rows = mine.shape[0]
    rank, hidden = up.shape
    vm = pl.BlockSpec(memory_space=pltpu.VMEM)
    return pl.pallas_call(
        functools.partial(gate_kernel, n=n, part=rows // 8),
        in_specs=[vm] * 5,
        out_specs=[vm, vm],
        out_shape=[
            jax.ShapeDtypeStruct((rows, rank), F32),
            jax.ShapeDtypeStruct((rank, hidden), F32),
        ],
        compiler_params=params(),
        cost_estimate=pl.CostEstimate(
            flops=2 * rows * hidden * (2 * hidden + 3 * rank),
            bytes_accessed=rows * hidden * 12,
            transcendentals=rows * hidden,
        ),
        name="gate_stage",
    )(mine, his, cot, pick, up)


def down_kernel(xl_ref, *refs):
    x_refs, (mine_ref, plus_ref, minus_ref, out_ref) = refs[:8], refs[8:]
    half = plus_ref.shape[0]
    low = jnp.concatenate(
        [mine_ref[:half] + plus_ref[...], mine_ref[half:] + minus_ref[...]], axis=0
    ).astype(BF16)
    x = jnp.concatenate([r[0] for r in x_refs], axis=0)
    out_ref[0] = lax.dot_general(low, x, TN, preferred_element_type=F32).astype(BF16)


def down_terms(xs, xl, mine, plus, minus, ys, block):
    chunks, part, lanes = xs[0].shape
    per = chunks // 2
    rows, rank = mine.shape
    x_spec = pl.BlockSpec((1, part, block), lambda y, v: (v[0] * per + y // 4, 0, y % 4))
    full = pl.BlockSpec((rows, rank), lambda y, v: (0, 0))
    half = pl.BlockSpec((rows // 2, rank), lambda y, v: (0, 0))
    return pl.pallas_call(
        down_kernel,
        grid_spec=pltpu.PrefetchScalarGridSpec(
            num_scalar_prefetch=1,
            grid=(ys,),
            in_specs=[x_spec] * 8 + [full, half, half],
            out_specs=pl.BlockSpec((1, rank, block), lambda y, v: (y, 0, 0)),
        ),
        out_shape=jax.ShapeDtypeStruct((ys, rank, block), BF16),
        compiler_params=params(),
        cost_estimate=pl.CostEstimate(
            flops=2 * rows * rank * ys * block,
            bytes_accessed=(rows + rank) * ys * block * 2,
            transcendentals=0,
        ),
        name="down_terms",
    )(xl, *xs, mine, plus, minus)


def chosen(condition):
    return condition.astype(BF16)


def cotangent_rows(grads, plan, counts, place):
    rows = grads.shape[0]
    lanes = lax.axis_size(WIDE)
    seg = rows // counts.shape[0]
    local = jnp.arange(rows, dtype=jnp.int32)
    slots = lax.dynamic_slice_in_dim(plan, place * rows, rows, 0)
    rank = jnp.sum((slots[None, :] < slots[:, None]).astype(jnp.int32), axis=1)
    owner = jnp.arange(plan.shape[0], dtype=jnp.int32) // rows
    held = plan[None, :] == (place * rows + local)[:, None]
    source = jnp.sum(jnp.where(held, owner[None, :], 0), axis=1)
    before = (source[None, :] == source[:, None]) & (local[None, :] < local[:, None])
    spot = source * (rows // lanes) + jnp.sum(before.astype(jnp.int32), axis=1)
    sent = jnp.dot(
        chosen(spot[None, :] == local[:, None]), grads, preferred_element_type=F32
    ).astype(BF16)
    back = exchange(sent, WIDE)
    live = local % seg < jnp.repeat(counts, seg, total_repeat_length=rows)
    pick = (rank[:, None] == local[None, :]) & live[:, None]
    return jnp.dot(chosen(pick), back, preferred_element_type=F32).astype(BF16)


def unit_order(slab, xl, ys, n, hidden):
    spans = slab.shape[0]
    per_span = hidden // spans
    units = n // (2 * spans)
    at = jnp.arange(ys * 2 * n, dtype=jnp.int32)
    y, core = at // (2 * n), at // n % 2
    gate, span, unit = at // (n // 2) % 2 == 0, at // units % spans, at % units
    k = ((y * 2 + xl) * 2 + core) * units + unit
    h = jnp.arange(hidden, dtype=jnp.int32)
    stored = jnp.repeat(slab, per_span, total_repeat_length=hidden)
    return chosen(
        gate[None, :]
        & (stored[:, None] == span[None, :])
        & ((h % per_span)[:, None] == k[None, :])
    )


def shards(x, grads, frozen, slab, down, up, counts, plan):
    ys = lax.axis_size("y")
    lanes = lax.axis_size(WIDE)
    copies = lax.axis_size(DP)
    xl, core = lax.axis_index("xl"), lax.axis_index("core")
    rows, width = x.shape
    block, rank = down.shape
    hidden = up.shape[1]
    half = rows // 2
    n = 2 * frozen.shape[0] * frozen.shape[2]
    core_id = core.astype(jnp.int32).reshape(1)
    xl_id = xl.astype(jnp.int32).reshape(1)

    swapped = exchange(split_weights(frozen, ys, block), "core")
    chunks = swapped.shape[1]
    down_rows = down.T.reshape(4, rank // 4, block).transpose(1, 0, 2).reshape(rank // 4, 4 * block)
    near_down = shift(down_rows, "xl", 1)
    both_down = jnp.where(
        xl == 0,
        jnp.concatenate([down_rows, near_down], axis=0),
        jnp.concatenate([near_down, down_rows], axis=0),
    )
    sent = jnp.concatenate(
        [swapped.transpose(1, 0, 2, 3).reshape(chunks * 2 * n, 4 * block), both_down], axis=0
    )
    gathered = lax.all_gather(sent[None], "y", axis=0, tiled=True)

    own_a, own_b, other_a, other_b = split_rows(x, core_id, ys, block)
    next_own = shift(own_a, RING, 1)
    prev_own = shift(own_b, RING, -1)
    pair_a = shift(other_a, "core", 1)
    pair_b = shift(other_b, "core", 1)
    next_pair = shift(pair_a, RING, 1)
    prev_pair = shift(pair_b, RING, -1)
    xs = [own_a, pair_a, prev_own, prev_pair, next_own, next_pair, own_b, pair_b]

    cot = cotangent_rows(grads, plan[0], counts, lax.axis_index(WIDE))
    cot_pair = shift(cot, "core", 1)
    cot_a = jnp.concatenate([cot[:half], cot_pair[:half]], axis=0)
    cot_b = jnp.concatenate([cot[half:], cot_pair[half:]], axis=0)
    cots = jnp.concatenate([cot_a, shift(cot_b, RING, -1), shift(cot_a, RING, 1), cot_b], axis=0)

    mine = products(xs, gathered, n, rank, block)
    his = shift(mine, "core", 1)
    low, up_part = gate_stage(mine, his, cots, unit_order(slab, xl, ys, n, hidden), up, n)

    group = low.shape[0] // 2
    plus = shift(low[group:], RING, -1)
    minus = shift(low[:group], RING, 1)

    up_share = exchange(up_part, WIDE).reshape(lanes, rank // lanes, hidden).sum(0)
    up_all = exchange(jnp.tile(up_share, (copies, 1)), DP)
    up_share = up_all.reshape(copies, rank // lanes, hidden).sum(0)
    up_grad = exchange(jnp.tile(up_share, (lanes, 1)), WIDE)

    terms = down_terms(xs, xl_id, low, plus, minus, ys, block)
    terms = terms.reshape(ys, copies, rank // copies, block).transpose(1, 0, 2, 3)
    terms = exchange(terms.reshape(copies * ys, rank // copies, block), REPLICAS)
    share = terms.astype(F32).sum(0)
    full = exchange(jnp.tile(share[None], (copies, 1, 1)), DP)
    return full.reshape(rank, block).T, up_grad


def solution(mesh):
    dp, wide = mesh.devices.shape
    fine = Mesh(mesh.devices.reshape(dp // 2, 2, wide // 4, 2, 2), EVERY)
    placed = (
        P(EVERY, None),
        P(EVERY, None),
        P(None, None, WIDE, None),
        P(),
        P(WIDE, None),
        P(),
        P(EVERY),
        P(DP, None),
    )
    return jax.shard_map(
        shards, mesh=fine, in_specs=placed, out_specs=(P(WIDE, None), P()), check_vma=False
    )
```

time: 778 us -> 222 us (0.29)
  waiting for transfers between devices: 678 us -> 59.5 us
  starting transfers between devices: 8.92 us -> 94.5 us
  matrix products: 37.2 us -> 0.37 us
  Pallas kernels: 0 us -> 19.8 us
    psum x2 -> x0, waiting for transfers between devices: 424 us -> none  [the longest x1 263 us: shards(): up_grad = lax.psum(up_partial, ('dp', 'wide'))]
    all_gather x2 -> x1, waiting for transfers between devices: 132 us -> 6.27 us  [shards(): gathered = lax.all_gather(sent[None], 'y', axis=0, tiled=True)]
    reduce_scatter x1 -> x0, waiting for transfers between devices: 121 us -> none  [shards(): lax.psum_scatter(rounded, 'wide', scatter_dimension=0, tiled=True)]
    all_to_all x1 -> x7, starting transfers between devices: 8.72 us -> 53.4 us  [exchange(): return lax.all_to_all(array, axes, split_axis=0, concat_axis=0, tiled=True)]
    all_to_all x1 -> x7, waiting for transfers between devices: 0.01 us -> 41.3 us  [exchange(): return lax.all_to_all(array, axes, split_axis=0, concat_axis=0, tiled=True)]
    ppermute x0 -> x13, starting transfers between devices: none -> 41.1 us  [shift(): lax.ppermute(array, axes, [(i, (i + step) % size) for i in range(size)])]
    dot_general x5 -> x2, matrix products: 37.2 us -> 0.37 us  [the longest x1 0.22 us: cotangent_rows(): return jnp.dot(chosen(pick), back, preferred_element_type=F32).astype(BF16)]
    pallas_call x0 -> x5, Pallas kernels: none -> 19.8 us  [the longest x1 7.04 us: products(): pl.pallas_call(functools.partial(products_kernel, block=block), grid=(chu...]
  transfers between devices with their start and end apart: 6 -> 21, of which waited for: 5 -> 11; matrix products, arithmetic and copies ran while one was open for 5% -> 6% of each run, Pallas kernels for 0% -> 9%
where the time goes in v1:
time: 222 us; the launch traced here: 218 us
  starting transfers between devices  94.5 us (43%)
  waiting for transfers between devices  59.5 us (27%)
  local copies, waits for them, and re-layouts  22 us (10%)
  Pallas kernels  19.8 us (9%)
  between operations  14.5 us (7%)
  other arithmetic  7.35 us (3%)
    all_to_all x7, starting transfers between devices, exchange(): return lax.all_to_all(array, axes, split_axis=0, concat_axis=0, tiled=True)  53.4 us
    all_to_all x7, waiting for transfers between devices, exchange(): return lax.all_to_all(array, axes, split_axis=0, concat_axis=0, tiled=True)  41.3 us
    ppermute x13, starting transfers between devices, shift(): lax.ppermute(array, axes, [(i, (i + step) % size) for i in range(size)])  41.1 us
    ppermute x13, waiting for transfers between devices, shift(): lax.ppermute(array, axes, [(i, (i + step) % size) for i in range(size)])  11.9 us
    unnamed x29, local copies, waits for them, and re-layouts  10.2 us
    pallas_call x1, Pallas kernels, products(): pl.pallas_call(functools.partial(products_kernel, block=block), grid=(chu...  7.04 us
    all_gather x1, waiting for transfers between devices, shards(): gathered = lax.all_gather(sent[None], 'y', axis=0, tiled=True)  6.27 us
    pallas_call x1, Pallas kernels, down_terms(): pl.pallas_call(down_kernel, grid_spec=pltpu.PrefetchScalarGridSpec(num_sc...  5.65 us
  transfers between devices with their start and end apart: 21, of which 11 were waited for; matrix products, arithmetic and copies ran while one was open for 6% of the time, Pallas kernels for 9%

profile of v1, /device:TPU:6, one launch (start us, length us, event | category | flops | bytes accessed | tf_op | source)
XLA Modules:
  0.0 218.1 jit_solution(11068097146948037969)
XLA Ops:
  7.2 0.9 copy.35
  8.1 2.7 %collective-permute-start.6 = (bf16[16,2048]{1,0:T(8,128)(2,1)S(1)}, bf16[16,2048]{1,0:T(8,128)(2,1)S(1)}, u32[]{:S(2)}, u32[]{:S(2)}) collective-permute-start(bf16[16,2048]{1,0:T(8,128)(2,1)S(1)} %bitcast.52), channel_id=1, source_target_pairs={{0,2},{2,0},{1,3},{3,1},{4,6},{6,4},{5,7},{7,5},{8,10},{10,8},{9,1... | collective-permute-start | bytes 196616 | tf_op jit(solution)/shard_map/ppermute | solution.py:25
  10.8 1.0 copy-done.4
  11.8 2.8 %split_weights.1 = bf16[2,2,2,16,2048]{4,3,2,1,0:T(8,128)(2,1)} custom-call(bf16[4,2,2,16384]{3,2,1,0:T(2,128)(2,1)S(1)} %copy-done.4), custom_call_target="tpu_custom_call" | custom-call | bytes 1048576 | tf_op jit(solution)/shard_map/split_weights/pallas_call | solution.py:83
  14.7 3.5 %all-to-all-start = ((bf16[2,4,16,2048]{3,2,1,0:T(8,128)(2,1)}), bf16[2,4,16,2048]{3,2,1,0:T(8,128)(2,1)S(1)}, u32[]{:S(2)}, u32[]{:S(2)}) async-start(bf16[2,4,16,2048]{3,2,1,0:T(8,128)(2,1)} %bitcast.6), calls=%async_computation | async-start | bytes 1048576 | tf_op jit(solution)/shard_map/all_to_all | solution.py:29
  18.2 1.7 all-to-all-done
  20.0 0.9 pad_maximum_fusion
  20.9 2.2 copy-done.2
  23.1 3.6 %split_rows.1 = (bf16[2,2,64,2048]{3,2,1,0:T(8,128)(2,1)S(1)}, bf16[2,2,64,2048]{3,2,1,0:T(8,128)(2,1)S(1)}, bf16[2,2,64,2048]{3,2,1,0:T(8,128)(2,1)}, bf16[2,2,64,2048]{3,2,1,0:T(8,128)(2,1)}) custom-call(s32[1]{0:T(128)} %bitcast.1.core_ref, bf16[128,16384]{1,0:T(8,128)(2,1)S(1)} %copy-done.2), custom_call_target="tpu_custom_call" | custom-call | bytes 8388608 | tf_op jit(solution)/shard_map/split_rows/pallas_call | solution.py:53
  26.7 2.0 collective-permute-start
  28.7 3.1 %collective-permute-start.1 = (bf16[4,64,2048]{2,1,0:T(8,128)(2,1)S(1)}, bf16[4,64,2048]{2,1,0:T(8,128)(2,1)}, u32[]{:S(2)}, u32[]{:S(2)}) collective-permute-start(bf16[4,64,2048]{2,1,0:T(8,128)(2,1)S(1)} %bitcast.46), channel_id=1, source_target_pairs={{0,34},{2,0},{32,2},{34,32},{1,35},{3,1},{33,3},{35,33},{4,38},{6,... | collective-permute-start | bytes 3145736 | tf_op jit(solution)/shard_map/ppermute | solution.py:25
  31.9 2.0 collective-permute-start.2
  33.9 6.0 %collective-permute-start.4 = (bf16[4,64,2048]{2,1,0:T(8,128)(2,1)S(1)}, bf16[4,64,2048]{2,1,0:T(8,128)(2,1)}, u32[]{:S(2)}, u32[]{:S(2)}) collective-permute-start(bf16[4,64,2048]{2,1,0:T(8,128)(2,1)S(1)} %bitcast.43), channel_id=1, source_target_pairs={{0,2},{2,32},{32,34},{34,0},{1,3},{3,33},{33,35},{35,1},{4,6},{6,3... | collective-permute-start | bytes 3145736 | tf_op jit(solution)/shard_map/ppermute | solution.py:25
  40.0 0.4 select_reduce_fusion
  40.7 0.7 all_to_all.34
  41.3 6.6 %all-to-all-start.1 = ((bf16[32,4,256]{2,1,0:T(4,128)(2,1)}), bf16[32,4,256]{2,1,0:T(4,128)(2,1)S(1)}, u32[]{:S(2)}, u32[]{:S(2)}) async-start(bf16[32,4,256]{2,1,0:T(4,128)(2,1)} %all_to_all.34), calls=%async_computation.1 | async-start | bytes 131072 | tf_op jit(solution)/shard_map/all_to_all | solution.py:29
  48.0 0.6 fusion.26
  48.6 1.3 fusion.21
  49.9 0.6 fusion.25
  50.6 2.5 %compare_select_fusion.1 = s32[256,1]{0,1:T(1,128)S(1)} fusion(s32[256,1]{0,1:T(1,128)S(1)} %bitcast.59, s32[256,1]{0,1:T(1,128)S(1)} %bitcast.58, s32[]{:T(128)} %bitcast.21, s32[]{:T(128)} %bitcast.22, s32[]{:T(128)} %bitcast.24, s32[]{:T(128)} %bitcast.23), kind=kLoop, calls=%fused_computation.34 | loop fusion | flops 2048 | bytes 3088 | tf_op jit(solution)/shard_map/jit(_take)/gather | solution.py:268
  53.3 2.1 collective-permute-start.3
  55.5 4.9 %collective-permute-start.5 = (bf16[4,64,2048]{2,1,0:T(8,128)(2,1)}, bf16[4,64,2048]{2,1,0:T(8,128)(2,1)}, u32[]{:S(2)}, u32[]{:S(2)}) collective-permute-start(bf16[4,64,2048]{2,1,0:T(8,128)(2,1)} %collective-permute-done.refs_1_), channel_id=1, source_target_pairs={{0,2},{2,32},{32,34},{34,0},{1,3},{3,33},{33,35},{35,1},{4,6},{6,3... | collective-permute-start | bytes 3145736 | tf_op jit(solution)/shard_map/ppermute | solution.py:25
  60.6 5.1 %all-to-all-done.1 = bf16[32,4,256]{2,1,0:T(4,128)(2,1)S(1)} async-done(((bf16[32,4,256]{2,1,0:T(4,128)(2,1)}), bf16[32,4,256]{2,1,0:T(4,128)(2,1)S(1)}, u32[]{:S(2)}, u32[]{:S(2)}) %all-to-all-start.1) | async-done | bytes 65568 | tf_op jit(solution)/shard_map/all_to_all | solution.py:29
  66.0 2.1 collective-permute-start.8
  68.1 1.0 collective-permute-done.8
  69.2 0.6 pad_maximum_fusion.1
  69.8 1.9 collective-permute-start.9
  71.7 0.6 pad_maximum_fusion.2
  72.3 5.1 %collective-permute-start.10 = (bf16[128,256]{1,0:T(8,128)(2,1)}, bf16[128,256]{1,0:T(8,128)(2,1)}, u32[]{:S(2)}, u32[]{:S(2)}) collective-permute-start(bf16[128,256]{1,0:T(8,128)(2,1)} %pad_maximum_fusion.2), channel_id=1, source_target_pairs={{0,2},{2,32},{32,34},{34,0},{1,3},{3,33},{33,35},{35,1},{4,6},{6,3... | collective-permute-start | bytes 196616 | tf_op jit(solution)/shard_map/ppermute | solution.py:25
  77.5 5.2 %collective-permute-done.3.refs_3_ = bf16[4,64,2048]{2,1,0:T(8,128)(2,1)} collective-permute-done((bf16[4,64,2048]{2,1,0:T(8,128)(2,1)}, bf16[4,64,2048]{2,1,0:T(8,128)(2,1)}, u32[]{:S(2)}, u32[]{:S(2)}) %collective-permute-start.3) | collective-permute-done | bytes 1048608 | tf_op jit(solution)/shard_map/ppermute | solution.py:25
  82.7 5.6 %collective-permute-done.5.refs_5_ = bf16[4,64,2048]{2,1,0:T(8,128)(2,1)} collective-permute-done((bf16[4,64,2048]{2,1,0:T(8,128)(2,1)}, bf16[4,64,2048]{2,1,0:T(8,128)(2,1)}, u32[]{:S(2)}, u32[]{:S(2)}) %collective-permute-start.5) | collective-permute-done | bytes 1048608 | tf_op jit(solution)/shard_map/ppermute | solution.py:25
  88.3 6.3 %all-gather.3.cloned.1.call-done = bf16[1280,2048]{1,0:T(8,128)(2,1)} async-done(((bf16[160,2048]{1,0:T(8,128)(2,1)}), bf16[1280,2048]{1,0:T(8,128)(2,1)}) %all-gather.3.cloned.1.call-update) | async-done | bytes 5242896 | tf_op jit(solution)/shard_map/all_gather | solution.py:301
  94.6 2.5 %copy-done.1 = bf16[1280,2048]{1,0:T(8,128)(2,1)S(1)} copy-done((bf16[1280,2048]{1,0:T(8,128)(2,1)S(1)}, bf16[1280,2048]{1,0:T(8,128)(2,1)}, u32[]{:S(2)}) %copy-start.1) | copy-done | bytes 5242904
  97.1 7.0 %products.1.mine_ref = f32[512,320]{1,0:T(8,128)S(1)} custom-call(bf16[4,64,2048]{2,1,0:T(8,128)(2,1)S(1)} %bitcast.44, bf16[4,64,2048]{2,1,0:T(8,128)(2,1)} %collective-permute-done.refs_1_, bf16[4,64,2048]{2,1,0:T(8,128)(2,1)} %collective-permute-done.1.refs_2_, bf16[4,64,2048]{2,1,0:T(8,128)(2,1)} %collective-permute-done.3.refs_3_, ...), custom_call_target="tpu_custom_call" | custom-call | flops 2684354560 | bytes 13631488 | tf_op jit(solution)/shard_map/products/pallas_call | solution.py:130
  104.1 1.1 copy.29
  105.2 1.9 collective-permute-start.7
  107.1 0.8 constant_dynamic-update-slice_fusion.3
  108.0 0.8 constant_dynamic-update-slice_fusion.2
  108.9 0.7 copy-done.5
  109.6 2.2 %copy.30.his_ref = f32[512,320]{1,0:T(8,128)} copy(f32[512,320]{0,1:T(8,128)} %collective-permute-done.7) | data formatting | bytes 1310720 | tf_op jit(solution)/shard_map/ppermute | solution.py:25
  111.8 1.1 copy-done.3
  113.0 0.9 copy-done.6
  113.9 0.7 gate_stage.1
  114.6 0.7 all_to_all.39
  115.3 6.2 %all-to-all-start.4 = ((f32[32,2,256]{2,1,0:T(2,128)}), f32[32,2,256]{2,1,0:T(2,128)S(1)}, u32[]{:S(2)}, u32[]{:S(2)}) async-start(f32[32,2,256]{2,1,0:T(2,128)} %all_to_all.39), calls=%async_computation.4 | async-start | bytes 131072 | tf_op jit(solution)/shard_map/all_to_all | solution.py:29
  121.5 2.1 collective-permute-start.11
  123.7 4.9 %collective-permute-start.12 = (f32[256,64]{1,0:T(8,128)S(1)}, f32[256,64]{1,0:T(8,128)S(1)}, u32[]{:S(2)}, u32[]{:S(2)}) collective-permute-start(f32[256,64]{1,0:T(8,128)S(1)} %get-tuple-element.38), channel_id=1, source_target_pairs={{0,2},{2,32},{32,34},{34,0},{1,3},{3,33},{33,35},{35,1},{4,6},{6,3... | collective-permute-start | bytes 196616 | tf_op jit(solution)/shard_map/ppermute | solution.py:25
  128.6 0.8 all-to-all-done.4
  129.4 0.6 tile.7
  130.0 10.4 %all-to-all-start.5 = ((f32[16,2,256]{2,1,0:T(2,128)}), f32[16,2,256]{2,1,0:T(2,128)S(1)}, u32[]{:S(2)}, u32[]{:S(2)}) async-start(f32[16,2,256]{2,1,0:T(2,128)} %tile.7), calls=%async_computation.5 | async-start | bytes 65536 | tf_op jit(solution)/shard_map/all_to_all | solution.py:29
  140.4 5.7 %down_terms.1 = bf16[8,64,512]{2,1,0:T(8,128)(2,1)S(1)} custom-call(s32[1]{0:T(128)} %bitcast.xl_ref, bf16[4,64,2048]{2,1,0:T(8,128)(2,1)S(1)} %bitcast.45, bf16[4,64,2048]{2,1,0:T(8,128)(2,1)} %collective-permute-done.refs_1_, bf16[4,64,2048]{2,1,0:T(8,128)(2,1)} %collective-permute-done.1.refs_2_, bf16[4,64,2048]{2,1,0:T(8,128)(2,1)} %collective-permute-done.3.refs_3_, ...), custom_call_target="tpu_custom_call" | custom-call | flops 268435456 | bytes 4718592 | tf_op jit(solution)/shard_map/down_terms/pallas_call | solution.py:215
  146.2 0.3 copy.37
  146.5 1.2 copy.32
  147.8 14.9 %all-to-all-start.2 = ((bf16[128,4,512]{2,1,0:T(4,128)(2,1)}), bf16[128,4,512]{2,1,0:T(4,128)(2,1)S(1)}, u32[]{:S(2)}, u32[]{:S(2)}) async-start(bf16[128,4,512]{2,1,0:T(4,128)(2,1)} %copy.32), calls=%async_computation.2 | async-start | bytes 1048576 | tf_op jit(solution)/shard_map/all_to_all | solution.py:29
  162.7 18.1 %all-to-all-done.2 = bf16[128,4,512]{2,1,0:T(4,128)(2,1)S(1)} async-done(((bf16[128,4,512]{2,1,0:T(4,128)(2,1)}), bf16[128,4,512]{2,1,0:T(4,128)(2,1)S(1)}, u32[]{:S(2)}, u32[]{:S(2)}) %all-to-all-start.2) | async-done | bytes 524320 | tf_op jit(solution)/shard_map/all_to_all | solution.py:29
  180.9 0.6 tile.8
  181.5 5.7 %all-to-all-start.6 = ((f32[32,2,256]{2,1,0:T(2,128)}), f32[32,2,256]{2,1,0:T(2,128)S(1)}, u32[]{:S(2)}, u32[]{:S(2)}) async-start(f32[32,2,256]{2,1,0:T(2,128)} %tile.8), calls=%async_computation.6 | async-start | bytes 131072 | tf_op jit(solution)/shard_map/all_to_all | solution.py:29
  187.2 0.3 convert_reduce_fusion
  187.5 7.6 %all-to-all-done.6 = f32[32,2,256]{2,1,0:T(2,128)S(1)} async-done(((f32[32,2,256]{2,1,0:T(2,128)}), f32[32,2,256]{2,1,0:T(2,128)S(1)}, u32[]{:S(2)}, u32[]{:S(2)}) %all-to-all-start.6) | async-done | bytes 65568 | tf_op jit(solution)/shard_map/all_to_all | solution.py:29
  195.1 0.7 tile.6
  195.7 6.2 %all-to-all-start.3 = ((f32[16,4,512]{2,1,0:T(4,128)}), f32[16,4,512]{2,1,0:T(4,128)S(1)}, u32[]{:S(2)}, u32[]{:S(2)}) async-start(f32[16,4,512]{2,1,0:T(4,128)} %tile.6), calls=%async_computation.3 | async-start | bytes 262144 | tf_op jit(solution)/shard_map/all_to_all | solution.py:29
  202.0 0.7 all_to_all.43
  202.6 7.9 %all-to-all-done.3 = f32[16,4,512]{2,1,0:T(4,128)S(1)} async-done(((f32[16,4,512]{2,1,0:T(4,128)}), f32[16,4,512]{2,1,0:T(4,128)S(1)}, u32[]{:S(2)}, u32[]{:S(2)}) %all-to-all-start.3) | async-done | bytes 131104 | tf_op jit(solution)/shard_map/all_to_all | solution.py:29
  210.5 0.7 reshape.340
  (58 shorter events, 1.7 us)
Async XLA Ops:
  7.2 33.4 %copy-start = (bf16[128,256]{1,0:T(8,128)(2,1)S(1)}, bf16[128,256]{1,0:T(8,128)(2,1)}, u32[]{:S(2)}) copy-start(bf16[128,256]{1,0:T(8,128)(2,1)} %param.13) | copy-start | bytes 196612
  8.1 11.9 %collective-permute-start.6 = (bf16[16,2048]{1,0:T(8,128)(2,1)S(1)}, bf16[16,2048]{1,0:T(8,128)(2,1)S(1)}, u32[]{:S(2)}, u32[]{:S(2)}) collective-permute-start(bf16[16,2048]{1,0:T(8,128)(2,1)S(1)} %bitcast.52), channel_id=1, source_target_pairs={{0,2},{2,0},{1,3},{3,1},{4,6},{6,4},{5,7},{7,5},{8,10},{10,8},{9,1... | collective-permute-start | bytes 196616 | tf_op jit(solution)/shard_map/ppermute | solution.py:25
  10.8 1.0 copy-start.4
  14.7 5.2 %all-to-all-start = ((bf16[2,4,16,2048]{3,2,1,0:T(8,128)(2,1)}), bf16[2,4,16,2048]{3,2,1,0:T(8,128)(2,1)S(1)}, u32[]{:S(2)}, u32[]{:S(2)}) async-start(bf16[2,4,16,2048]{3,2,1,0:T(8,128)(2,1)} %bitcast.6), calls=%async_computation | async-start | bytes 1048576 | tf_op jit(solution)/shard_map/all_to_all | solution.py:29
  18.2 76.4 %all-gather.3.cloned.1.call-start = ((), (), s32[]{:S(2)}) async-start(), calls=%async_computation.7 | async-start | bytes 5898240 | tf_op jit(solution)/shard_map/all_gather | solution.py:301
  20.9 2.2 %copy-start.2 = (bf16[128,16384]{1,0:T(8,128)(2,1)S(1)}, bf16[128,16384]{1,0:T(8,128)(2,1)}, u32[]{:S(2)}) copy-start(bf16[128,16384]{1,0:T(8,128)(2,1)} %x_ref.1) | copy-start | bytes 12582916
  23.1 16.8 %copy-start.8 = (s32[1,4096]{1,0:T(1,128)S(1)}, s32[1,4096]{1,0:T(1,128)}, u32[]{:S(2)}) copy-start(s32[1,4096]{1,0:T(1,128)} %param.19) | copy-start | bytes 49156
  23.1 24.9 %copy-start.11 = (s32[2]{0:T(128)S(1)}, s32[2]{0:T(128)}, u32[]{:S(2)}) copy-start(s32[2]{0:T(128)} %param.18) | copy-start | bytes 28
  23.1 25.5 %copy-start.12 = (pred[128]{0:T(512)(128)(4,1)S(1)}, pred[128]{0:T(512)(128)(4,1)}, u32[]{:S(2)}) copy-start(pred[128]{0:T(512)(128)(4,1)} %constant.309) | copy-start | bytes 388
  23.1 26.8 %copy-start.9 = (s32[4]{0:T(128)S(1)}, s32[4]{0:T(128)}, u32[]{:S(2)}) copy-start(s32[4]{0:T(128)} %param.15) | copy-start | bytes 52
  23.1 27.4 %copy-start.10 = (s32[2,128]{1,0:T(2,128)S(1)}, s32[2,128]{1,0:T(2,128)}, u32[]{:S(2)}) copy-start(s32[2,128]{1,0:T(2,128)} %constant.291.clone.1) | copy-start | bytes 3076
  26.7 28.8 %collective-permute-start = (bf16[4,64,2048]{2,1,0:T(8,128)(2,1)}, bf16[4,64,2048]{2,1,0:T(8,128)(2,1)}, u32[]{:S(2)}, u32[]{:S(2)}) collective-permute-start(bf16[4,64,2048]{2,1,0:T(8,128)(2,1)} %bitcast.3), channel_id=1, source_target_pairs={{0,1},{1,0},{2,3},{3,2},{4,5},{5,4},{6,7},{7,6},{8,9},{9,8},{10,11... | collective-permute-start | bytes 3145736 | tf_op jit(solution)/shard_map/ppermute | solution.py:25
  28.7 43.6 %collective-permute-start.1 = (bf16[4,64,2048]{2,1,0:T(8,128)(2,1)S(1)}, bf16[4,64,2048]{2,1,0:T(8,128)(2,1)}, u32[]{:S(2)}, u32[]{:S(2)}) collective-permute-start(bf16[4,64,2048]{2,1,0:T(8,128)(2,1)S(1)} %bitcast.46), channel_id=1, source_target_pairs={{0,34},{2,0},{32,2},{34,32},{1,35},{3,1},{33,3},{35,33},{4,38},{6,... | collective-permute-start | bytes 3145736 | tf_op jit(solution)/shard_map/ppermute | solution.py:25
  31.9 21.5 %collective-permute-start.2 = (bf16[4,64,2048]{2,1,0:T(8,128)(2,1)}, bf16[4,64,2048]{2,1,0:T(8,128)(2,1)}, u32[]{:S(2)}, u32[]{:S(2)}) collective-permute-start(bf16[4,64,2048]{2,1,0:T(8,128)(2,1)} %bitcast.5), channel_id=1, source_target_pairs={{0,1},{1,0},{2,3},{3,2},{4,5},{5,4},{6,7},{7,6},{8,9},{9,8},{10,11... | collective-permute-start | bytes 3145736 | tf_op jit(solution)/shard_map/ppermute | solution.py:25
  33.9 43.6 %collective-permute-start.4 = (bf16[4,64,2048]{2,1,0:T(8,128)(2,1)S(1)}, bf16[4,64,2048]{2,1,0:T(8,128)(2,1)}, u32[]{:S(2)}, u32[]{:S(2)}) collective-permute-start(bf16[4,64,2048]{2,1,0:T(8,128)(2,1)S(1)} %bitcast.43), channel_id=1, source_target_pairs={{0,2},{2,32},{32,34},{34,0},{1,3},{3,33},{33,35},{35,1},{4,6},{6,3... | collective-permute-start | bytes 3145736 | tf_op jit(solution)/shard_map/ppermute | solution.py:25
  41.3 24.4 %all-to-all-start.1 = ((bf16[32,4,256]{2,1,0:T(4,128)(2,1)}), bf16[32,4,256]{2,1,0:T(4,128)(2,1)S(1)}, u32[]{:S(2)}, u32[]{:S(2)}) async-start(bf16[32,4,256]{2,1,0:T(4,128)(2,1)} %all_to_all.34), calls=%async_computation.1 | async-start | bytes 131072 | tf_op jit(solution)/shard_map/all_to_all | solution.py:29
  53.3 29.3 %collective-permute-start.3 = (bf16[4,64,2048]{2,1,0:T(8,128)(2,1)}, bf16[4,64,2048]{2,1,0:T(8,128)(2,1)}, u32[]{:S(2)}, u32[]{:S(2)}) collective-permute-start(bf16[4,64,2048]{2,1,0:T(8,128)(2,1)} %collective-permute-done.2.refs_7_), channel_id=1, source_target_pairs={{0,34},{2,0},{32,2},{34,32},{1,35},{3,1},{33,3},{35,33},{4,38},{6,... | collective-permute-start | bytes 3145736 | tf_op jit(solution)/shard_map/ppermute | solution.py:25
  55.5 32.8 %collective-permute-start.5 = (bf16[4,64,2048]{2,1,0:T(8,128)(2,1)}, bf16[4,64,2048]{2,1,0:T(8,128)(2,1)}, u32[]{:S(2)}, u32[]{:S(2)}) collective-permute-start(bf16[4,64,2048]{2,1,0:T(8,128)(2,1)} %collective-permute-done.refs_1_), channel_id=1, source_target_pairs={{0,2},{2,32},{32,34},{34,0},{1,3},{3,33},{33,35},{35,1},{4,6},{6,3... | collective-permute-start | bytes 3145736 | tf_op jit(solution)/shard_map/ppermute | solution.py:25
  66.0 3.1 %collective-permute-start.8 = (bf16[128,256]{1,0:T(8,128)(2,1)S(1)}, bf16[128,256]{1,0:T(8,128)(2,1)S(1)}, u32[]{:S(2)}, u32[]{:S(2)}) collective-permute-start(bf16[128,256]{1,0:T(8,128)(2,1)S(1)} %convolution_convert_fusion), channel_id=1, source_target_pairs={{0,1},{1,0},{2,3},{3,2},{4,5},{5,4},{6,7},{7,6},{8,9},{9,8},{10,11... | collective-permute-start | bytes 196616 | tf_op jit(solution)/shard_map/ppermute | solution.py:25
  69.8 37.3 %collective-permute-start.9 = (bf16[128,256]{1,0:T(8,128)(2,1)}, bf16[128,256]{1,0:T(8,128)(2,1)}, u32[]{:S(2)}, u32[]{:S(2)}) collective-permute-start(bf16[128,256]{1,0:T(8,128)(2,1)} %pad_maximum_fusion.1), channel_id=1, source_target_pairs={{0,34},{2,0},{32,2},{34,32},{1,35},{3,1},{33,3},{35,33},{4,38},{6,... | collective-permute-start | bytes 196616 | tf_op jit(solution)/shard_map/ppermute | solution.py:25
  72.3 35.6 %collective-permute-start.10 = (bf16[128,256]{1,0:T(8,128)(2,1)}, bf16[128,256]{1,0:T(8,128)(2,1)}, u32[]{:S(2)}, u32[]{:S(2)}) collective-permute-start(bf16[128,256]{1,0:T(8,128)(2,1)} %pad_maximum_fusion.2), channel_id=1, source_target_pairs={{0,2},{2,32},{32,34},{34,0},{1,3},{3,33},{33,35},{35,1},{4,6},{6,3... | collective-permute-start | bytes 196616 | tf_op jit(solution)/shard_map/ppermute | solution.py:25
  94.6 2.5 %copy-start.1 = (bf16[1280,2048]{1,0:T(8,128)(2,1)S(1)}, bf16[1280,2048]{1,0:T(8,128)(2,1)}, u32[]{:S(2)}) copy-start(bf16[1280,2048]{1,0:T(8,128)(2,1)} %all-gather.3.cloned.1.call-done) | copy-start | bytes 15728644
  104.1 7.7 %copy-start.7 = (bf16[64,256]{1,0:T(8,128)(2,1)S(1)}, bf16[64,256]{1,0:T(8,128)(2,1)}, u32[]{:S(2)}) copy-start(bf16[64,256]{1,0:T(8,128)(2,1)} %up_ref.1) | copy-start | bytes 98308
  105.2 4.4 %collective-permute-start.7 = (f32[512,320]{0,1:T(8,128)}, f32[512,320]{0,1:T(8,128)}, u32[]{:S(2)}, u32[]{:S(2)}) collective-permute-start(f32[512,320]{0,1:T(8,128)} %copy.29), channel_id=1, source_target_pairs={{0,1},{1,0},{2,3},{3,2},{4,5},{5,4},{6,7},{7,6},{8,9},{9,8},{10,11... | collective-permute-start | bytes 1966088 | tf_op jit(solution)/shard_map/ppermute | solution.py:25
  108.8 0.7 copy-start.5
  111.8 1.1 copy-start.3
  113.0 0.9 copy-start.6
  115.3 14.1 %all-to-all-start.4 = ((f32[32,2,256]{2,1,0:T(2,128)}), f32[32,2,256]{2,1,0:T(2,128)S(1)}, u32[]{:S(2)}, u32[]{:S(2)}) async-start(f32[32,2,256]{2,1,0:T(2,128)} %all_to_all.39), calls=%async_computation.4 | async-start | bytes 131072 | tf_op jit(solution)/shard_map/all_to_all | solution.py:29
  121.5 18.9 %collective-permute-start.11 = (f32[256,64]{1,0:T(8,128)S(1)}, f32[256,64]{1,0:T(8,128)S(1)}, u32[]{:S(2)}, u32[]{:S(2)}) collective-permute-start(f32[256,64]{1,0:T(8,128)S(1)} %get-tuple-element.39), channel_id=1, source_target_pairs={{0,34},{2,0},{32,2},{34,32},{1,35},{3,1},{33,3},{35,33},{4,38},{6,... | collective-permute-start | bytes 196616 | tf_op jit(solution)/shard_map/ppermute | solution.py:25
  123.7 16.7 %collective-permute-start.12 = (f32[256,64]{1,0:T(8,128)S(1)}, f32[256,64]{1,0:T(8,128)S(1)}, u32[]{:S(2)}, u32[]{:S(2)}) collective-permute-start(f32[256,64]{1,0:T(8,128)S(1)} %get-tuple-element.38), channel_id=1, source_target_pairs={{0,2},{2,32},{32,34},{34,0},{1,3},{3,33},{33,35},{35,1},{4,6},{6,3... | collective-permute-start | bytes 196616 | tf_op jit(solution)/shard_map/ppermute | solution.py:25
  130.0 17.8 %all-to-all-start.5 = ((f32[16,2,256]{2,1,0:T(2,128)}), f32[16,2,256]{2,1,0:T(2,128)S(1)}, u32[]{:S(2)}, u32[]{:S(2)}) async-start(f32[16,2,256]{2,1,0:T(2,128)} %tile.7), calls=%async_computation.5 | async-start | bytes 65536 | tf_op jit(solution)/shard_map/all_to_all | solution.py:29
  147.8 33.0 %all-to-all-start.2 = ((bf16[128,4,512]{2,1,0:T(4,128)(2,1)}), bf16[128,4,512]{2,1,0:T(4,128)(2,1)S(1)}, u32[]{:S(2)}, u32[]{:S(2)}) async-start(bf16[128,4,512]{2,1,0:T(4,128)(2,1)} %copy.32), calls=%async_computation.2 | async-start | bytes 1048576 | tf_op jit(solution)/shard_map/all_to_all | solution.py:29
  181.5 13.5 %all-to-all-start.6 = ((f32[32,2,256]{2,1,0:T(2,128)}), f32[32,2,256]{2,1,0:T(2,128)S(1)}, u32[]{:S(2)}, u32[]{:S(2)}) async-start(f32[32,2,256]{2,1,0:T(2,128)} %tile.8), calls=%async_computation.6 | async-start | bytes 131072 | tf_op jit(solution)/shard_map/all_to_all | solution.py:29
  195.7 14.8 %all-to-all-start.3 = ((f32[16,4,512]{2,1,0:T(4,128)}), f32[16,4,512]{2,1,0:T(4,128)S(1)}, u32[]{:S(2)}, u32[]{:S(2)}) async-start(f32[16,4,512]{2,1,0:T(4,128)} %tile.6), calls=%async_computation.3 | async-start | bytes 262144 | tf_op jit(solution)/shard_map/all_to_all | solution.py:29
Sparse Core Ops, SparseCore 0:
  21.1 73.4 all-gather.2

commit v2 on v1

--- a/solution.py
+++ b/solution.py
@@ -15,7 +15,7 @@
 RING = ("xh", "xl")
 REPLICAS = ("z", "xh", "y")
 EVERY = ("z", "xh", "y", "xl", "core")
-VMEM_LIMIT = 40 * 1024 * 1024
+MIB = 1024 * 1024
 NT = (((1,), (1,)), ((), ()))
 TN = (((0,), (0,)), ((), ()))
 
@@ -29,8 +29,8 @@
     return lax.all_to_all(array, axes, split_axis=0, concat_axis=0, tiled=True)
 
 
-def params():
-    return pltpu.CompilerParams(vmem_limit_bytes=VMEM_LIMIT)
+def params(mib):
+    return pltpu.CompilerParams(vmem_limit_bytes=mib * MIB)
 
 
 def split_rows_kernel(core_ref, x_ref, own_a, own_b, other_a, other_b, *, block):
@@ -59,7 +59,7 @@
             out_specs=[spec] * 4,
         ),
         out_shape=[shape] * 4,
-        compiler_params=params(),
+        compiler_params=params(24),
         cost_estimate=pl.CostEstimate(flops=0, bytes_accessed=rows * width * 4, transcendentals=0),
         name="split_rows",
     )(core, x)
@@ -73,8 +73,9 @@
     ).astype(BF16)
     for parity in range(2):
         for xl in range(2):
-            at = (xl * 2 + parity) * block
-            out_ref[parity, xl, 0] = rows[:, at : at + block]
+            for y in range(4):
+                at = ((y * 2 + xl) * 2 + parity) * block
+                out_ref[parity, xl, 0, :, y * block : (y + 1) * block] = rows[:, at : at + block]
 
 
 def split_weights(w, ys, block):
@@ -82,18 +83,18 @@
     n = 2 * spans * units
     out = pl.pallas_call(
         functools.partial(split_weights_kernel, block=block),
-        grid=(ys,),
-        in_specs=[pl.BlockSpec((spans, 2, units, 4 * block), lambda y: (0, 0, 0, y))],
-        out_specs=pl.BlockSpec((2, 2, 1, n, block), lambda y: (0, 0, y // 4, 0, y % 4)),
+        grid=(ys // 4,),
+        in_specs=[pl.BlockSpec((spans, 2, units, 16 * block), lambda y: (0, 0, 0, y))],
+        out_specs=pl.BlockSpec((2, 2, 1, n, 4 * block), lambda y: (0, 0, y, 0, 0)),
         out_shape=jax.ShapeDtypeStruct((2, 2, ys // 4, n, 4 * block), BF16),
-        compiler_params=params(),
+        compiler_params=params(24),
         cost_estimate=pl.CostEstimate(flops=0, bytes_accessed=w.size * 4, transcendentals=0),
         name="split_weights",
     )(w)
     return out.reshape(2, 2 * (ys // 4), n, 4 * block)
 
 
-def products_kernel(*refs, block):
+def products_kernel(*refs, block, rank):
     x_refs, (w_ref, down_ref, out_ref) = refs[:8], refs[8:]
     x = jnp.concatenate([r[0] for r in x_refs], axis=0)
     w = w_ref[...].reshape(-1, w_ref.shape[-1])
@@ -113,31 +114,33 @@
     @pl.when(pl.program_id(0) == 0)
     def _():
         out_ref[:, :units] = wide
-        out_ref[:, units:] = low
+        out_ref[:, units : units + rank] = low
+        out_ref[:, units + rank :] = jnp.zeros_like(out_ref[:, units + rank :])
 
     @pl.when(pl.program_id(0) > 0)
     def _():
         out_ref[:, :units] += wide
-        out_ref[:, units:] += low
+        out_ref[:, units : units + rank] += low
 
 
 def products(xs, gathered, n, rank, block):
     chunks, part, lanes = xs[0].shape
     ys = gathered.shape[0]
     units = ys * 2 * n
+    columns = units + pl.cdiv(rank, 128) * 128
     x_spec = pl.BlockSpec((1, part, lanes), lambda k: (k, 0, 0))
     per = chunks // 2
     return pl.pallas_call(
-        functools.partial(products_kernel, block=block),
+        functools.partial(products_kernel, block=block, rank=rank),
         grid=(chunks,),
         in_specs=[x_spec] * 8
         + [
             pl.BlockSpec((ys, 2 * n, lanes), lambda k: (0, k, 0)),
             pl.BlockSpec((4, rank // 4, lanes), lambda k: (k % per, 2 * chunks + k // per, 0)),
         ],
-        out_specs=pl.BlockSpec((8 * part, units + rank), lambda k: (0, 0)),
-        out_shape=jax.ShapeDtypeStruct((8 * part, units + rank), F32),
-        compiler_params=params(),
+        out_specs=pl.BlockSpec((8 * part, columns), lambda k: (0, 0)),
+        out_shape=jax.ShapeDtypeStruct((8 * part, columns), F32),
+        compiler_params=params(60),
         cost_estimate=pl.CostEstimate(
             flops=2 * 8 * part * chunks * lanes * (units + rank),
             bytes_accessed=(8 * part + units + rank) * chunks * lanes * 2,
@@ -153,82 +156,101 @@
     )
 
 
-def gate_kernel(mine_ref, his_ref, cot_ref, pick_ref, up_ref, low_ref, up_grad_ref, *, n, part):
+def gate_kernel(mine_ref, his_ref, a_ref, next_b_ref, prev_a_ref, b_ref, pick_ref, up_ref,
+                plus_ref, minus_ref, *, n, part, rank):
     units = pick_ref.shape[1]
     total = mine_ref[...] + swap_pairs(his_ref, part)
-    low = total[:, units:].astype(BF16)
+    low = total[:, units : units + rank].astype(BF16)
     pick = pick_ref[...]
     up = jnp.dot(up_ref[...], pick, preferred_element_type=F32).astype(BF16)
-    cot = jnp.dot(cot_ref[...], pick, preferred_element_type=F32)
+    cot = jnp.concatenate(
+        [a_ref[...], next_b_ref[...], prev_a_ref[...], b_ref[...]], axis=0
+    )
+    cot = jnp.dot(cot, pick, preferred_element_type=F32)
     both = total[:, :units]
     gate = both + jnp.dot(low, up, preferred_element_type=F32)
     upper = pltpu.roll(both, units - n // 2, 1)
     s = jax.nn.sigmoid(gate)
     grad = (cot * upper * s * (1.0 + gate * (1.0 - s))).astype(BF16)
-    low_ref[...] = lax.dot_general(grad, up, NT, preferred_element_type=F32)
+    low_grad = lax.dot_general(grad, up, NT, preferred_element_type=F32)
     ordered = lax.dot_general(grad, pick, NT, preferred_element_type=F32).astype(BF16)
-    first = [i for i in range(8) if i % 2 == 0]
-    low_m = jnp.concatenate([low[i * part : (i + 1) * part] for i in first], axis=0)
-    ordered_m = jnp.concatenate([ordered[i * part : (i + 1) * part] for i in first], axis=0)
-    up_grad_ref[...] = lax.dot_general(low_m, ordered_m, TN, preferred_element_type=F32)
-
-
-def gate_stage(mine, his, cot, pick, up, n):
+    up_grad = lax.dot_general(low, ordered, TN, preferred_element_type=F32)
+    group = 4 * part
+    pieces = [up_grad[:, i * rank : (i + 1) * rank] for i in range(up_grad.shape[1] // rank)]
+    plus_ref[:, :rank] = low_grad[:group]
+    plus_ref[:, rank:] = jnp.concatenate(pieces, axis=0)
+    minus_ref[...] = low_grad[group:]
+
+
+def gate_stage(mine, his, cots, pick, up, n):
     rows = mine.shape[0]
     rank, hidden = up.shape
     vm = pl.BlockSpec(memory_space=pltpu.VMEM)
     return pl.pallas_call(
-        functools.partial(gate_kernel, n=n, part=rows // 8),
-        in_specs=[vm] * 5,
+        functools.partial(gate_kernel, n=n, part=rows // 8, rank=rank),
+        in_specs=[vm] * 8,
         out_specs=[vm, vm],
         out_shape=[
-            jax.ShapeDtypeStruct((rows, rank), F32),
-            jax.ShapeDtypeStruct((rank, hidden), F32),
+            jax.ShapeDtypeStruct((rows // 2, 2 * rank), F32),
+            jax.ShapeDtypeStruct((rows // 2, rank), F32),
         ],
-        compiler_params=params(),
+        compiler_params=params(24),
         cost_estimate=pl.CostEstimate(
             flops=2 * rows * hidden * (2 * hidden + 3 * rank),
             bytes_accessed=rows * hidden * 12,
             transcendentals=rows * hidden,
         ),
         name="gate_stage",
-    )(mine, his, cot, pick, up)
-
-
-def down_kernel(xl_ref, *refs):
-    x_refs, (mine_ref, plus_ref, minus_ref, out_ref) = refs[:8], refs[8:]
-    half = plus_ref.shape[0]
+    )(mine, his, *cots, pick, up)
+
+
+def down_kernel(xl_ref, *refs, block):
+    x_refs, (plus_ref, minus_ref, from_next, from_prev, out_ref) = refs[:8], refs[8:]
+    rank = minus_ref.shape[1]
     low = jnp.concatenate(
-        [mine_ref[:half] + plus_ref[...], mine_ref[half:] + minus_ref[...]], axis=0
+        [plus_ref[:, :rank] + from_next[...], minus_ref[...] + from_prev[:, :rank]], axis=0
     ).astype(BF16)
+    up = plus_ref[:, rank:] + from_prev[:, rank:]
+    up = jnp.concatenate(
+        [up[i * rank : (i + 1) * rank] for i in range(up.shape[0] // rank)], axis=1
+    )
     x = jnp.concatenate([r[0] for r in x_refs], axis=0)
-    out_ref[0] = lax.dot_general(low, x, TN, preferred_element_type=F32).astype(BF16)
-
-
-def down_terms(xs, xl, mine, plus, minus, ys, block):
+    terms = lax.dot_general(low, x, TN, preferred_element_type=F32)
+    lanes = out_ref.shape[-1]
+    for i in range(4):
+        row = jnp.concatenate([terms[:, i * block : (i + 1) * block], up], axis=1)
+        for h in range(2):
+            for g in range(rank // 8):
+                piece = row[g * 8 : (g + 1) * 8, h * lanes : (h + 1) * lanes]
+                out_ref[h * (rank // 8) + g, i] = piece.astype(BF16)
+
+
+def down_terms(xs, xl, plus, minus, from_next, from_prev, ys, block):
     chunks, part, lanes = xs[0].shape
     per = chunks // 2
-    rows, rank = mine.shape
-    x_spec = pl.BlockSpec((1, part, block), lambda y, v: (v[0] * per + y // 4, 0, y % 4))
-    full = pl.BlockSpec((rows, rank), lambda y, v: (0, 0))
-    half = pl.BlockSpec((rows // 2, rank), lambda y, v: (0, 0))
+    group, rank = minus.shape
+    hidden = group // rank * rank
+    piece = (block + hidden) // 2
+    x_spec = pl.BlockSpec((1, part, lanes), lambda k, v: (v[0] * per + k, 0, 0))
+    both = pl.BlockSpec((group, 2 * rank), lambda k, v: (0, 0))
+    single = pl.BlockSpec((group, rank), lambda k, v: (0, 0))
     return pl.pallas_call(
-        down_kernel,
+        functools.partial(down_kernel, block=block),
         grid_spec=pltpu.PrefetchScalarGridSpec(
             num_scalar_prefetch=1,
-            grid=(ys,),
-            in_specs=[x_spec] * 8 + [full, half, half],
-            out_specs=pl.BlockSpec((1, rank, block), lambda y, v: (y, 0, 0)),
-        ),
-        out_shape=jax.ShapeDtypeStruct((ys, rank, block), BF16),
-        compiler_params=params(),
+            grid=(per,),
+            in_specs=[x_spec] * 8 + [both, single, single, both],
+            out_specs=pl.BlockSpec((rank // 4, 4, 8, piece), lambda k, v: (0, k, 0, 0)),
+        ),
+        out_shape=jax.ShapeDtypeStruct((rank // 4, ys, 8, piece), BF16),
+        compiler_params=params(60),
         cost_estimate=pl.CostEstimate(
-            flops=2 * rows * rank * ys * block,
-            bytes_accessed=(rows + rank) * ys * block * 2,
+            flops=2 * 2 * group * rank * ys * block,
+            bytes_accessed=(2 * group + rank) * ys * block * 2,
             transcendentals=0,
         ),
         name="down_terms",
-    )(xl, *xs, mine, plus, minus)
+    )(xl, *xs, plus, minus, from_next, from_prev)
 
 
 def chosen(condition):
@@ -275,7 +297,6 @@
 
 def shards(x, grads, frozen, slab, down, up, counts, plan):
     ys = lax.axis_size("y")
-    lanes = lax.axis_size(WIDE)
     copies = lax.axis_size(DP)
     xl, core = lax.axis_index("xl"), lax.axis_index("core")
     rows, width = x.shape
@@ -300,40 +321,40 @@
     )
     gathered = lax.all_gather(sent[None], "y", axis=0, tiled=True)
 
-    own_a, own_b, other_a, other_b = split_rows(x, core_id, ys, block)
+    parts = split_rows(x, core_id, ys, block)
+    own_a, own_b, other_a, other_b, grads = lax.optimization_barrier((*parts, grads))
     next_own = shift(own_a, RING, 1)
     prev_own = shift(own_b, RING, -1)
     pair_a = shift(other_a, "core", 1)
     pair_b = shift(other_b, "core", 1)
     next_pair = shift(pair_a, RING, 1)
     prev_pair = shift(pair_b, RING, -1)
-    xs = [own_a, pair_a, prev_own, prev_pair, next_own, next_pair, own_b, pair_b]
-
     cot = cotangent_rows(grads, plan[0], counts, lax.axis_index(WIDE))
     cot_pair = shift(cot, "core", 1)
     cot_a = jnp.concatenate([cot[:half], cot_pair[:half]], axis=0)
     cot_b = jnp.concatenate([cot[half:], cot_pair[half:]], axis=0)
-    cots = jnp.concatenate([cot_a, shift(cot_b, RING, -1), shift(cot_a, RING, 1), cot_b], axis=0)
-
+    cot_a, cot_b, next_own, prev_own = lax.optimization_barrier(
+        (cot_a, cot_b, next_own, prev_own)
+    )
+    cots = [cot_a, shift(cot_b, RING, -1), shift(cot_a, RING, 1), cot_b]
+
+    gathered, cots, pick = lax.optimization_barrier(
+        (gathered, cots, unit_order(slab, xl, ys, n, hidden))
+    )
+    xs = [own_a, pair_a, prev_own, prev_pair, next_own, next_pair, own_b, pair_b]
     mine = products(xs, gathered, n, rank, block)
     his = shift(mine, "core", 1)
-    low, up_part = gate_stage(mine, his, cots, unit_order(slab, xl, ys, n, hidden), up, n)
-
-    group = low.shape[0] // 2
-    plus = shift(low[group:], RING, -1)
-    minus = shift(low[:group], RING, 1)
-
-    up_share = exchange(up_part, WIDE).reshape(lanes, rank // lanes, hidden).sum(0)
-    up_all = exchange(jnp.tile(up_share, (copies, 1)), DP)
-    up_share = up_all.reshape(copies, rank // lanes, hidden).sum(0)
-    up_grad = exchange(jnp.tile(up_share, (lanes, 1)), WIDE)
-
-    terms = down_terms(xs, xl_id, low, plus, minus, ys, block)
-    terms = terms.reshape(ys, copies, rank // copies, block).transpose(1, 0, 2, 3)
-    terms = exchange(terms.reshape(copies * ys, rank // copies, block), REPLICAS)
-    share = terms.astype(F32).sum(0)
-    full = exchange(jnp.tile(share[None], (copies, 1, 1)), DP)
-    return full.reshape(rank, block).T, up_grad
+    plus, minus = gate_stage(mine, his, cots, pick, up, n)
+    from_prev = shift(plus, RING, 1)
+    from_next = shift(minus, RING, -1)
+
+    terms = down_terms(xs, xl_id, plus, minus, from_next, from_prev, ys, block)
+    lanes = terms.shape[-1]
+    terms = exchange(terms.reshape(copies * ys, 8, lanes), REPLICAS)
+    total = terms.astype(F32).sum(0)
+    full = exchange(jnp.tile(total[None], (copies, 1, 1)), DP)
+    full = full.reshape(2, rank // 8, 8, lanes).transpose(1, 2, 0, 3).reshape(rank, 2 * lanes)
+    return full[:, :block].T, full[:, block:]
 
 
 def solution(mesh):

time: 222 us -> 193 us (0.87)
  blocking collectives: 0 us -> 59.1 us
  starting transfers between devices: 94.5 us -> 46.5 us
  waiting for transfers between devices: 59.5 us -> 37.7 us
  local copies, waits for them, and re-layouts: 22 us -> 10.4 us
  Pallas kernels: 19.8 us -> 16.2 us
    all_to_all x0 -> x2, blocking collectives: none -> 59.1 us  [exchange(): return lax.all_to_all(array, axes, split_axis=0, concat_axis=0, tiled=True)]
    all_to_all x7 -> x2, starting transfers between devices: 53.4 us -> 12.2 us  [exchange(): return lax.all_to_all(array, axes, split_axis=0, concat_axis=0, tiled=True)]
    all_to_all x7 -> x2, waiting for transfers between devices: 41.3 us -> 1.68 us  [exchange(): return lax.all_to_all(array, axes, split_axis=0, concat_axis=0, tiled=True)]
    ppermute x13, waiting for transfers between devices: 11.9 us -> 36 us  [shift(): lax.ppermute(array, axes, [(i, (i + step) % size) for i in range(size)])]
    ppermute x13, starting transfers between devices: 41.1 us -> 34.2 us  [shift(): lax.ppermute(array, axes, [(i, (i + step) % size) for i in range(size)])]
    all_gather x1, waiting for transfers between devices: 6.27 us -> 0.01 us  [shards(): gathered = lax.all_gather(sent[None], 'y', axis=0, tiled=True)]
    unnamed x29 -> x35, local copies, waits for them, and re-layouts: 10.2 us -> 6.09 us
    reshape x4 -> x0, local copies, waits for them, and re-layouts: 2.31 us -> none  [the longest x1 1.19 us: shards(): terms.reshape(copies * ys, rank // copies, block)]
  transfers between devices with their start and end apart: 21 -> 16, of which waited for: 11 -> 8; matrix products, arithmetic and copies ran while one was open for 6% -> 3% of each run, Pallas kernels for 9% -> 1%
where the time goes in v2:
time: 193 us; the launch traced here: 191 us
  blocking collectives  59.1 us (31%)
  starting transfers between devices  46.5 us (24%)
  waiting for transfers between devices  37.7 us (20%)
  Pallas kernels  16.2 us (8%)
  between operations  14.5 us (8%)
  local copies, waits for them, and re-layouts  10.4 us (5%)
  other arithmetic  5.99 us (3%)
    all_to_all x2, blocking collectives, exchange(): return lax.all_to_all(array, axes, split_axis=0, concat_axis=0, tiled=True)  59.1 us
    ppermute x13, waiting for transfers between devices, shift(): lax.ppermute(array, axes, [(i, (i + step) % size) for i in range(size)])  36 us
    ppermute x13, starting transfers between devices, shift(): lax.ppermute(array, axes, [(i, (i + step) % size) for i in range(size)])  34.2 us
    all_to_all x2, starting transfers between devices, exchange(): return lax.all_to_all(array, axes, split_axis=0, concat_axis=0, tiled=True)  12.2 us
    pallas_call x1, Pallas kernels, products(): pl.pallas_call(functools.partial(products_kernel, block=block, rank=rank)...  8.94 us
    unnamed x35, local copies, waits for them, and re-layouts  6.09 us
    pallas_call x1, Pallas kernels, down_terms(): pl.pallas_call(functools.partial(down_kernel, block=block), grid_spec=plt...  3.88 us
  transfers between devices with their start and end apart: 16, of which 8 were waited for; matrix products, arithmetic and copies ran while one was open for 3% of the time, Pallas kernels for 1%

profile of v2, /device:TPU:6, one launch (start us, length us, event | category | flops | bytes accessed | tf_op | source)
XLA Modules:
  0.0 190.7 jit_solution(14990763829066839708)
XLA Ops:
  7.2 0.0 copy-start
  7.2 0.9 copy.20
  8.1 2.7 %collective-permute-start.7 = (bf16[16,2048]{1,0:T(8,128)(2,1)S(1)}, bf16[16,2048]{1,0:T(8,128)(2,1)S(1)}, u32[]{:S(2)}, u32[]{:S(2)}) collective-permute-start(bf16[16,2048]{1,0:T(8,128)(2,1)S(1)} %bitcast.62), channel_id=1, source_target_pairs={{0,2},{2,0},{1,3},{3,1},{4,6},{6,4},{5,7},{7,5},{8,10},{10,8},{9,1... | collective-permute-start | bytes 196616 | tf_op jit(solution)/shard_map/ppermute | solution.py:25
  10.8 0.0 copy-start.5
  10.8 1.0 copy-done.5
  11.8 1.1 split_weights.1
  12.9 3.5 %all-to-all-start.1 = ((bf16[2,4,16,2048]{3,2,1,0:T(8,128)(2,1)}), bf16[2,4,16,2048]{3,2,1,0:T(8,128)(2,1)S(1)}, u32[]{:S(2)}, u32[]{:S(2)}) async-start(bf16[2,4,16,2048]{3,2,1,0:T(8,128)(2,1)} %bitcast.10), calls=%async_computation.1 | async-start | bytes 1048576 | tf_op jit(solution)/shard_map/all_to_all | solution.py:29
  16.4 0.0 all-gather.3.cloned.1.call-start
  16.5 1.7 all-to-all-done.1
  18.3 0.9 pad_maximum_fusion
  19.1 0.0 all-gather.3.cloned.1.call-update
  19.2 0.0 copy-start.3
  19.2 2.2 %copy-done.3 = bf16[128,16384]{1,0:T(8,128)(2,1)S(1)} copy-done((bf16[128,16384]{1,0:T(8,128)(2,1)S(1)}, bf16[128,16384]{1,0:T(8,128)(2,1)}, u32[]{:S(2)}) %copy-start.3) | copy-done | bytes 4194328
  21.4 0.0 copy-start.14
  21.4 1.4 split_rows.1
  22.8 1.0 copy-done.9
  23.8 0.4 select_reduce_fusion
  24.2 0.2 convert_reduce_fusion.1
  24.4 0.2 convolution_convert_fusion.1
  24.5 0.7 all_to_all.17
  25.2 8.7 %all-to-all-start = ((bf16[32,4,256]{2,1,0:T(4,128)(2,1)}), bf16[32,4,256]{2,1,0:T(4,128)(2,1)S(1)}, u32[]{:S(2)}, u32[]{:S(2)}) async-start(bf16[32,4,256]{2,1,0:T(4,128)(2,1)} %all_to_all.17), calls=%async_computation | async-start | bytes 131072 | tf_op jit(solution)/shard_map/all_to_all | solution.py:29
  33.9 2.1 %collective-permute-start = (bf16[4,64,2048]{2,1,0:T(8,128)(2,1)}, bf16[4,64,2048]{2,1,0:T(8,128)(2,1)}, u32[]{:S(2)}, u32[]{:S(2)}) collective-permute-start(bf16[4,64,2048]{2,1,0:T(8,128)(2,1)} %bitcast.53), channel_id=1, source_target_pairs={{0,1},{1,0},{2,3},{3,2},{4,5},{5,4},{6,7},{7,6},{8,9},{9,8},{10,11... | collective-permute-start | bytes 3145736 | tf_op jit(solution)/shard_map/ppermute | solution.py:25
  36.0 2.3 %collective-permute-start.4 = (bf16[4,64,2048]{2,1,0:T(8,128)(2,1)S(1)}, bf16[4,64,2048]{2,1,0:T(8,128)(2,1)}, u32[]{:S(2)}, u32[]{:S(2)}) collective-permute-start(bf16[4,64,2048]{2,1,0:T(8,128)(2,1)S(1)} %bitcast.52), channel_id=1, source_target_pairs={{0,1},{1,0},{2,3},{3,2},{4,5},{5,4},{6,7},{7,6},{8,9},{9,8},{10,11... | collective-permute-start | bytes 3145736 | tf_op jit(solution)/shard_map/ppermute | solution.py:25
  38.3 2.1 %collective-permute-start.2 = (bf16[4,64,2048]{2,1,0:T(8,128)(2,1)S(1)}, bf16[4,64,2048]{2,1,0:T(8,128)(2,1)}, u32[]{:S(2)}, u32[]{:S(2)}) collective-permute-start(bf16[4,64,2048]{2,1,0:T(8,128)(2,1)S(1)} %bitcast.46), channel_id=1, source_target_pairs={{0,2},{2,32},{32,34},{34,0},{1,3},{3,33},{33,35},{35,1},{4,6},{6,3... | collective-permute-start | bytes 3145736 | tf_op jit(solution)/shard_map/ppermute | solution.py:25
  40.4 3.8 %collective-permute-start.3 = (bf16[4,64,2048]{2,1,0:T(8,128)(2,1)S(1)}, bf16[4,64,2048]{2,1,0:T(8,128)(2,1)}, u32[]{:S(2)}, u32[]{:S(2)}) collective-permute-start(bf16[4,64,2048]{2,1,0:T(8,128)(2,1)S(1)} %bitcast.49), channel_id=1, source_target_pairs={{0,34},{2,0},{32,2},{34,32},{1,35},{3,1},{33,3},{35,33},{4,38},{6,... | collective-permute-start | bytes 3145736 | tf_op jit(solution)/shard_map/ppermute | solution.py:25
  44.2 0.6 fusion.25
  44.7 1.3 fusion.21
  46.1 0.7 fusion.24
  46.7 0.1 add_add_fusion.1
  46.8 2.6 %compare_select_fusion.1 = s32[256,1]{0,1:T(1,128)S(1)} fusion(s32[256,1]{0,1:T(1,128)S(1)} %bitcast.68, s32[256,1]{0,1:T(1,128)S(1)} %bitcast.67, s32[]{:T(128)} %bitcast.21, s32[]{:T(128)} %bitcast.22, s32[]{:T(128)} %bitcast.24, s32[]{:T(128)} %bitcast.23), kind=kLoop, calls=%fused_computation.29 | loop fusion | flops 2048 | bytes 3088 | tf_op jit(solution)/shard_map/jit(_take)/gather | solution.py:290
  49.4 0.1 and_select_fusion.7
  49.5 0.2 convert_reduce_fusion.2
  49.7 0.0 collective-permute-done.refs_1_
  49.7 3.3 %collective-permute-start.6 = (bf16[4,64,2048]{2,1,0:T(8,128)(2,1)}, bf16[4,64,2048]{2,1,0:T(8,128)(2,1)}, u32[]{:S(2)}, u32[]{:S(2)}) collective-permute-start(bf16[4,64,2048]{2,1,0:T(8,128)(2,1)} %collective-permute-done.refs_1_), channel_id=1, source_target_pairs={{0,2},{2,32},{32,34},{34,0},{1,3},{3,33},{33,35},{35,1},{4,6},{6,3... | collective-permute-start | bytes 3145736 | tf_op jit(solution)/shard_map/ppermute | solution.py:25
  53.0 0.0 collective-permute-done.4.refs_7_
  53.0 2.5 %collective-permute-start.5 = (bf16[4,64,2048]{2,1,0:T(8,128)(2,1)}, bf16[4,64,2048]{2,1,0:T(8,128)(2,1)}, u32[]{:S(2)}, u32[]{:S(2)}) collective-permute-start(bf16[4,64,2048]{2,1,0:T(8,128)(2,1)} %collective-permute-done.4.refs_7_), channel_id=1, source_target_pairs={{0,34},{2,0},{32,2},{34,32},{1,35},{3,1},{33,3},{35,33},{4,38},{6,... | collective-permute-start | bytes 3145736 | tf_op jit(solution)/shard_map/ppermute | solution.py:25
  55.6 0.2 convolution_convert_fusion
  55.8 1.9 %collective-permute-start.1 = (bf16[128,256]{1,0:T(8,128)(2,1)S(1)}, bf16[128,256]{1,0:T(8,128)(2,1)S(1)}, u32[]{:S(2)}, u32[]{:S(2)}) collective-permute-start(bf16[128,256]{1,0:T(8,128)(2,1)S(1)} %convolution_convert_fusion), channel_id=1, source_target_pairs={{0,1},{1,0},{2,3},{3,2},{4,5},{5,4},{6,7},{7,6},{8,9},{9,8},{10,11... | collective-permute-start | bytes 196616 | tf_op jit(solution)/shard_map/ppermute | solution.py:25
  57.8 1.2 collective-permute-done.1
  59.0 7.3 %collective-permute-done.2.refs_4_ = bf16[4,64,2048]{2,1,0:T(8,128)(2,1)} collective-permute-done((bf16[4,64,2048]{2,1,0:T(8,128)(2,1)S(1)}, bf16[4,64,2048]{2,1,0:T(8,128)(2,1)}, u32[]{:S(2)}, u32[]{:S(2)}) %collective-permute-start.2) | collective-permute-done | bytes 1048608 | tf_op jit(solution)/shard_map/ppermute | solution.py:25
  66.3 3.3 %collective-permute-done.3.refs_2_ = bf16[4,64,2048]{2,1,0:T(8,128)(2,1)} collective-permute-done((bf16[4,64,2048]{2,1,0:T(8,128)(2,1)S(1)}, bf16[4,64,2048]{2,1,0:T(8,128)(2,1)}, u32[]{:S(2)}, u32[]{:S(2)}) %collective-permute-start.3) | collective-permute-done | bytes 1048608 | tf_op jit(solution)/shard_map/ppermute | solution.py:25
  69.6 2.5 %collective-permute-start.9 = (bf16[128,256]{1,0:T(8,128)(2,1)S(1)}, bf16[128,256]{1,0:T(8,128)(2,1)S(1)}, u32[]{:S(2)}, u32[]{:S(2)}) collective-permute-start(bf16[128,256]{1,0:T(8,128)(2,1)S(1)} %get-tuple-element.61.a_ref), channel_id=1, source_target_pairs={{0,2},{2,32},{32,34},{34,0},{1,3},{3,33},{33,35},{35,1},{4,6},{6,3... | collective-permute-start | bytes 196616 | tf_op jit(solution)/shard_map/ppermute | solution.py:25
  72.1 3.3 %collective-permute-start.8 = (bf16[128,256]{1,0:T(8,128)(2,1)S(1)}, bf16[128,256]{1,0:T(8,128)(2,1)S(1)}, u32[]{:S(2)}, u32[]{:S(2)}) collective-permute-start(bf16[128,256]{1,0:T(8,128)(2,1)S(1)} %get-tuple-element.64.b_ref), channel_id=1, source_target_pairs={{0,34},{2,0},{32,2},{34,32},{1,35},{3,1},{33,3},{35,33},{4,38},{6,... | collective-permute-start | bytes 196616 | tf_op jit(solution)/shard_map/ppermute | solution.py:25
  75.4 0.1 and_convert_fusion.pick_ref
  75.6 13.7 %collective-permute-done.9.prev_a_ref = bf16[128,256]{1,0:T(8,128)(2,1)S(1)} collective-permute-done((bf16[128,256]{1,0:T(8,128)(2,1)S(1)}, bf16[128,256]{1,0:T(8,128)(2,1)S(1)}, u32[]{:S(2)}, u32[]{:S(2)}) %collective-permute-start.9) | collective-permute-done | bytes 65568 | tf_op jit(solution)/shard_map/ppermute | solution.py:25
  89.3 3.1 %collective-permute-done.8.next_b_ref = bf16[128,256]{1,0:T(8,128)(2,1)S(1)} collective-permute-done((bf16[128,256]{1,0:T(8,128)(2,1)S(1)}, bf16[128,256]{1,0:T(8,128)(2,1)S(1)}, u32[]{:S(2)}, u32[]{:S(2)}) %collective-permute-start.8) | collective-permute-done | bytes 65568 | tf_op jit(solution)/shard_map/ppermute | solution.py:25
  92.4 8.9 %products.1.mine_ref = f32[512,384]{1,0:T(8,128)} custom-call(bf16[4,64,2048]{2,1,0:T(8,128)(2,1)} %bitcast.47, bf16[4,64,2048]{2,1,0:T(8,128)(2,1)} %collective-permute-done.refs_1_, bf16[4,64,2048]{2,1,0:T(8,128)(2,1)} %collective-permute-done.3.refs_2_, bf16[4,64,2048]{2,1,0:T(8,128)(2,1)} %collective-permute-done.5.refs_3_, ...), custom_call_target="tpu_custom_call" | custom-call | flops 2684354560 | bytes 13631488 | tf_op jit(solution)/shard_map/products/pallas_call | solution.py:133
  101.4 1.9 %collective-permute-start.10 = (f32[512,384]{1,0:T(8,128)}, f32[512,384]{1,0:T(8,128)S(1)}, u32[]{:S(2)}, u32[]{:S(2)}) collective-permute-start(f32[512,384]{1,0:T(8,128)} %products.1.mine_ref), channel_id=1, source_target_pairs={{0,1},{1,0},{2,3},{3,2},{4,5},{5,4},{6,7},{7,6},{8,9},{9,8},{10,11... | collective-permute-start | bytes 2359304 | tf_op jit(solution)/shard_map/ppermute | solution.py:25
  103.3 2.5 %collective-permute-done.10.his_ref = f32[512,384]{1,0:T(8,128)S(1)} collective-permute-done((f32[512,384]{1,0:T(8,128)}, f32[512,384]{1,0:T(8,128)S(1)}, u32[]{:S(2)}, u32[]{:S(2)}) %collective-permute-start.10) | collective-permute-done | bytes 786464 | tf_op jit(solution)/shard_map/ppermute | solution.py:25
  105.8 1.1 copy-done.4
  106.9 0.9 gate_stage.1
  107.8 0.0 copy-start.6
  107.8 2.4 %collective-permute-start.12 = (f32[256,128]{1,0:T(8,128)S(1)}, f32[256,128]{1,0:T(8,128)S(1)}, u32[]{:S(2)}, u32[]{:S(2)}) collective-permute-start(f32[256,128]{1,0:T(8,128)S(1)} %get-tuple-element.66.refs_8_), channel_id=1, source_target_pairs={{0,2},{2,32},{32,34},{34,0},{1,3},{3,33},{33,35},{35,1},{4,6},{6,3... | collective-permute-start | bytes 393224 | tf_op jit(solution)/shard_map/ppermute | solution.py:25
  110.2 3.5 %collective-permute-start.11 = (f32[256,64]{1,0:T(8,128)S(1)}, f32[256,64]{1,0:T(8,128)S(1)}, u32[]{:S(2)}, u32[]{:S(2)}) collective-permute-start(f32[256,64]{1,0:T(8,128)S(1)} %get-tuple-element.67.refs_9_), channel_id=1, source_target_pairs={{0,34},{2,0},{32,2},{34,32},{1,35},{3,1},{33,3},{35,33},{4,38},{6,... | collective-permute-start | bytes 196616 | tf_op jit(solution)/shard_map/ppermute | solution.py:25
  113.6 4.9 %collective-permute-done.11.refs_10_ = f32[256,64]{1,0:T(8,128)S(1)} collective-permute-done((f32[256,64]{1,0:T(8,128)S(1)}, f32[256,64]{1,0:T(8,128)S(1)}, u32[]{:S(2)}, u32[]{:S(2)}) %collective-permute-start.11) | collective-permute-done | bytes 65568 | tf_op jit(solution)/shard_map/ppermute | solution.py:25
  118.5 0.6 copy-done.11
  119.2 0.0 copy-done.10
  119.2 3.9 %down_terms.1 = bf16[16,8,8,384]{3,2,1,0:T(8,128)(2,1)} custom-call(s32[1]{0:T(128)} %bitcast.xl_ref, bf16[4,64,2048]{2,1,0:T(8,128)(2,1)} %bitcast.48, bf16[4,64,2048]{2,1,0:T(8,128)(2,1)} %collective-permute-done.refs_1_, bf16[4,64,2048]{2,1,0:T(8,128)(2,1)} %collective-permute-done.3.refs_2_, bf16[4,64,2048]{2,1,0:T(8,128)(2,1)} %collective-permute-done.5.refs_3_, ...), custom_call_target="tpu_custom_call" | custom-call | flops 268435456 | bytes 4718592 | tf_op jit(solution)/shard_map/down_terms/pallas_call | solution.py:237
  123.1 42.7 %all_to_all.27 = bf16[128,8,384]{2,1,0:T(8,128)(2,1)S(1)} all-to-all(bf16[128,8,384]{2,1,0:T(8,128)(2,1)} %bitcast.56), channel_id=1, replica_groups=mesh['z'=8,'xh'=2,'y'=8,'xl'=2,'core'=2] {'z','xh','y'}, dimensions={0} | all-to-all | bytes 1572864 | tf_op jit(solution)/shard_map/all_to_all | solution.py:29
  165.8 0.2 convert_reduce_fusion
  166.0 16.4 %all_to_all.28 = f32[16,8,384]{2,1,0:T(8,128)S(1)} all-to-all(f32[16,8,384]{2,1,0:T(8,128)S(1)} %tile.2), channel_id=1, replica_groups=mesh['z'=8,'xh'=2,'y'=8,'xl'=2,'core'=2] {'z','xh'}, dimensions={0} | all-to-all | bytes 393216 | tf_op jit(solution)/shard_map/all_to_all | solution.py:29
  182.4 0.2 copy.23
  182.6 0.6 slice.66
  183.2 0.7 slice_bitcast_fusion
  (44 shorter events, 0.2 us)
Async XLA Ops:
  7.2 17.2 %copy-start = (bf16[128,256]{1,0:T(8,128)(2,1)S(1)}, bf16[128,256]{1,0:T(8,128)(2,1)}, u32[]{:S(2)}) copy-start(bf16[128,256]{1,0:T(8,128)(2,1)} %param.13) | copy-start | bytes 196612
  8.1 10.2 %collective-permute-start.7 = (bf16[16,2048]{1,0:T(8,128)(2,1)S(1)}, bf16[16,2048]{1,0:T(8,128)(2,1)S(1)}, u32[]{:S(2)}, u32[]{:S(2)}) collective-permute-start(bf16[16,2048]{1,0:T(8,128)(2,1)S(1)} %bitcast.62), channel_id=1, source_target_pairs={{0,2},{2,0},{1,3},{3,1},{4,6},{6,4},{5,7},{7,5},{8,10},{10,8},{9,1... | collective-permute-start | bytes 196616 | tf_op jit(solution)/shard_map/ppermute | solution.py:25
  10.8 1.0 copy-start.5
  12.9 5.2 %all-to-all-start.1 = ((bf16[2,4,16,2048]{3,2,1,0:T(8,128)(2,1)}), bf16[2,4,16,2048]{3,2,1,0:T(8,128)(2,1)S(1)}, u32[]{:S(2)}, u32[]{:S(2)}) async-start(bf16[2,4,16,2048]{3,2,1,0:T(8,128)(2,1)} %bitcast.10), calls=%async_computation.1 | async-start | bytes 1048576 | tf_op jit(solution)/shard_map/all_to_all | solution.py:29
  16.4 76.0 %all-gather.3.cloned.1.call-start = ((), (), s32[]{:S(2)}) async-start(), calls=%async_computation.4 | async-start | bytes 5898240 | tf_op jit(solution)/shard_map/all_gather | solution.py:322
  19.2 2.2 %copy-start.3 = (bf16[128,16384]{1,0:T(8,128)(2,1)S(1)}, bf16[128,16384]{1,0:T(8,128)(2,1)}, u32[]{:S(2)}) copy-start(bf16[128,16384]{1,0:T(8,128)(2,1)} %x_ref.1) | copy-start | bytes 12582916
  21.4 2.4 %copy-start.12 = (s32[1,4096]{1,0:T(1,128)S(1)}, s32[1,4096]{1,0:T(1,128)}, u32[]{:S(2)}) copy-start(s32[1,4096]{1,0:T(1,128)} %param.19) | copy-start | bytes 49156
  21.4 22.8 %copy-start.15 = (s32[2]{0:T(128)S(1)}, s32[2]{0:T(128)}, u32[]{:S(2)}) copy-start(s32[2]{0:T(128)} %param.18) | copy-start | bytes 28
  21.4 23.4 %copy-start.16 = (pred[128]{0:T(512)(128)(4,1)S(1)}, pred[128]{0:T(512)(128)(4,1)}, u32[]{:S(2)}) copy-start(pred[128]{0:T(512)(128)(4,1)} %constant.309) | copy-start | bytes 388
  21.4 24.7 %copy-start.13 = (s32[4]{0:T(128)S(1)}, s32[4]{0:T(128)}, u32[]{:S(2)}) copy-start(s32[4]{0:T(128)} %param.15) | copy-start | bytes 52
  21.4 25.3 %copy-start.14 = (s32[2,128]{1,0:T(2,128)S(1)}, s32[2,128]{1,0:T(2,128)}, u32[]{:S(2)}) copy-start(s32[2,128]{1,0:T(2,128)} %constant.291.clone.1) | copy-start | bytes 3076
  22.8 1.0 copy-start.9
  23.8 68.6 %copy-start.1 = (bf16[2,2,64,2048]{3,2,1,0:T(8,128)(2,1)}, bf16[2,2,64,2048]{3,2,1,0:T(8,128)(2,1)S(1)}, u32[]{:S(2)}) copy-start(bf16[2,2,64,2048]{3,2,1,0:T(8,128)(2,1)S(1)} %get-tuple-element.47) | copy-start | bytes 3145732
  23.8 68.6 %copy-start.2 = (bf16[2,2,64,2048]{3,2,1,0:T(8,128)(2,1)}, bf16[2,2,64,2048]{3,2,1,0:T(8,128)(2,1)S(1)}, u32[]{:S(2)}) copy-start(bf16[2,2,64,2048]{3,2,1,0:T(8,128)(2,1)S(1)} %get-tuple-element.48) | copy-start | bytes 3145732
  25.2 30.4 %all-to-all-start = ((bf16[32,4,256]{2,1,0:T(4,128)(2,1)}), bf16[32,4,256]{2,1,0:T(4,128)(2,1)S(1)}, u32[]{:S(2)}, u32[]{:S(2)}) async-start(bf16[32,4,256]{2,1,0:T(4,128)(2,1)} %all_to_all.17), calls=%async_computation | async-start | bytes 131072 | tf_op jit(solution)/shard_map/all_to_all | solution.py:29
  33.9 15.7 %collective-permute-start = (bf16[4,64,2048]{2,1,0:T(8,128)(2,1)}, bf16[4,64,2048]{2,1,0:T(8,128)(2,1)}, u32[]{:S(2)}, u32[]{:S(2)}) collective-permute-start(bf16[4,64,2048]{2,1,0:T(8,128)(2,1)} %bitcast.53), channel_id=1, source_target_pairs={{0,1},{1,0},{2,3},{3,2},{4,5},{5,4},{6,7},{7,6},{8,9},{9,8},{10,11... | collective-permute-start | bytes 3145736 | tf_op jit(solution)/shard_map/ppermute | solution.py:25
  36.0 17.0 %collective-permute-start.4 = (bf16[4,64,2048]{2,1,0:T(8,128)(2,1)S(1)}, bf16[4,64,2048]{2,1,0:T(8,128)(2,1)}, u32[]{:S(2)}, u32[]{:S(2)}) collective-permute-start(bf16[4,64,2048]{2,1,0:T(8,128)(2,1)S(1)} %bitcast.52), channel_id=1, source_target_pairs={{0,1},{1,0},{2,3},{3,2},{4,5},{5,4},{6,7},{7,6},{8,9},{9,8},{10,11... | collective-permute-start | bytes 3145736 | tf_op jit(solution)/shard_map/ppermute | solution.py:25
  38.3 28.0 %collective-permute-start.2 = (bf16[4,64,2048]{2,1,0:T(8,128)(2,1)S(1)}, bf16[4,64,2048]{2,1,0:T(8,128)(2,1)}, u32[]{:S(2)}, u32[]{:S(2)}) collective-permute-start(bf16[4,64,2048]{2,1,0:T(8,128)(2,1)S(1)} %bitcast.46), channel_id=1, source_target_pairs={{0,2},{2,32},{32,34},{34,0},{1,3},{3,33},{33,35},{35,1},{4,6},{6,3... | collective-permute-start | bytes 3145736 | tf_op jit(solution)/shard_map/ppermute | solution.py:25
  40.4 29.2 %collective-permute-start.3 = (bf16[4,64,2048]{2,1,0:T(8,128)(2,1)S(1)}, bf16[4,64,2048]{2,1,0:T(8,128)(2,1)}, u32[]{:S(2)}, u32[]{:S(2)}) collective-permute-start(bf16[4,64,2048]{2,1,0:T(8,128)(2,1)S(1)} %bitcast.49), channel_id=1, source_target_pairs={{0,34},{2,0},{32,2},{34,32},{1,35},{3,1},{33,3},{35,33},{4,38},{6,... | collective-permute-start | bytes 3145736 | tf_op jit(solution)/shard_map/ppermute | solution.py:25
  49.7 42.7 %collective-permute-start.6 = (bf16[4,64,2048]{2,1,0:T(8,128)(2,1)}, bf16[4,64,2048]{2,1,0:T(8,128)(2,1)}, u32[]{:S(2)}, u32[]{:S(2)}) collective-permute-start(bf16[4,64,2048]{2,1,0:T(8,128)(2,1)} %collective-permute-done.refs_1_), channel_id=1, source_target_pairs={{0,2},{2,32},{32,34},{34,0},{1,3},{3,33},{33,35},{35,1},{4,6},{6,3... | collective-permute-start | bytes 3145736 | tf_op jit(solution)/shard_map/ppermute | solution.py:25
  53.0 39.4 %collective-permute-start.5 = (bf16[4,64,2048]{2,1,0:T(8,128)(2,1)}, bf16[4,64,2048]{2,1,0:T(8,128)(2,1)}, u32[]{:S(2)}, u32[]{:S(2)}) collective-permute-start(bf16[4,64,2048]{2,1,0:T(8,128)(2,1)} %collective-permute-done.4.refs_7_), channel_id=1, source_target_pairs={{0,34},{2,0},{32,2},{34,32},{1,35},{3,1},{33,3},{35,33},{4,38},{6,... | collective-permute-start | bytes 3145736 | tf_op jit(solution)/shard_map/ppermute | solution.py:25
  55.8 3.1 %collective-permute-start.1 = (bf16[128,256]{1,0:T(8,128)(2,1)S(1)}, bf16[128,256]{1,0:T(8,128)(2,1)S(1)}, u32[]{:S(2)}, u32[]{:S(2)}) collective-permute-start(bf16[128,256]{1,0:T(8,128)(2,1)S(1)} %convolution_convert_fusion), channel_id=1, source_target_pairs={{0,1},{1,0},{2,3},{3,2},{4,5},{5,4},{6,7},{7,6},{8,9},{9,8},{10,11... | collective-permute-start | bytes 196616 | tf_op jit(solution)/shard_map/ppermute | solution.py:25
  69.6 19.7 %collective-permute-start.9 = (bf16[128,256]{1,0:T(8,128)(2,1)S(1)}, bf16[128,256]{1,0:T(8,128)(2,1)S(1)}, u32[]{:S(2)}, u32[]{:S(2)}) collective-permute-start(bf16[128,256]{1,0:T(8,128)(2,1)S(1)} %get-tuple-element.61.a_ref), channel_id=1, source_target_pairs={{0,2},{2,32},{32,34},{34,0},{1,3},{3,33},{33,35},{35,1},{4,6},{6,3... | collective-permute-start | bytes 196616 | tf_op jit(solution)/shard_map/ppermute | solution.py:25
  72.1 20.3 %collective-permute-start.8 = (bf16[128,256]{1,0:T(8,128)(2,1)S(1)}, bf16[128,256]{1,0:T(8,128)(2,1)S(1)}, u32[]{:S(2)}, u32[]{:S(2)}) collective-permute-start(bf16[128,256]{1,0:T(8,128)(2,1)S(1)} %get-tuple-element.64.b_ref), channel_id=1, source_target_pairs={{0,34},{2,0},{32,2},{34,32},{1,35},{3,1},{33,3},{35,33},{4,38},{6,... | collective-permute-start | bytes 196616 | tf_op jit(solution)/shard_map/ppermute | solution.py:25
  92.4 13.4 %copy-start.8 = (bf16[64,256]{1,0:T(8,128)(2,1)S(1)}, bf16[64,256]{1,0:T(8,128)(2,1)}, u32[]{:S(2)}) copy-start(bf16[64,256]{1,0:T(8,128)(2,1)} %up_ref.1) | copy-start | bytes 98308
  101.4 4.4 %collective-permute-start.10 = (f32[512,384]{1,0:T(8,128)}, f32[512,384]{1,0:T(8,128)S(1)}, u32[]{:S(2)}, u32[]{:S(2)}) collective-permute-start(f32[512,384]{1,0:T(8,128)} %products.1.mine_ref), channel_id=1, source_target_pairs={{0,1},{1,0},{2,3},{3,2},{4,5},{5,4},{6,7},{7,6},{8,9},{9,8},{10,11... | collective-permute-start | bytes 2359304 | tf_op jit(solution)/shard_map/ppermute | solution.py:25
  105.8 1.1 copy-start.4
  107.8 10.8 %copy-start.6 = (f32[256,128]{1,0:T(8,128)}, f32[256,128]{1,0:T(8,128)S(1)}, u32[]{:S(2)}) copy-start(f32[256,128]{1,0:T(8,128)S(1)} %get-tuple-element.66.refs_8_) | copy-start | bytes 393220
  107.8 10.8 %copy-start.7 = (f32[256,64]{1,0:T(8,128)}, f32[256,64]{1,0:T(8,128)S(1)}, u32[]{:S(2)}) copy-start(f32[256,64]{1,0:T(8,128)S(1)} %get-tuple-element.67.refs_9_) | copy-start | bytes 196612
  107.8 10.7 %collective-permute-start.12 = (f32[256,128]{1,0:T(8,128)S(1)}, f32[256,128]{1,0:T(8,128)S(1)}, u32[]{:S(2)}, u32[]{:S(2)}) collective-permute-start(f32[256,128]{1,0:T(8,128)S(1)} %get-tuple-element.66.refs_8_), channel_id=1, source_target_pairs={{0,2},{2,32},{32,34},{34,0},{1,3},{3,33},{33,35},{35,1},{4,6},{6,3... | collective-permute-start | bytes 393224 | tf_op jit(solution)/shard_map/ppermute | solution.py:25
  110.2 8.4 %collective-permute-start.11 = (f32[256,64]{1,0:T(8,128)S(1)}, f32[256,64]{1,0:T(8,128)S(1)}, u32[]{:S(2)}, u32[]{:S(2)}) collective-permute-start(f32[256,64]{1,0:T(8,128)S(1)} %get-tuple-element.67.refs_9_), channel_id=1, source_target_pairs={{0,34},{2,0},{32,2},{34,32},{1,35},{3,1},{33,3},{35,33},{4,38},{6,... | collective-permute-start | bytes 196616 | tf_op jit(solution)/shard_map/ppermute | solution.py:25
  118.5 0.6 copy-start.11
  118.5 0.7 copy-start.10
Sparse Core Ops, SparseCore 0:
  19.3 72.0 all-gather.2

commit v3 on v2

--- a/solution.py
+++ b/solution.py
@@ -13,7 +13,6 @@
 DP = ("z", "xh")
 WIDE = ("y", "xl", "core")
 RING = ("xh", "xl")
-REPLICAS = ("z", "xh", "y")
 EVERY = ("z", "xh", "y", "xl", "core")
 MIB = 1024 * 1024
 NT = (((1,), (1,)), ((), ()))
@@ -94,33 +93,53 @@
     return out.reshape(2, 2 * (ys // 4), n, 4 * block)
 
 
-def products_kernel(*refs, block, rank):
-    x_refs, (w_ref, down_ref, out_ref) = refs[:8], refs[8:]
-    x = jnp.concatenate([r[0] for r in x_refs], axis=0)
-    w = w_ref[...].reshape(-1, w_ref.shape[-1])
-    down = jnp.concatenate(
-        [
-            jnp.concatenate(
-                [down_ref[y, :, t * block : (t + 1) * block] for t in range(4)], axis=0
-            )
-            for y in range(4)
-        ],
-        axis=1,
-    )
-    units = w.shape[0]
-    wide = lax.dot_general(x, w, NT, preferred_element_type=F32)
-    low = lax.dot_general(x, down, NT, preferred_element_type=F32)
-
-    @pl.when(pl.program_id(0) == 0)
-    def _():
-        out_ref[:, :units] = wide
-        out_ref[:, units : units + rank] = low
-        out_ref[:, units + rank :] = jnp.zeros_like(out_ref[:, units + rank :])
-
-    @pl.when(pl.program_id(0) > 0)
-    def _():
-        out_ref[:, :units] += wide
-        out_ref[:, units : units + rank] += low
+def products_kernel(*refs, block, rank, n):
+    x_refs, (g_ref, out_ref, w_ref, down_ref, sems) = refs[:8], refs[8:]
+    chunks = x_refs[0].shape[0]
+    ys = g_ref.shape[0]
+    copies = [
+        pltpu.make_async_copy(g_ref.at[:, 2 * chunks * n :, :], down_ref, sems.at[chunks])
+    ] + [
+        pltpu.make_async_copy(
+            g_ref.at[:, 2 * k * n : 2 * (k + 1) * n, :], w_ref.at[k], sems.at[k]
+        )
+        for k in range(chunks)
+    ]
+    for copy in copies:
+        copy.start()
+    copies[0].wait()
+    units = ys * 2 * n
+    part = rank // 4
+    wide = low = None
+    for k in range(chunks):
+        copies[k + 1].wait()
+        x = jnp.concatenate([r[k] for r in x_refs], axis=0)
+        w = w_ref[k].reshape(units, -1)
+        xl, first = divmod(k, chunks // 2)
+        down = jnp.concatenate(
+            [
+                jnp.concatenate(
+                    [
+                        down_ref[
+                            first * 4 + y,
+                            xl * part : (xl + 1) * part,
+                            t * block : (t + 1) * block,
+                        ]
+                        for t in range(4)
+                    ],
+                    axis=0,
+                )
+                for y in range(4)
+            ],
+            axis=1,
+        )
+        more_wide = lax.dot_general(x, w, NT, preferred_element_type=F32)
+        more_low = lax.dot_general(x, down, NT, preferred_element_type=F32)
+        wide = more_wide if wide is None else wide + more_wide
+        low = more_low if low is None else low + more_low
+    out_ref[:, :units] = wide
+    out_ref[:, units : units + rank] = low
+    out_ref[:, units + rank :] = jnp.zeros_like(out_ref[:, units + rank :])
 
 
 def products(xs, gathered, n, rank, block):
@@ -128,26 +147,25 @@
     ys = gathered.shape[0]
     units = ys * 2 * n
     columns = units + pl.cdiv(rank, 128) * 128
-    x_spec = pl.BlockSpec((1, part, lanes), lambda k: (k, 0, 0))
-    per = chunks // 2
+    vm = pl.BlockSpec(memory_space=pltpu.VMEM)
     return pl.pallas_call(
-        functools.partial(products_kernel, block=block, rank=rank),
-        grid=(chunks,),
-        in_specs=[x_spec] * 8
-        + [
-            pl.BlockSpec((ys, 2 * n, lanes), lambda k: (0, k, 0)),
-            pl.BlockSpec((4, rank // 4, lanes), lambda k: (k % per, 2 * chunks + k // per, 0)),
+        functools.partial(products_kernel, block=block, rank=rank, n=n),
+        in_specs=[vm] * 8 + [pl.BlockSpec(memory_space=pltpu.HBM)],
+        out_specs=vm,
+        out_shape=jax.ShapeDtypeStruct((8 * part, columns), F32),
+        scratch_shapes=[
+            pltpu.VMEM((chunks, ys, 2 * n, lanes), BF16),
+            pltpu.VMEM((ys, rank // 2, lanes), BF16),
+            pltpu.SemaphoreType.DMA((chunks + 1,)),
         ],
-        out_specs=pl.BlockSpec((8 * part, columns), lambda k: (0, 0)),
-        out_shape=jax.ShapeDtypeStruct((8 * part, columns), F32),
-        compiler_params=params(60),
+        compiler_params=params(51),
         cost_estimate=pl.CostEstimate(
             flops=2 * 8 * part * chunks * lanes * (units + rank),
             bytes_accessed=(8 * part + units + rank) * chunks * lanes * 2,
             transcendentals=0,
         ),
         name="products",
-    )(*xs, gathered, gathered)
+    )(*xs, gathered)
 
 
 def swap_pairs(ref, part):
@@ -214,36 +232,26 @@
     up = jnp.concatenate(
         [up[i * rank : (i + 1) * rank] for i in range(up.shape[0] // rank)], axis=1
     )
-    x = jnp.concatenate([r[0] for r in x_refs], axis=0)
-    terms = lax.dot_general(low, x, TN, preferred_element_type=F32)
-    lanes = out_ref.shape[-1]
-    for i in range(4):
-        row = jnp.concatenate([terms[:, i * block : (i + 1) * block], up], axis=1)
-        for h in range(2):
+    per = x_refs[0].shape[0] // 2
+    for k in range(per):
+        x = jnp.concatenate([r[xl_ref[0] * per + k] for r in x_refs], axis=0)
+        terms = lax.dot_general(low, x, TN, preferred_element_type=F32)
+        for i in range(4):
+            row = jnp.concatenate([terms[:, i * block : (i + 1) * block], up], axis=1)
             for g in range(rank // 8):
-                piece = row[g * 8 : (g + 1) * 8, h * lanes : (h + 1) * lanes]
-                out_ref[h * (rank // 8) + g, i] = piece.astype(BF16)
+                out_ref[g, k * 4 + i] = row[g * 8 : (g + 1) * 8].astype(BF16)
 
 
 def down_terms(xs, xl, plus, minus, from_next, from_prev, ys, block):
-    chunks, part, lanes = xs[0].shape
-    per = chunks // 2
     group, rank = minus.shape
     hidden = group // rank * rank
-    piece = (block + hidden) // 2
-    x_spec = pl.BlockSpec((1, part, lanes), lambda k, v: (v[0] * per + k, 0, 0))
-    both = pl.BlockSpec((group, 2 * rank), lambda k, v: (0, 0))
-    single = pl.BlockSpec((group, rank), lambda k, v: (0, 0))
+    vm = pl.BlockSpec(memory_space=pltpu.VMEM)
     return pl.pallas_call(
         functools.partial(down_kernel, block=block),
-        grid_spec=pltpu.PrefetchScalarGridSpec(
-            num_scalar_prefetch=1,
-            grid=(per,),
-            in_specs=[x_spec] * 8 + [both, single, single, both],
-            out_specs=pl.BlockSpec((rank // 4, 4, 8, piece), lambda k, v: (0, k, 0, 0)),
-        ),
-        out_shape=jax.ShapeDtypeStruct((rank // 4, ys, 8, piece), BF16),
-        compiler_params=params(60),
+        in_specs=[pl.BlockSpec(memory_space=pltpu.SMEM)] + [vm] * 12,
+        out_specs=vm,
+        out_shape=jax.ShapeDtypeStruct((rank // 8, ys, 8, block + hidden), BF16),
+        compiler_params=params(24),
         cost_estimate=pl.CostEstimate(
             flops=2 * 2 * group * rank * ys * block,
             bytes_accessed=(2 * group + rank) * ys * block * 2,
@@ -321,12 +329,12 @@
     )
     gathered = lax.all_gather(sent[None], "y", axis=0, tiled=True)
 
-    parts = split_rows(x, core_id, ys, block)
-    own_a, own_b, other_a, other_b, grads = lax.optimization_barrier((*parts, grads))
+    own_a, own_b, other_a, other_b = split_rows(x, core_id, ys, block)
     next_own = shift(own_a, RING, 1)
     prev_own = shift(own_b, RING, -1)
     pair_a = shift(other_a, "core", 1)
     pair_b = shift(other_b, "core", 1)
+    pair_a, pair_b, grads = lax.optimization_barrier((pair_a, pair_b, grads))
     next_pair = shift(pair_a, RING, 1)
     prev_pair = shift(pair_b, RING, -1)
     cot = cotangent_rows(grads, plan[0], counts, lax.axis_index(WIDE))
@@ -350,10 +358,10 @@
 
     terms = down_terms(xs, xl_id, plus, minus, from_next, from_prev, ys, block)
     lanes = terms.shape[-1]
-    terms = exchange(terms.reshape(copies * ys, 8, lanes), REPLICAS)
-    total = terms.astype(F32).sum(0)
+    terms = exchange(terms.reshape(-1, 8, lanes), ("z", "y"))
+    total = terms.astype(F32).sum(0).astype(BF16)
     full = exchange(jnp.tile(total[None], (copies, 1, 1)), DP)
-    full = full.reshape(2, rank // 8, 8, lanes).transpose(1, 2, 0, 3).reshape(rank, 2 * lanes)
+    full = full.astype(F32).reshape(rank // 8, -1, 8, lanes).sum(1).reshape(rank, lanes)
     return full[:, :block].T, full[:, block:]
 
 

time: 193 us -> 183 us (0.948)
  blocking collectives: 59.1 us -> 50.5 us
  waiting for transfers between devices: 37.7 us -> 33.1 us
  local copies, waits for them, and re-layouts: 10.4 us -> 8.04 us
  starting transfers between devices: 46.5 us -> 48.8 us
  Pallas kernels: 16.2 us -> 18.3 us
    ppermute x13, waiting for transfers between devices: 36 us -> 22.3 us  [shift(): lax.ppermute(array, axes, [(i, (i + step) % size) for i in range(size)])]
    all_to_all x2, blocking collectives: 59.1 us -> 50.5 us  [exchange(): return lax.all_to_all(array, axes, split_axis=0, concat_axis=0, tiled=True)]
    all_to_all x2, waiting for transfers between devices: 1.68 us -> 7.09 us  [exchange(): return lax.all_to_all(array, axes, split_axis=0, concat_axis=0, tiled=True)]
    ppermute x13, starting transfers between devices: 34.2 us -> 39.5 us  [shift(): lax.ppermute(array, axes, [(i, (i + step) % size) for i in range(size)])]
    all_gather x1, waiting for transfers between devices: 0.01 us -> 3.73 us  [shards(): gathered = lax.all_gather(sent[None], 'y', axis=0, tiled=True)]
    all_to_all x2, starting transfers between devices: 12.2 us -> 9.18 us  [exchange(): return lax.all_to_all(array, axes, split_axis=0, concat_axis=0, tiled=True)]
    pallas_call x1, Pallas kernels: 1.38 us -> 3.59 us  [split_rows(): pl.pallas_call(functools.partial(split_rows_kernel, block=block), grid_sp...]
    unnamed x35 -> x26, local copies, waits for them, and re-layouts: 6.09 us -> 3.9 us
  transfers between devices with their start and end apart: 16 -> 16, of which waited for: 8 -> 8; matrix products, arithmetic and copies ran while one was open for 3% -> 4% of each run, Pallas kernels for 1% -> 3%
where the time goes in v3:
time: 183 us; the launch traced here: 180 us
  blocking collectives  50.5 us (28%)
  starting transfers between devices  48.8 us (27%)
  waiting for transfers between devices  33.1 us (18%)
  Pallas kernels  18.3 us (10%)
  between operations  14.4 us (8%)
  local copies, waits for them, and re-layouts  8.04 us (4%)
  other arithmetic  6.93 us (4%)
    all_to_all x2, blocking collectives, exchange(): return lax.all_to_all(array, axes, split_axis=0, concat_axis=0, tiled=True)  50.5 us
    ppermute x13, starting transfers between devices, shift(): lax.ppermute(array, axes, [(i, (i + step) % size) for i in range(size)])  39.5 us
    ppermute x13, waiting for transfers between devices, shift(): lax.ppermute(array, axes, [(i, (i + step) % size) for i in range(size)])  22.3 us
    pallas_call x1, Pallas kernels, products(): pl.pallas_call(functools.partial(products_kernel, block=block, rank=rank,...  9.35 us
    all_to_all x2, starting transfers between devices, exchange(): return lax.all_to_all(array, axes, split_axis=0, concat_axis=0, tiled=True)  9.18 us
    all_to_all x2, waiting for transfers between devices, exchange(): return lax.all_to_all(array, axes, split_axis=0, concat_axis=0, tiled=True)  7.09 us
    unnamed x26, local copies, waits for them, and re-layouts  3.9 us
    all_gather x1, waiting for transfers between devices, shards(): gathered = lax.all_gather(sent[None], 'y', axis=0, tiled=True)  3.73 us
  transfers between devices with their start and end apart: 16, of which 8 were waited for; matrix products, arithmetic and copies ran while one was open for 4% of the time, Pallas kernels for 3%

profile of v3, /device:TPU:6, one launch (start us, length us, event | category | flops | bytes accessed | tf_op | source)
XLA Modules:
  0.0 180.5 jit_solution(16946277384323073035)
XLA Ops:
  7.2 0.0 copy-start
  7.2 0.9 copy.14
  8.1 2.7 %collective-permute-start.7 = (bf16[16,2048]{1,0:T(8,128)(2,1)S(1)}, bf16[16,2048]{1,0:T(8,128)(2,1)S(1)}, u32[]{:S(2)}, u32[]{:S(2)}) collective-permute-start(bf16[16,2048]{1,0:T(8,128)(2,1)S(1)} %bitcast.54), channel_id=1, source_target_pairs={{0,2},{2,0},{1,3},{3,1},{4,6},{6,4},{5,7},{7,5},{8,10},{10,8},{9,1... | collective-permute-start | bytes 196616 | tf_op jit(solution)/shard_map/ppermute | solution.py:24
  10.8 0.0 copy-start.4
  10.8 1.0 copy-done.4
  11.8 1.1 split_weights.1
  13.0 3.5 %all-to-all-start.1 = ((bf16[2,4,16,2048]{3,2,1,0:T(8,128)(2,1)}), bf16[2,4,16,2048]{3,2,1,0:T(8,128)(2,1)S(1)}, u32[]{:S(2)}, u32[]{:S(2)}) async-start(bf16[2,4,16,2048]{3,2,1,0:T(8,128)(2,1)} %bitcast.10), calls=%async_computation.1 | async-start | bytes 1048576 | tf_op jit(solution)/shard_map/all_to_all | solution.py:28
  16.5 0.0 all-gather.3.cloned.1.call-start
  16.5 1.7 all-to-all-done.1
  18.2 0.0 collective-permute-done.7
  18.3 0.9 pad_maximum_fusion
  19.2 0.0 all-gather.3.cloned.1.call-update
  19.2 0.0 copy-start.3
  19.2 2.2 %copy-done.3 = bf16[128,16384]{1,0:T(8,128)(2,1)S(1)} copy-done((bf16[128,16384]{1,0:T(8,128)(2,1)S(1)}, bf16[128,16384]{1,0:T(8,128)(2,1)}, u32[]{:S(2)}) %copy-start.3) | copy-done | bytes 4194328
  21.4 0.0 copy-start.10
  21.4 3.6 %split_rows.1 = (bf16[2,2,64,2048]{3,2,1,0:T(8,128)(2,1)S(1)}, bf16[2,2,64,2048]{3,2,1,0:T(8,128)(2,1)S(1)}, bf16[2,2,64,2048]{3,2,1,0:T(8,128)(2,1)}, bf16[2,2,64,2048]{3,2,1,0:T(8,128)(2,1)}) custom-call(s32[1]{0:T(128)} %bitcast.1.core_ref, bf16[128,16384]{1,0:T(8,128)(2,1)S(1)} %copy-done.3), custom_call_target="tpu_custom_call" | custom-call | bytes 8388608 | tf_op jit(solution)/shard_map/split_rows/pallas_call | solution.py:52
  25.0 2.0 %collective-permute-start = (bf16[4,64,2048]{2,1,0:T(8,128)(2,1)}, bf16[4,64,2048]{2,1,0:T(8,128)(2,1)S(1)}, u32[]{:S(2)}, u32[]{:S(2)}) collective-permute-start(bf16[4,64,2048]{2,1,0:T(8,128)(2,1)} %bitcast.3), channel_id=1, source_target_pairs={{0,1},{1,0},{2,3},{3,2},{4,5},{5,4},{6,7},{7,6},{8,9},{9,8},{10,11... | collective-permute-start | bytes 3145736 | tf_op jit(solution)/shard_map/ppermute | solution.py:24
  27.0 7.0 %collective-permute-start.3 = (bf16[4,64,2048]{2,1,0:T(8,128)(2,1)S(1)}, bf16[4,64,2048]{2,1,0:T(8,128)(2,1)}, u32[]{:S(2)}, u32[]{:S(2)}) collective-permute-start(bf16[4,64,2048]{2,1,0:T(8,128)(2,1)S(1)} %bitcast.42), channel_id=1, source_target_pairs={{0,2},{2,32},{32,34},{34,0},{1,3},{3,33},{33,35},{35,1},{4,6},{6,3... | collective-permute-start | bytes 3145736 | tf_op jit(solution)/shard_map/ppermute | solution.py:24
  34.0 2.0 %collective-permute-start.1 = (bf16[4,64,2048]{2,1,0:T(8,128)(2,1)}, bf16[4,64,2048]{2,1,0:T(8,128)(2,1)}, u32[]{:S(2)}, u32[]{:S(2)}) collective-permute-start(bf16[4,64,2048]{2,1,0:T(8,128)(2,1)} %bitcast.4), channel_id=1, source_target_pairs={{0,1},{1,0},{2,3},{3,2},{4,5},{5,4},{6,7},{7,6},{8,9},{9,8},{10,11... | collective-permute-start | bytes 3145736 | tf_op jit(solution)/shard_map/ppermute | solution.py:24
  36.0 1.9 %collective-permute-start.4 = (bf16[4,64,2048]{2,1,0:T(8,128)(2,1)S(1)}, bf16[4,64,2048]{2,1,0:T(8,128)(2,1)}, u32[]{:S(2)}, u32[]{:S(2)}) collective-permute-start(bf16[4,64,2048]{2,1,0:T(8,128)(2,1)S(1)} %bitcast.45), channel_id=1, source_target_pairs={{0,34},{2,0},{32,2},{34,32},{1,35},{3,1},{33,3},{35,33},{4,38},{6,... | collective-permute-start | bytes 3145736 | tf_op jit(solution)/shard_map/ppermute | solution.py:24
  38.0 0.6 fusion.25
  38.6 0.6 fusion.24
  39.2 0.2 convert_reduce_fusion.2
  39.4 0.4 select_reduce_fusion
  39.8 1.3 fusion.21
  41.1 0.2 convert_reduce_fusion.1
  41.3 0.1 add_add_fusion.1
  41.3 2.4 %compare_select_fusion.1 = s32[256,1]{0,1:T(1,128)S(1)} fusion(s32[256,1]{0,1:T(1,128)S(1)} %bitcast.60, s32[256,1]{0,1:T(1,128)S(1)} %bitcast.59, s32[]{:T(128)} %bitcast.21, s32[]{:T(128)} %bitcast.22, s32[]{:T(128)} %bitcast.24, s32[]{:T(128)} %bitcast.23), kind=kLoop, calls=%fused_computation.28 | loop fusion | flops 2048 | bytes 3088 | tf_op jit(solution)/shard_map/jit(_take)/gather | solution.py:298
  43.7 0.1 and_select_fusion.7
  43.8 0.0 collective-permute-done.refs_1_
  43.8 0.2 convolution_convert_fusion.1
  44.0 0.7 all_to_all.17
  44.7 5.7 %all-to-all-start = ((bf16[32,4,256]{2,1,0:T(4,128)(2,1)}), bf16[32,4,256]{2,1,0:T(4,128)(2,1)S(1)}, u32[]{:S(2)}, u32[]{:S(2)}) async-start(bf16[32,4,256]{2,1,0:T(4,128)(2,1)} %all_to_all.17), calls=%async_computation | async-start | bytes 131072 | tf_op jit(solution)/shard_map/all_to_all | solution.py:28
  50.4 3.3 %collective-permute-start.6 = (bf16[4,64,2048]{2,1,0:T(8,128)(2,1)S(1)}, bf16[4,64,2048]{2,1,0:T(8,128)(2,1)}, u32[]{:S(2)}, u32[]{:S(2)}) collective-permute-start(bf16[4,64,2048]{2,1,0:T(8,128)(2,1)S(1)} %collective-permute-done.refs_1_), channel_id=1, source_target_pairs={{0,2},{2,32},{32,34},{34,0},{1,3},{3,33},{33,35},{35,1},{4,6},{6,3... | collective-permute-start | bytes 3145736 | tf_op jit(solution)/shard_map/ppermute | solution.py:24
  53.7 2.5 %collective-permute-start.5 = (bf16[4,64,2048]{2,1,0:T(8,128)(2,1)}, bf16[4,64,2048]{2,1,0:T(8,128)(2,1)}, u32[]{:S(2)}, u32[]{:S(2)}) collective-permute-start(bf16[4,64,2048]{2,1,0:T(8,128)(2,1)} %collective-permute-done.1.refs_7_), channel_id=1, source_target_pairs={{0,34},{2,0},{32,2},{34,32},{1,35},{3,1},{33,3},{35,33},{4,38},{6,... | collective-permute-start | bytes 3145736 | tf_op jit(solution)/shard_map/ppermute | solution.py:24
  56.2 0.5 fusion.17
  56.8 5.4 %all-to-all-done = bf16[32,4,256]{2,1,0:T(4,128)(2,1)S(1)} async-done(((bf16[32,4,256]{2,1,0:T(4,128)(2,1)}), bf16[32,4,256]{2,1,0:T(4,128)(2,1)S(1)}, u32[]{:S(2)}, u32[]{:S(2)}) %all-to-all-start) | async-done | bytes 65568 | tf_op jit(solution)/shard_map/all_to_all | solution.py:28
  62.2 0.2 convolution_convert_fusion
  62.4 1.9 %collective-permute-start.2 = (bf16[128,256]{1,0:T(8,128)(2,1)S(1)}, bf16[128,256]{1,0:T(8,128)(2,1)S(1)}, u32[]{:S(2)}, u32[]{:S(2)}) collective-permute-start(bf16[128,256]{1,0:T(8,128)(2,1)S(1)} %convolution_convert_fusion), channel_id=1, source_target_pairs={{0,1},{1,0},{2,3},{3,2},{4,5},{5,4},{6,7},{7,6},{8,9},{9,8},{10,11... | collective-permute-start | bytes 196616 | tf_op jit(solution)/shard_map/ppermute | solution.py:24
  64.4 1.2 collective-permute-done.2
  65.6 0.0 collective-permute-done.3.refs_4_
  65.6 6.3 %collective-permute-start.9 = (bf16[128,256]{1,0:T(8,128)(2,1)S(1)}, bf16[128,256]{1,0:T(8,128)(2,1)S(1)}, u32[]{:S(2)}, u32[]{:S(2)}) collective-permute-start(bf16[128,256]{1,0:T(8,128)(2,1)S(1)} %get-tuple-element.57.a_ref), channel_id=1, source_target_pairs={{0,2},{2,32},{32,34},{34,0},{1,3},{3,33},{33,35},{35,1},{4,6},{6,3... | collective-permute-start | bytes 196616 | tf_op jit(solution)/shard_map/ppermute | solution.py:24
  71.9 1.9 %collective-permute-start.8 = (bf16[128,256]{1,0:T(8,128)(2,1)S(1)}, bf16[128,256]{1,0:T(8,128)(2,1)S(1)}, u32[]{:S(2)}, u32[]{:S(2)}) collective-permute-start(bf16[128,256]{1,0:T(8,128)(2,1)S(1)} %get-tuple-element.60.b_ref), channel_id=1, source_target_pairs={{0,34},{2,0},{32,2},{34,32},{1,35},{3,1},{33,3},{35,33},{4,38},{6,... | collective-permute-start | bytes 196616 | tf_op jit(solution)/shard_map/ppermute | solution.py:24
  73.9 0.7 and_convert_fusion.pick_ref
  74.6 6.2 %collective-permute-done.9.prev_a_ref = bf16[128,256]{1,0:T(8,128)(2,1)S(1)} collective-permute-done((bf16[128,256]{1,0:T(8,128)(2,1)S(1)}, bf16[128,256]{1,0:T(8,128)(2,1)S(1)}, u32[]{:S(2)}, u32[]{:S(2)}) %collective-permute-start.9) | collective-permute-done | bytes 65568 | tf_op jit(solution)/shard_map/ppermute | solution.py:24
  80.8 7.7 %collective-permute-done.8.next_b_ref = bf16[128,256]{1,0:T(8,128)(2,1)S(1)} collective-permute-done((bf16[128,256]{1,0:T(8,128)(2,1)S(1)}, bf16[128,256]{1,0:T(8,128)(2,1)S(1)}, u32[]{:S(2)}, u32[]{:S(2)}) %collective-permute-start.8) | collective-permute-done | bytes 65568 | tf_op jit(solution)/shard_map/ppermute | solution.py:24
  88.5 0.6 copy-done.5
  89.1 3.7 %all-gather.3.cloned.1.call-done = bf16[1280,2048]{1,0:T(8,128)(2,1)} async-done(((bf16[160,2048]{1,0:T(8,128)(2,1)}), bf16[1280,2048]{1,0:T(8,128)(2,1)}) %all-gather.3.cloned.1.call-update) | async-done | bytes 5242896 | tf_op jit(solution)/shard_map/all_gather | solution.py:330
  92.9 0.0 collective-permute-done.6.refs_5_
  92.9 0.0 collective-permute-done.5.refs_3_
  92.9 9.4 %products.1.mine_ref = f32[512,384]{1,0:T(8,128)S(1)} custom-call(bf16[4,64,2048]{2,1,0:T(8,128)(2,1)S(1)} %bitcast.43, bf16[4,64,2048]{2,1,0:T(8,128)(2,1)S(1)} %collective-permute-done.refs_1_, bf16[4,64,2048]{2,1,0:T(8,128)(2,1)} %collective-permute-done.4.refs_2_, bf16[4,64,2048]{2,1,0:T(8,128)(2,1)} %collective-permute-done.5.refs_3_, ...), custom_call_target="tpu_custom_call" | custom-call | flops 2684354560 | bytes 13631488 | tf_op jit(solution)/shard_map/products/pallas_call | solution.py:151
  102.2 2.1 %collective-permute-start.10 = (f32[512,384]{1,0:T(8,128)S(1)}, f32[512,384]{1,0:T(8,128)S(1)}, u32[]{:S(2)}, u32[]{:S(2)}) collective-permute-start(f32[512,384]{1,0:T(8,128)S(1)} %products.1.mine_ref), channel_id=1, source_target_pairs={{0,1},{1,0},{2,3},{3,2},{4,5},{5,4},{6,7},{7,6},{8,9},{9,8},{10,11... | collective-permute-start | bytes 2359304 | tf_op jit(solution)/shard_map/ppermute | solution.py:24
  104.3 2.3 %collective-permute-done.10.his_ref = f32[512,384]{1,0:T(8,128)S(1)} collective-permute-done((f32[512,384]{1,0:T(8,128)S(1)}, f32[512,384]{1,0:T(8,128)S(1)}, u32[]{:S(2)}, u32[]{:S(2)}) %collective-permute-start.10) | collective-permute-done | bytes 786464 | tf_op jit(solution)/shard_map/ppermute | solution.py:24
  106.6 0.9 gate_stage.1
  107.4 2.5 %collective-permute-start.12 = (f32[256,128]{1,0:T(8,128)S(1)}, f32[256,128]{1,0:T(8,128)S(1)}, u32[]{:S(2)}, u32[]{:S(2)}) collective-permute-start(f32[256,128]{1,0:T(8,128)S(1)} %get-tuple-element.62.refs_8_), channel_id=1, source_target_pairs={{0,2},{2,32},{32,34},{34,0},{1,3},{3,33},{33,35},{35,1},{4,6},{6,3... | collective-permute-start | bytes 393224 | tf_op jit(solution)/shard_map/ppermute | solution.py:24
  109.9 3.4 %collective-permute-start.11 = (f32[256,64]{1,0:T(8,128)S(1)}, f32[256,64]{1,0:T(8,128)S(1)}, u32[]{:S(2)}, u32[]{:S(2)}) collective-permute-start(f32[256,64]{1,0:T(8,128)S(1)} %get-tuple-element.63.refs_9_), channel_id=1, source_target_pairs={{0,34},{2,0},{32,2},{34,32},{1,35},{3,1},{33,3},{35,33},{4,38},{6,... | collective-permute-start | bytes 196616 | tf_op jit(solution)/shard_map/ppermute | solution.py:24
  113.3 5.0 %collective-permute-done.11.refs_10_ = f32[256,64]{1,0:T(8,128)S(1)} collective-permute-done((f32[256,64]{1,0:T(8,128)S(1)}, f32[256,64]{1,0:T(8,128)S(1)}, u32[]{:S(2)}, u32[]{:S(2)}) %collective-permute-start.11) | collective-permute-done | bytes 65568 | tf_op jit(solution)/shard_map/ppermute | solution.py:24
  118.3 0.0 collective-permute-done.12.refs_11_
  118.3 3.4 %down_terms.1 = bf16[8,8,8,768]{3,2,1,0:T(8,128)(2,1)S(1)} custom-call(s32[1]{0:T(128)} %bitcast.xl_ref, bf16[4,64,2048]{2,1,0:T(8,128)(2,1)S(1)} %bitcast.44, bf16[4,64,2048]{2,1,0:T(8,128)(2,1)S(1)} %collective-permute-done.refs_1_, bf16[4,64,2048]{2,1,0:T(8,128)(2,1)} %collective-permute-done.4.refs_2_, ...), custom_call_target="tpu_custom_call" | custom-call | flops 268435456 | bytes 4718592 | tf_op jit(solution)/shard_map/down_terms/pallas_call | solution.py:249
  121.6 34.6 %all_to_all.27 = bf16[64,8,768]{2,1,0:T(8,128)(2,1)S(1)} all-to-all(bf16[64,8,768]{2,1,0:T(8,128)(2,1)S(1)} %bitcast.48), channel_id=1, replica_groups=mesh['z'=8,'xh'=2,'y'=8,'xl'=2,'core'=2] {'z','y'}, dimensions={0} | all-to-all | bytes 1572864 | tf_op jit(solution)/shard_map/all_to_all | solution.py:28
  156.2 0.1 reduce_sum.51
  156.4 15.9 %all_to_all.28 = bf16[16,8,768]{2,1,0:T(8,128)(2,1)S(1)} all-to-all(bf16[16,8,768]{2,1,0:T(8,128)(2,1)S(1)} %tile.2), channel_id=1, replica_groups=mesh['z'=8,'xh'=2,'y'=8,'xl'=2,'core'=2] {'z','xh'}, dimensions={0} | all-to-all | bytes 393216 | tf_op jit(solution)/shard_map/all_to_all | solution.py:28
  172.3 0.6 slice.66
  173.0 0.7 slice_bitcast_fusion
  (35 shorter events, 0.2 us)
Async XLA Ops:
  7.2 36.7 %copy-start = (bf16[128,256]{1,0:T(8,128)(2,1)S(1)}, bf16[128,256]{1,0:T(8,128)(2,1)}, u32[]{:S(2)}) copy-start(bf16[128,256]{1,0:T(8,128)(2,1)} %param.13) | copy-start | bytes 196612
  8.1 10.2 %collective-permute-start.7 = (bf16[16,2048]{1,0:T(8,128)(2,1)S(1)}, bf16[16,2048]{1,0:T(8,128)(2,1)S(1)}, u32[]{:S(2)}, u32[]{:S(2)}) collective-permute-start(bf16[16,2048]{1,0:T(8,128)(2,1)S(1)} %bitcast.54), channel_id=1, source_target_pairs={{0,2},{2,0},{1,3},{3,1},{4,6},{6,4},{5,7},{7,5},{8,10},{10,8},{9,1... | collective-permute-start | bytes 196616 | tf_op jit(solution)/shard_map/ppermute | solution.py:24
  10.8 1.0 copy-start.4
  13.0 5.2 %all-to-all-start.1 = ((bf16[2,4,16,2048]{3,2,1,0:T(8,128)(2,1)}), bf16[2,4,16,2048]{3,2,1,0:T(8,128)(2,1)S(1)}, u32[]{:S(2)}, u32[]{:S(2)}) async-start(bf16[2,4,16,2048]{3,2,1,0:T(8,128)(2,1)} %bitcast.10), calls=%async_computation.1 | async-start | bytes 1048576 | tf_op jit(solution)/shard_map/all_to_all | solution.py:28
  16.5 76.4 %all-gather.3.cloned.1.call-start = ((), (), s32[]{:S(2)}) async-start(), calls=%async_computation.4 | async-start | bytes 5898240 | tf_op jit(solution)/shard_map/all_gather | solution.py:330
  19.2 2.2 %copy-start.3 = (bf16[128,16384]{1,0:T(8,128)(2,1)S(1)}, bf16[128,16384]{1,0:T(8,128)(2,1)}, u32[]{:S(2)}) copy-start(bf16[128,16384]{1,0:T(8,128)(2,1)} %x_ref.1) | copy-start | bytes 12582916
  21.4 16.6 %copy-start.8 = (s32[1,4096]{1,0:T(1,128)S(1)}, s32[1,4096]{1,0:T(1,128)}, u32[]{:S(2)}) copy-start(s32[1,4096]{1,0:T(1,128)} %param.19) | copy-start | bytes 49156
  21.4 16.6 %copy-start.11 = (s32[2]{0:T(128)S(1)}, s32[2]{0:T(128)}, u32[]{:S(2)}) copy-start(s32[2]{0:T(128)} %param.18) | copy-start | bytes 28
  21.4 17.2 %copy-start.9 = (s32[4]{0:T(128)S(1)}, s32[4]{0:T(128)}, u32[]{:S(2)}) copy-start(s32[4]{0:T(128)} %param.15) | copy-start | bytes 52
  21.4 18.4 %copy-start.12 = (pred[128]{0:T(512)(128)(4,1)S(1)}, pred[128]{0:T(512)(128)(4,1)}, u32[]{:S(2)}) copy-start(pred[128]{0:T(512)(128)(4,1)} %constant.311) | copy-start | bytes 388
  21.4 19.9 %copy-start.10 = (s32[2,128]{1,0:T(2,128)S(1)}, s32[2,128]{1,0:T(2,128)}, u32[]{:S(2)}) copy-start(s32[2,128]{1,0:T(2,128)} %constant.292.clone.1) | copy-start | bytes 3076
  25.0 67.9 %copy-start.1 = (bf16[2,2,64,2048]{3,2,1,0:T(8,128)(2,1)}, bf16[2,2,64,2048]{3,2,1,0:T(8,128)(2,1)S(1)}, u32[]{:S(2)}) copy-start(bf16[2,2,64,2048]{3,2,1,0:T(8,128)(2,1)S(1)} %get-tuple-element.50) | copy-start | bytes 3145732
  25.0 18.8 %collective-permute-start = (bf16[4,64,2048]{2,1,0:T(8,128)(2,1)}, bf16[4,64,2048]{2,1,0:T(8,128)(2,1)S(1)}, u32[]{:S(2)}, u32[]{:S(2)}) collective-permute-start(bf16[4,64,2048]{2,1,0:T(8,128)(2,1)} %bitcast.3), channel_id=1, source_target_pairs={{0,1},{1,0},{2,3},{3,2},{4,5},{5,4},{6,7},{7,6},{8,9},{9,8},{10,11... | collective-permute-start | bytes 3145736 | tf_op jit(solution)/shard_map/ppermute | solution.py:24
  27.0 38.5 %collective-permute-start.3 = (bf16[4,64,2048]{2,1,0:T(8,128)(2,1)S(1)}, bf16[4,64,2048]{2,1,0:T(8,128)(2,1)}, u32[]{:S(2)}, u32[]{:S(2)}) collective-permute-start(bf16[4,64,2048]{2,1,0:T(8,128)(2,1)S(1)} %bitcast.42), channel_id=1, source_target_pairs={{0,2},{2,32},{32,34},{34,0},{1,3},{3,33},{33,35},{35,1},{4,6},{6,3... | collective-permute-start | bytes 3145736 | tf_op jit(solution)/shard_map/ppermute | solution.py:24
  34.0 9.8 %collective-permute-start.1 = (bf16[4,64,2048]{2,1,0:T(8,128)(2,1)}, bf16[4,64,2048]{2,1,0:T(8,128)(2,1)}, u32[]{:S(2)}, u32[]{:S(2)}) collective-permute-start(bf16[4,64,2048]{2,1,0:T(8,128)(2,1)} %bitcast.4), channel_id=1, source_target_pairs={{0,1},{1,0},{2,3},{3,2},{4,5},{5,4},{6,7},{7,6},{8,9},{9,8},{10,11... | collective-permute-start | bytes 3145736 | tf_op jit(solution)/shard_map/ppermute | solution.py:24
  36.0 29.6 %collective-permute-start.4 = (bf16[4,64,2048]{2,1,0:T(8,128)(2,1)S(1)}, bf16[4,64,2048]{2,1,0:T(8,128)(2,1)}, u32[]{:S(2)}, u32[]{:S(2)}) collective-permute-start(bf16[4,64,2048]{2,1,0:T(8,128)(2,1)S(1)} %bitcast.45), channel_id=1, source_target_pairs={{0,34},{2,0},{32,2},{34,32},{1,35},{3,1},{33,3},{35,33},{4,38},{6,... | collective-permute-start | bytes 3145736 | tf_op jit(solution)/shard_map/ppermute | solution.py:24
  44.7 17.5 %all-to-all-start = ((bf16[32,4,256]{2,1,0:T(4,128)(2,1)}), bf16[32,4,256]{2,1,0:T(4,128)(2,1)S(1)}, u32[]{:S(2)}, u32[]{:S(2)}) async-start(bf16[32,4,256]{2,1,0:T(4,128)(2,1)} %all_to_all.17), calls=%async_computation | async-start | bytes 131072 | tf_op jit(solution)/shard_map/all_to_all | solution.py:28
  50.4 42.5 %collective-permute-start.6 = (bf16[4,64,2048]{2,1,0:T(8,128)(2,1)S(1)}, bf16[4,64,2048]{2,1,0:T(8,128)(2,1)}, u32[]{:S(2)}, u32[]{:S(2)}) collective-permute-start(bf16[4,64,2048]{2,1,0:T(8,128)(2,1)S(1)} %collective-permute-done.refs_1_), channel_id=1, source_target_pairs={{0,2},{2,32},{32,34},{34,0},{1,3},{3,33},{33,35},{35,1},{4,6},{6,3... | collective-permute-start | bytes 3145736 | tf_op jit(solution)/shard_map/ppermute | solution.py:24
  53.7 39.2 %collective-permute-start.5 = (bf16[4,64,2048]{2,1,0:T(8,128)(2,1)}, bf16[4,64,2048]{2,1,0:T(8,128)(2,1)}, u32[]{:S(2)}, u32[]{:S(2)}) collective-permute-start(bf16[4,64,2048]{2,1,0:T(8,128)(2,1)} %collective-permute-done.1.refs_7_), channel_id=1, source_target_pairs={{0,34},{2,0},{32,2},{34,32},{1,35},{3,1},{33,3},{35,33},{4,38},{6,... | collective-permute-start | bytes 3145736 | tf_op jit(solution)/shard_map/ppermute | solution.py:24
  62.4 3.1 %collective-permute-start.2 = (bf16[128,256]{1,0:T(8,128)(2,1)S(1)}, bf16[128,256]{1,0:T(8,128)(2,1)S(1)}, u32[]{:S(2)}, u32[]{:S(2)}) collective-permute-start(bf16[128,256]{1,0:T(8,128)(2,1)S(1)} %convolution_convert_fusion), channel_id=1, source_target_pairs={{0,1},{1,0},{2,3},{3,2},{4,5},{5,4},{6,7},{7,6},{8,9},{9,8},{10,11... | collective-permute-start | bytes 196616 | tf_op jit(solution)/shard_map/ppermute | solution.py:24
  65.6 15.2 %collective-permute-start.9 = (bf16[128,256]{1,0:T(8,128)(2,1)S(1)}, bf16[128,256]{1,0:T(8,128)(2,1)S(1)}, u32[]{:S(2)}, u32[]{:S(2)}) collective-permute-start(bf16[128,256]{1,0:T(8,128)(2,1)S(1)} %get-tuple-element.57.a_ref), channel_id=1, source_target_pairs={{0,2},{2,32},{32,34},{34,0},{1,3},{3,33},{33,35},{35,1},{4,6},{6,3... | collective-permute-start | bytes 196616 | tf_op jit(solution)/shard_map/ppermute | solution.py:24
  71.9 16.5 %collective-permute-start.8 = (bf16[128,256]{1,0:T(8,128)(2,1)S(1)}, bf16[128,256]{1,0:T(8,128)(2,1)S(1)}, u32[]{:S(2)}, u32[]{:S(2)}) collective-permute-start(bf16[128,256]{1,0:T(8,128)(2,1)S(1)} %get-tuple-element.60.b_ref), channel_id=1, source_target_pairs={{0,34},{2,0},{32,2},{34,32},{1,35},{3,1},{33,3},{35,33},{4,38},{6,... | collective-permute-start | bytes 196616 | tf_op jit(solution)/shard_map/ppermute | solution.py:24
  88.5 0.6 copy-start.5
  92.9 13.7 %copy-start.6 = (bf16[128,256]{1,0:T(8,128)(2,1)S(1)}, bf16[128,256]{1,0:T(8,128)(2,1)}, u32[]{:S(2)}) copy-start(bf16[128,256]{1,0:T(8,128)(2,1)} %copy-done.5) | copy-start | bytes 196612
  92.9 13.7 %copy-start.7 = (bf16[64,256]{1,0:T(8,128)(2,1)S(1)}, bf16[64,256]{1,0:T(8,128)(2,1)}, u32[]{:S(2)}) copy-start(bf16[64,256]{1,0:T(8,128)(2,1)} %up_ref.1) | copy-start | bytes 98308
  102.2 16.0 %copy-start.2 = (bf16[2,2,64,2048]{3,2,1,0:T(8,128)(2,1)S(1)}, bf16[2,2,64,2048]{3,2,1,0:T(8,128)(2,1)}, u32[]{:S(2)}) copy-start(bf16[2,2,64,2048]{3,2,1,0:T(8,128)(2,1)} %copy-done.1) | copy-start | bytes 3145732
  102.2 4.3 %collective-permute-start.10 = (f32[512,384]{1,0:T(8,128)S(1)}, f32[512,384]{1,0:T(8,128)S(1)}, u32[]{:S(2)}, u32[]{:S(2)}) collective-permute-start(f32[512,384]{1,0:T(8,128)S(1)} %products.1.mine_ref), channel_id=1, source_target_pairs={{0,1},{1,0},{2,3},{3,2},{4,5},{5,4},{6,7},{7,6},{8,9},{9,8},{10,11... | collective-permute-start | bytes 2359304 | tf_op jit(solution)/shard_map/ppermute | solution.py:24
  107.4 10.8 %collective-permute-start.12 = (f32[256,128]{1,0:T(8,128)S(1)}, f32[256,128]{1,0:T(8,128)S(1)}, u32[]{:S(2)}, u32[]{:S(2)}) collective-permute-start(f32[256,128]{1,0:T(8,128)S(1)} %get-tuple-element.62.refs_8_), channel_id=1, source_target_pairs={{0,2},{2,32},{32,34},{34,0},{1,3},{3,33},{33,35},{35,1},{4,6},{6,3... | collective-permute-start | bytes 393224 | tf_op jit(solution)/shard_map/ppermute | solution.py:24
  109.9 8.4 %collective-permute-start.11 = (f32[256,64]{1,0:T(8,128)S(1)}, f32[256,64]{1,0:T(8,128)S(1)}, u32[]{:S(2)}, u32[]{:S(2)}) collective-permute-start(f32[256,64]{1,0:T(8,128)S(1)} %get-tuple-element.63.refs_9_), channel_id=1, source_target_pairs={{0,34},{2,0},{32,2},{34,32},{1,35},{3,1},{33,3},{35,33},{4,38},{6,... | collective-permute-start | bytes 196616 | tf_op jit(solution)/shard_map/ppermute | solution.py:24
Sparse Core Ops, SparseCore 0:
  19.4 73.4 all-gather.2

commit v4 on v3

--- a/solution.py
+++ b/solution.py
@@ -110,11 +110,9 @@
     copies[0].wait()
     units = ys * 2 * n
     part = rank // 4
-    wide = low = None
+    total = None
     for k in range(chunks):
-        copies[k + 1].wait()
         x = jnp.concatenate([r[k] for r in x_refs], axis=0)
-        w = w_ref[k].reshape(units, -1)
         xl, first = divmod(k, chunks // 2)
         down = jnp.concatenate(
             [
@@ -133,12 +131,11 @@
             ],
             axis=1,
         )
-        more_wide = lax.dot_general(x, w, NT, preferred_element_type=F32)
-        more_low = lax.dot_general(x, down, NT, preferred_element_type=F32)
-        wide = more_wide if wide is None else wide + more_wide
-        low = more_low if low is None else low + more_low
-    out_ref[:, :units] = wide
-    out_ref[:, units : units + rank] = low
+        copies[k + 1].wait()
+        w = jnp.concatenate([w_ref[k].reshape(units, -1), down], axis=0)
+        more = lax.dot_general(w, x, NT, preferred_element_type=F32)
+        total = more if total is None else total + more
+    out_ref[:, : units + rank] = total.T
     out_ref[:, units + rank :] = jnp.zeros_like(out_ref[:, units + rank :])
 
 

time: 183 us -> 181 us (0.989)
  no operation moved by 1% of the time
where the time goes in v4:
time: 181 us; the launch traced here: 179 us
  blocking collectives  50.5 us (28%)
  starting transfers between devices  48.8 us (27%)
  waiting for transfers between devices  33.1 us (18%)
  Pallas kernels  17.1 us (9%)
  between operations  14.4 us (8%)
  local copies, waits for them, and re-layouts  8.04 us (4%)
  other arithmetic  6.93 us (4%)
    all_to_all x2, blocking collectives, exchange(): return lax.all_to_all(array, axes, split_axis=0, concat_axis=0, tiled=True)  50.5 us
    ppermute x13, starting transfers between devices, shift(): lax.ppermute(array, axes, [(i, (i + step) % size) for i in range(size)])  39.5 us
    ppermute x13, waiting for transfers between devices, shift(): lax.ppermute(array, axes, [(i, (i + step) % size) for i in range(size)])  22.3 us
    all_to_all x2, starting transfers between devices, exchange(): return lax.all_to_all(array, axes, split_axis=0, concat_axis=0, tiled=True)  9.18 us
    pallas_call x1, Pallas kernels, products(): pl.pallas_call(functools.partial(products_kernel, block=block, rank=rank,...  8.19 us
    all_to_all x2, waiting for transfers between devices, exchange(): return lax.all_to_all(array, axes, split_axis=0, concat_axis=0, tiled=True)  7.09 us
    unnamed x26, local copies, waits for them, and re-layouts  3.9 us
    all_gather x1, waiting for transfers between devices, shards(): gathered = lax.all_gather(sent[None], 'y', axis=0, tiled=True)  3.73 us
  transfers between devices with their start and end apart: 16, of which 8 were waited for; matrix products, arithmetic and copies ran while one was open for 4% of the time, Pallas kernels for 3%

profile of v4, /device:TPU:6, one launch (start us, length us, event | category | flops | bytes accessed | tf_op | source)
XLA Modules:
  0.0 179.3 jit_solution(15040863282197348726)
XLA Ops:
  7.2 0.0 copy-start
  7.2 0.9 copy.14
  8.1 2.7 %collective-permute-start.7 = (bf16[16,2048]{1,0:T(8,128)(2,1)S(1)}, bf16[16,2048]{1,0:T(8,128)(2,1)S(1)}, u32[]{:S(2)}, u32[]{:S(2)}) collective-permute-start(bf16[16,2048]{1,0:T(8,128)(2,1)S(1)} %bitcast.54), channel_id=1, source_target_pairs={{0,2},{2,0},{1,3},{3,1},{4,6},{6,4},{5,7},{7,5},{8,10},{10,8},{9,1... | collective-permute-start | bytes 196616 | tf_op jit(solution)/shard_map/ppermute | solution.py:24
  10.8 0.0 copy-start.4
  10.8 1.0 copy-done.4
  11.8 1.1 split_weights.1
  13.0 3.5 %all-to-all-start.1 = ((bf16[2,4,16,2048]{3,2,1,0:T(8,128)(2,1)}), bf16[2,4,16,2048]{3,2,1,0:T(8,128)(2,1)S(1)}, u32[]{:S(2)}, u32[]{:S(2)}) async-start(bf16[2,4,16,2048]{3,2,1,0:T(8,128)(2,1)} %bitcast.10), calls=%async_computation.1 | async-start | bytes 1048576 | tf_op jit(solution)/shard_map/all_to_all | solution.py:28
  16.5 0.0 all-gather.3.cloned.1.call-start
  16.5 1.7 all-to-all-done.1
  18.2 0.0 collective-permute-done.7
  18.3 0.9 pad_maximum_fusion
  19.2 0.0 all-gather.3.cloned.1.call-update
  19.2 0.0 copy-start.3
  19.2 2.2 %copy-done.3 = bf16[128,16384]{1,0:T(8,128)(2,1)S(1)} copy-done((bf16[128,16384]{1,0:T(8,128)(2,1)S(1)}, bf16[128,16384]{1,0:T(8,128)(2,1)}, u32[]{:S(2)}) %copy-start.3) | copy-done | bytes 4194328
  21.4 0.0 copy-start.10
  21.4 3.6 %split_rows.1 = (bf16[2,2,64,2048]{3,2,1,0:T(8,128)(2,1)S(1)}, bf16[2,2,64,2048]{3,2,1,0:T(8,128)(2,1)S(1)}, bf16[2,2,64,2048]{3,2,1,0:T(8,128)(2,1)}, bf16[2,2,64,2048]{3,2,1,0:T(8,128)(2,1)}) custom-call(s32[1]{0:T(128)} %bitcast.1.core_ref, bf16[128,16384]{1,0:T(8,128)(2,1)S(1)} %copy-done.3), custom_call_target="tpu_custom_call" | custom-call | bytes 8388608 | tf_op jit(solution)/shard_map/split_rows/pallas_call | solution.py:52
  25.0 2.0 %collective-permute-start = (bf16[4,64,2048]{2,1,0:T(8,128)(2,1)}, bf16[4,64,2048]{2,1,0:T(8,128)(2,1)S(1)}, u32[]{:S(2)}, u32[]{:S(2)}) collective-permute-start(bf16[4,64,2048]{2,1,0:T(8,128)(2,1)} %bitcast.3), channel_id=1, source_target_pairs={{0,1},{1,0},{2,3},{3,2},{4,5},{5,4},{6,7},{7,6},{8,9},{9,8},{10,11... | collective-permute-start | bytes 3145736 | tf_op jit(solution)/shard_map/ppermute | solution.py:24
  27.0 7.0 %collective-permute-start.3 = (bf16[4,64,2048]{2,1,0:T(8,128)(2,1)S(1)}, bf16[4,64,2048]{2,1,0:T(8,128)(2,1)}, u32[]{:S(2)}, u32[]{:S(2)}) collective-permute-start(bf16[4,64,2048]{2,1,0:T(8,128)(2,1)S(1)} %bitcast.42), channel_id=1, source_target_pairs={{0,2},{2,32},{32,34},{34,0},{1,3},{3,33},{33,35},{35,1},{4,6},{6,3... | collective-permute-start | bytes 3145736 | tf_op jit(solution)/shard_map/ppermute | solution.py:24
  34.0 2.0 %collective-permute-start.1 = (bf16[4,64,2048]{2,1,0:T(8,128)(2,1)}, bf16[4,64,2048]{2,1,0:T(8,128)(2,1)}, u32[]{:S(2)}, u32[]{:S(2)}) collective-permute-start(bf16[4,64,2048]{2,1,0:T(8,128)(2,1)} %bitcast.4), channel_id=1, source_target_pairs={{0,1},{1,0},{2,3},{3,2},{4,5},{5,4},{6,7},{7,6},{8,9},{9,8},{10,11... | collective-permute-start | bytes 3145736 | tf_op jit(solution)/shard_map/ppermute | solution.py:24
  36.0 1.9 %collective-permute-start.4 = (bf16[4,64,2048]{2,1,0:T(8,128)(2,1)S(1)}, bf16[4,64,2048]{2,1,0:T(8,128)(2,1)}, u32[]{:S(2)}, u32[]{:S(2)}) collective-permute-start(bf16[4,64,2048]{2,1,0:T(8,128)(2,1)S(1)} %bitcast.45), channel_id=1, source_target_pairs={{0,34},{2,0},{32,2},{34,32},{1,35},{3,1},{33,3},{35,33},{4,38},{6,... | collective-permute-start | bytes 3145736 | tf_op jit(solution)/shard_map/ppermute | solution.py:24
  38.0 0.6 fusion.25
  38.6 0.6 fusion.24
  39.2 0.2 convert_reduce_fusion.2
  39.4 0.4 select_reduce_fusion
  39.8 1.3 fusion.21
  41.1 0.2 convert_reduce_fusion.1
  41.3 0.1 add_add_fusion.1
  41.3 2.4 %compare_select_fusion.1 = s32[256,1]{0,1:T(1,128)S(1)} fusion(s32[256,1]{0,1:T(1,128)S(1)} %bitcast.60, s32[256,1]{0,1:T(1,128)S(1)} %bitcast.59, s32[]{:T(128)} %bitcast.21, s32[]{:T(128)} %bitcast.22, s32[]{:T(128)} %bitcast.24, s32[]{:T(128)} %bitcast.23), kind=kLoop, calls=%fused_computation.28 | loop fusion | flops 2048 | bytes 3088 | tf_op jit(solution)/shard_map/jit(_take)/gather | solution.py:295
  43.7 0.1 and_select_fusion.7
  43.8 0.0 collective-permute-done.refs_1_
  43.8 0.2 convolution_convert_fusion.1
  44.0 0.7 all_to_all.17
  44.7 5.7 %all-to-all-start = ((bf16[32,4,256]{2,1,0:T(4,128)(2,1)}), bf16[32,4,256]{2,1,0:T(4,128)(2,1)S(1)}, u32[]{:S(2)}, u32[]{:S(2)}) async-start(bf16[32,4,256]{2,1,0:T(4,128)(2,1)} %all_to_all.17), calls=%async_computation | async-start | bytes 131072 | tf_op jit(solution)/shard_map/all_to_all | solution.py:28
  50.4 3.3 %collective-permute-start.6 = (bf16[4,64,2048]{2,1,0:T(8,128)(2,1)S(1)}, bf16[4,64,2048]{2,1,0:T(8,128)(2,1)}, u32[]{:S(2)}, u32[]{:S(2)}) collective-permute-start(bf16[4,64,2048]{2,1,0:T(8,128)(2,1)S(1)} %collective-permute-done.refs_1_), channel_id=1, source_target_pairs={{0,2},{2,32},{32,34},{34,0},{1,3},{3,33},{33,35},{35,1},{4,6},{6,3... | collective-permute-start | bytes 3145736 | tf_op jit(solution)/shard_map/ppermute | solution.py:24
  53.7 2.5 %collective-permute-start.5 = (bf16[4,64,2048]{2,1,0:T(8,128)(2,1)}, bf16[4,64,2048]{2,1,0:T(8,128)(2,1)}, u32[]{:S(2)}, u32[]{:S(2)}) collective-permute-start(bf16[4,64,2048]{2,1,0:T(8,128)(2,1)} %collective-permute-done.1.refs_7_), channel_id=1, source_target_pairs={{0,34},{2,0},{32,2},{34,32},{1,35},{3,1},{33,3},{35,33},{4,38},{6,... | collective-permute-start | bytes 3145736 | tf_op jit(solution)/shard_map/ppermute | solution.py:24
  56.2 0.5 fusion.17
  56.8 5.4 %all-to-all-done = bf16[32,4,256]{2,1,0:T(4,128)(2,1)S(1)} async-done(((bf16[32,4,256]{2,1,0:T(4,128)(2,1)}), bf16[32,4,256]{2,1,0:T(4,128)(2,1)S(1)}, u32[]{:S(2)}, u32[]{:S(2)}) %all-to-all-start) | async-done | bytes 65568 | tf_op jit(solution)/shard_map/all_to_all | solution.py:28
  62.2 0.2 convolution_convert_fusion
  62.4 1.9 %collective-permute-start.2 = (bf16[128,256]{1,0:T(8,128)(2,1)S(1)}, bf16[128,256]{1,0:T(8,128)(2,1)S(1)}, u32[]{:S(2)}, u32[]{:S(2)}) collective-permute-start(bf16[128,256]{1,0:T(8,128)(2,1)S(1)} %convolution_convert_fusion), channel_id=1, source_target_pairs={{0,1},{1,0},{2,3},{3,2},{4,5},{5,4},{6,7},{7,6},{8,9},{9,8},{10,11... | collective-permute-start | bytes 196616 | tf_op jit(solution)/shard_map/ppermute | solution.py:24
  64.4 1.2 collective-permute-done.2
  65.6 0.0 collective-permute-done.3.refs_4_
  65.6 6.3 %collective-permute-start.9 = (bf16[128,256]{1,0:T(8,128)(2,1)S(1)}, bf16[128,256]{1,0:T(8,128)(2,1)S(1)}, u32[]{:S(2)}, u32[]{:S(2)}) collective-permute-start(bf16[128,256]{1,0:T(8,128)(2,1)S(1)} %get-tuple-element.57.a_ref), channel_id=1, source_target_pairs={{0,2},{2,32},{32,34},{34,0},{1,3},{3,33},{33,35},{35,1},{4,6},{6,3... | collective-permute-start | bytes 196616 | tf_op jit(solution)/shard_map/ppermute | solution.py:24
  71.9 1.9 %collective-permute-start.8 = (bf16[128,256]{1,0:T(8,128)(2,1)S(1)}, bf16[128,256]{1,0:T(8,128)(2,1)S(1)}, u32[]{:S(2)}, u32[]{:S(2)}) collective-permute-start(bf16[128,256]{1,0:T(8,128)(2,1)S(1)} %get-tuple-element.60.b_ref), channel_id=1, source_target_pairs={{0,34},{2,0},{32,2},{34,32},{1,35},{3,1},{33,3},{35,33},{4,38},{6,... | collective-permute-start | bytes 196616 | tf_op jit(solution)/shard_map/ppermute | solution.py:24
  73.9 0.7 and_convert_fusion.pick_ref
  74.6 6.2 %collective-permute-done.9.prev_a_ref = bf16[128,256]{1,0:T(8,128)(2,1)S(1)} collective-permute-done((bf16[128,256]{1,0:T(8,128)(2,1)S(1)}, bf16[128,256]{1,0:T(8,128)(2,1)S(1)}, u32[]{:S(2)}, u32[]{:S(2)}) %collective-permute-start.9) | collective-permute-done | bytes 65568 | tf_op jit(solution)/shard_map/ppermute | solution.py:24
  80.8 7.7 %collective-permute-done.8.next_b_ref = bf16[128,256]{1,0:T(8,128)(2,1)S(1)} collective-permute-done((bf16[128,256]{1,0:T(8,128)(2,1)S(1)}, bf16[128,256]{1,0:T(8,128)(2,1)S(1)}, u32[]{:S(2)}, u32[]{:S(2)}) %collective-permute-start.8) | collective-permute-done | bytes 65568 | tf_op jit(solution)/shard_map/ppermute | solution.py:24
  88.5 0.6 copy-done.5
  89.1 3.7 %all-gather.3.cloned.1.call-done = bf16[1280,2048]{1,0:T(8,128)(2,1)} async-done(((bf16[160,2048]{1,0:T(8,128)(2,1)}), bf16[1280,2048]{1,0:T(8,128)(2,1)}) %all-gather.3.cloned.1.call-update) | async-done | bytes 5242896 | tf_op jit(solution)/shard_map/all_gather | solution.py:327
  92.9 0.0 collective-permute-done.6.refs_5_
  92.9 0.0 collective-permute-done.5.refs_3_
  92.9 8.2 %products.1.mine_ref = f32[512,384]{1,0:T(8,128)S(1)} custom-call(bf16[4,64,2048]{2,1,0:T(8,128)(2,1)S(1)} %bitcast.43, bf16[4,64,2048]{2,1,0:T(8,128)(2,1)S(1)} %collective-permute-done.refs_1_, bf16[4,64,2048]{2,1,0:T(8,128)(2,1)} %collective-permute-done.4.refs_2_, bf16[4,64,2048]{2,1,0:T(8,128)(2,1)} %collective-permute-done.5.refs_3_, ...), custom_call_target="tpu_custom_call" | custom-call | flops 2684354560 | bytes 13631488 | tf_op jit(solution)/shard_map/products/pallas_call | solution.py:148
  101.1 2.1 %collective-permute-start.10 = (f32[512,384]{1,0:T(8,128)S(1)}, f32[512,384]{1,0:T(8,128)S(1)}, u32[]{:S(2)}, u32[]{:S(2)}) collective-permute-start(f32[512,384]{1,0:T(8,128)S(1)} %products.1.mine_ref), channel_id=1, source_target_pairs={{0,1},{1,0},{2,3},{3,2},{4,5},{5,4},{6,7},{7,6},{8,9},{9,8},{10,11... | collective-permute-start | bytes 2359304 | tf_op jit(solution)/shard_map/ppermute | solution.py:24
  103.1 2.3 %collective-permute-done.10.his_ref = f32[512,384]{1,0:T(8,128)S(1)} collective-permute-done((f32[512,384]{1,0:T(8,128)S(1)}, f32[512,384]{1,0:T(8,128)S(1)}, u32[]{:S(2)}, u32[]{:S(2)}) %collective-permute-start.10) | collective-permute-done | bytes 786464 | tf_op jit(solution)/shard_map/ppermute | solution.py:24
  105.4 0.9 gate_stage.1
  106.3 2.4 %collective-permute-start.12 = (f32[256,128]{1,0:T(8,128)S(1)}, f32[256,128]{1,0:T(8,128)S(1)}, u32[]{:S(2)}, u32[]{:S(2)}) collective-permute-start(f32[256,128]{1,0:T(8,128)S(1)} %get-tuple-element.62.refs_8_), channel_id=1, source_target_pairs={{0,2},{2,32},{32,34},{34,0},{1,3},{3,33},{33,35},{35,1},{4,6},{6,3... | collective-permute-start | bytes 393224 | tf_op jit(solution)/shard_map/ppermute | solution.py:24
  108.7 3.4 %collective-permute-start.11 = (f32[256,64]{1,0:T(8,128)S(1)}, f32[256,64]{1,0:T(8,128)S(1)}, u32[]{:S(2)}, u32[]{:S(2)}) collective-permute-start(f32[256,64]{1,0:T(8,128)S(1)} %get-tuple-element.63.refs_9_), channel_id=1, source_target_pairs={{0,34},{2,0},{32,2},{34,32},{1,35},{3,1},{33,3},{35,33},{4,38},{6,... | collective-permute-start | bytes 196616 | tf_op jit(solution)/shard_map/ppermute | solution.py:24
  112.1 5.0 %collective-permute-done.11.refs_10_ = f32[256,64]{1,0:T(8,128)S(1)} collective-permute-done((f32[256,64]{1,0:T(8,128)S(1)}, f32[256,64]{1,0:T(8,128)S(1)}, u32[]{:S(2)}, u32[]{:S(2)}) %collective-permute-start.11) | collective-permute-done | bytes 65568 | tf_op jit(solution)/shard_map/ppermute | solution.py:24
  117.1 0.0 collective-permute-done.12.refs_11_
  117.1 3.4 %down_terms.1 = bf16[8,8,8,768]{3,2,1,0:T(8,128)(2,1)S(1)} custom-call(s32[1]{0:T(128)} %bitcast.xl_ref, bf16[4,64,2048]{2,1,0:T(8,128)(2,1)S(1)} %bitcast.44, bf16[4,64,2048]{2,1,0:T(8,128)(2,1)S(1)} %collective-permute-done.refs_1_, bf16[4,64,2048]{2,1,0:T(8,128)(2,1)} %collective-permute-done.4.refs_2_, ...), custom_call_target="tpu_custom_call" | custom-call | flops 268435456 | bytes 4718592 | tf_op jit(solution)/shard_map/down_terms/pallas_call | solution.py:246
  120.5 34.6 %all_to_all.27 = bf16[64,8,768]{2,1,0:T(8,128)(2,1)S(1)} all-to-all(bf16[64,8,768]{2,1,0:T(8,128)(2,1)S(1)} %bitcast.48), channel_id=1, replica_groups=mesh['z'=8,'xh'=2,'y'=8,'xl'=2,'core'=2] {'z','y'}, dimensions={0} | all-to-all | bytes 1572864 | tf_op jit(solution)/shard_map/all_to_all | solution.py:28
  155.0 0.1 reduce_sum.51
  155.2 15.9 %all_to_all.28 = bf16[16,8,768]{2,1,0:T(8,128)(2,1)S(1)} all-to-all(bf16[16,8,768]{2,1,0:T(8,128)(2,1)S(1)} %tile.2), channel_id=1, replica_groups=mesh['z'=8,'xh'=2,'y'=8,'xl'=2,'core'=2] {'z','xh'}, dimensions={0} | all-to-all | bytes 393216 | tf_op jit(solution)/shard_map/all_to_all | solution.py:28
  171.1 0.6 slice.66
  171.8 0.7 slice_bitcast_fusion
  (35 shorter events, 0.2 us)
Async XLA Ops:
  7.2 36.7 %copy-start = (bf16[128,256]{1,0:T(8,128)(2,1)S(1)}, bf16[128,256]{1,0:T(8,128)(2,1)}, u32[]{:S(2)}) copy-start(bf16[128,256]{1,0:T(8,128)(2,1)} %param.13) | copy-start | bytes 196612
  8.1 10.2 %collective-permute-start.7 = (bf16[16,2048]{1,0:T(8,128)(2,1)S(1)}, bf16[16,2048]{1,0:T(8,128)(2,1)S(1)}, u32[]{:S(2)}, u32[]{:S(2)}) collective-permute-start(bf16[16,2048]{1,0:T(8,128)(2,1)S(1)} %bitcast.54), channel_id=1, source_target_pairs={{0,2},{2,0},{1,3},{3,1},{4,6},{6,4},{5,7},{7,5},{8,10},{10,8},{9,1... | collective-permute-start | bytes 196616 | tf_op jit(solution)/shard_map/ppermute | solution.py:24
  10.8 1.0 copy-start.4
  13.0 5.2 %all-to-all-start.1 = ((bf16[2,4,16,2048]{3,2,1,0:T(8,128)(2,1)}), bf16[2,4,16,2048]{3,2,1,0:T(8,128)(2,1)S(1)}, u32[]{:S(2)}, u32[]{:S(2)}) async-start(bf16[2,4,16,2048]{3,2,1,0:T(8,128)(2,1)} %bitcast.10), calls=%async_computation.1 | async-start | bytes 1048576 | tf_op jit(solution)/shard_map/all_to_all | solution.py:28
  16.5 76.4 %all-gather.3.cloned.1.call-start = ((), (), s32[]{:S(2)}) async-start(), calls=%async_computation.4 | async-start | bytes 5898240 | tf_op jit(solution)/shard_map/all_gather | solution.py:327
  19.2 2.2 %copy-start.3 = (bf16[128,16384]{1,0:T(8,128)(2,1)S(1)}, bf16[128,16384]{1,0:T(8,128)(2,1)}, u32[]{:S(2)}) copy-start(bf16[128,16384]{1,0:T(8,128)(2,1)} %x_ref.1) | copy-start | bytes 12582916
  21.4 16.6 %copy-start.8 = (s32[1,4096]{1,0:T(1,128)S(1)}, s32[1,4096]{1,0:T(1,128)}, u32[]{:S(2)}) copy-start(s32[1,4096]{1,0:T(1,128)} %param.19) | copy-start | bytes 49156
  21.4 16.6 %copy-start.11 = (s32[2]{0:T(128)S(1)}, s32[2]{0:T(128)}, u32[]{:S(2)}) copy-start(s32[2]{0:T(128)} %param.18) | copy-start | bytes 28
  21.4 17.2 %copy-start.9 = (s32[4]{0:T(128)S(1)}, s32[4]{0:T(128)}, u32[]{:S(2)}) copy-start(s32[4]{0:T(128)} %param.15) | copy-start | bytes 52
  21.4 18.4 %copy-start.12 = (pred[128]{0:T(512)(128)(4,1)S(1)}, pred[128]{0:T(512)(128)(4,1)}, u32[]{:S(2)}) copy-start(pred[128]{0:T(512)(128)(4,1)} %constant.311) | copy-start | bytes 388
  21.4 19.9 %copy-start.10 = (s32[2,128]{1,0:T(2,128)S(1)}, s32[2,128]{1,0:T(2,128)}, u32[]{:S(2)}) copy-start(s32[2,128]{1,0:T(2,128)} %constant.292.clone.1) | copy-start | bytes 3076
  25.0 67.9 %copy-start.1 = (bf16[2,2,64,2048]{3,2,1,0:T(8,128)(2,1)}, bf16[2,2,64,2048]{3,2,1,0:T(8,128)(2,1)S(1)}, u32[]{:S(2)}) copy-start(bf16[2,2,64,2048]{3,2,1,0:T(8,128)(2,1)S(1)} %get-tuple-element.50) | copy-start | bytes 3145732
  25.0 18.8 %collective-permute-start = (bf16[4,64,2048]{2,1,0:T(8,128)(2,1)}, bf16[4,64,2048]{2,1,0:T(8,128)(2,1)S(1)}, u32[]{:S(2)}, u32[]{:S(2)}) collective-permute-start(bf16[4,64,2048]{2,1,0:T(8,128)(2,1)} %bitcast.3), channel_id=1, source_target_pairs={{0,1},{1,0},{2,3},{3,2},{4,5},{5,4},{6,7},{7,6},{8,9},{9,8},{10,11... | collective-permute-start | bytes 3145736 | tf_op jit(solution)/shard_map/ppermute | solution.py:24
  27.0 38.5 %collective-permute-start.3 = (bf16[4,64,2048]{2,1,0:T(8,128)(2,1)S(1)}, bf16[4,64,2048]{2,1,0:T(8,128)(2,1)}, u32[]{:S(2)}, u32[]{:S(2)}) collective-permute-start(bf16[4,64,2048]{2,1,0:T(8,128)(2,1)S(1)} %bitcast.42), channel_id=1, source_target_pairs={{0,2},{2,32},{32,34},{34,0},{1,3},{3,33},{33,35},{35,1},{4,6},{6,3... | collective-permute-start | bytes 3145736 | tf_op jit(solution)/shard_map/ppermute | solution.py:24
  34.0 9.8 %collective-permute-start.1 = (bf16[4,64,2048]{2,1,0:T(8,128)(2,1)}, bf16[4,64,2048]{2,1,0:T(8,128)(2,1)}, u32[]{:S(2)}, u32[]{:S(2)}) collective-permute-start(bf16[4,64,2048]{2,1,0:T(8,128)(2,1)} %bitcast.4), channel_id=1, source_target_pairs={{0,1},{1,0},{2,3},{3,2},{4,5},{5,4},{6,7},{7,6},{8,9},{9,8},{10,11... | collective-permute-start | bytes 3145736 | tf_op jit(solution)/shard_map/ppermute | solution.py:24
  36.0 29.6 %collective-permute-start.4 = (bf16[4,64,2048]{2,1,0:T(8,128)(2,1)S(1)}, bf16[4,64,2048]{2,1,0:T(8,128)(2,1)}, u32[]{:S(2)}, u32[]{:S(2)}) collective-permute-start(bf16[4,64,2048]{2,1,0:T(8,128)(2,1)S(1)} %bitcast.45), channel_id=1, source_target_pairs={{0,34},{2,0},{32,2},{34,32},{1,35},{3,1},{33,3},{35,33},{4,38},{6,... | collective-permute-start | bytes 3145736 | tf_op jit(solution)/shard_map/ppermute | solution.py:24
  44.7 17.5 %all-to-all-start = ((bf16[32,4,256]{2,1,0:T(4,128)(2,1)}), bf16[32,4,256]{2,1,0:T(4,128)(2,1)S(1)}, u32[]{:S(2)}, u32[]{:S(2)}) async-start(bf16[32,4,256]{2,1,0:T(4,128)(2,1)} %all_to_all.17), calls=%async_computation | async-start | bytes 131072 | tf_op jit(solution)/shard_map/all_to_all | solution.py:28
  50.4 42.5 %collective-permute-start.6 = (bf16[4,64,2048]{2,1,0:T(8,128)(2,1)S(1)}, bf16[4,64,2048]{2,1,0:T(8,128)(2,1)}, u32[]{:S(2)}, u32[]{:S(2)}) collective-permute-start(bf16[4,64,2048]{2,1,0:T(8,128)(2,1)S(1)} %collective-permute-done.refs_1_), channel_id=1, source_target_pairs={{0,2},{2,32},{32,34},{34,0},{1,3},{3,33},{33,35},{35,1},{4,6},{6,3... | collective-permute-start | bytes 3145736 | tf_op jit(solution)/shard_map/ppermute | solution.py:24
  53.7 39.2 %collective-permute-start.5 = (bf16[4,64,2048]{2,1,0:T(8,128)(2,1)}, bf16[4,64,2048]{2,1,0:T(8,128)(2,1)}, u32[]{:S(2)}, u32[]{:S(2)}) collective-permute-start(bf16[4,64,2048]{2,1,0:T(8,128)(2,1)} %collective-permute-done.1.refs_7_), channel_id=1, source_target_pairs={{0,34},{2,0},{32,2},{34,32},{1,35},{3,1},{33,3},{35,33},{4,38},{6,... | collective-permute-start | bytes 3145736 | tf_op jit(solution)/shard_map/ppermute | solution.py:24
  62.4 3.1 %collective-permute-start.2 = (bf16[128,256]{1,0:T(8,128)(2,1)S(1)}, bf16[128,256]{1,0:T(8,128)(2,1)S(1)}, u32[]{:S(2)}, u32[]{:S(2)}) collective-permute-start(bf16[128,256]{1,0:T(8,128)(2,1)S(1)} %convolution_convert_fusion), channel_id=1, source_target_pairs={{0,1},{1,0},{2,3},{3,2},{4,5},{5,4},{6,7},{7,6},{8,9},{9,8},{10,11... | collective-permute-start | bytes 196616 | tf_op jit(solution)/shard_map/ppermute | solution.py:24
  65.6 15.2 %collective-permute-start.9 = (bf16[128,256]{1,0:T(8,128)(2,1)S(1)}, bf16[128,256]{1,0:T(8,128)(2,1)S(1)}, u32[]{:S(2)}, u32[]{:S(2)}) collective-permute-start(bf16[128,256]{1,0:T(8,128)(2,1)S(1)} %get-tuple-element.57.a_ref), channel_id=1, source_target_pairs={{0,2},{2,32},{32,34},{34,0},{1,3},{3,33},{33,35},{35,1},{4,6},{6,3... | collective-permute-start | bytes 196616 | tf_op jit(solution)/shard_map/ppermute | solution.py:24
  71.9 16.5 %collective-permute-start.8 = (bf16[128,256]{1,0:T(8,128)(2,1)S(1)}, bf16[128,256]{1,0:T(8,128)(2,1)S(1)}, u32[]{:S(2)}, u32[]{:S(2)}) collective-permute-start(bf16[128,256]{1,0:T(8,128)(2,1)S(1)} %get-tuple-element.60.b_ref), channel_id=1, source_target_pairs={{0,34},{2,0},{32,2},{34,32},{1,35},{3,1},{33,3},{35,33},{4,38},{6,... | collective-permute-start | bytes 196616 | tf_op jit(solution)/shard_map/ppermute | solution.py:24
  88.5 0.6 copy-start.5
  92.9 12.5 %copy-start.6 = (bf16[128,256]{1,0:T(8,128)(2,1)S(1)}, bf16[128,256]{1,0:T(8,128)(2,1)}, u32[]{:S(2)}) copy-start(bf16[128,256]{1,0:T(8,128)(2,1)} %copy-done.5) | copy-start | bytes 196612
  92.9 12.5 %copy-start.7 = (bf16[64,256]{1,0:T(8,128)(2,1)S(1)}, bf16[64,256]{1,0:T(8,128)(2,1)}, u32[]{:S(2)}) copy-start(bf16[64,256]{1,0:T(8,128)(2,1)} %up_ref.1) | copy-start | bytes 98308
  101.1 16.0 %copy-start.2 = (bf16[2,2,64,2048]{3,2,1,0:T(8,128)(2,1)S(1)}, bf16[2,2,64,2048]{3,2,1,0:T(8,128)(2,1)}, u32[]{:S(2)}) copy-start(bf16[2,2,64,2048]{3,2,1,0:T(8,128)(2,1)} %copy-done.1) | copy-start | bytes 3145732
  101.1 4.3 %collective-permute-start.10 = (f32[512,384]{1,0:T(8,128)S(1)}, f32[512,384]{1,0:T(8,128)S(1)}, u32[]{:S(2)}, u32[]{:S(2)}) collective-permute-start(f32[512,384]{1,0:T(8,128)S(1)} %products.1.mine_ref), channel_id=1, source_target_pairs={{0,1},{1,0},{2,3},{3,2},{4,5},{5,4},{6,7},{7,6},{8,9},{9,8},{10,11... | collective-permute-start | bytes 2359304 | tf_op jit(solution)/shard_map/ppermute | solution.py:24
  106.3 10.8 %collective-permute-start.12 = (f32[256,128]{1,0:T(8,128)S(1)}, f32[256,128]{1,0:T(8,128)S(1)}, u32[]{:S(2)}, u32[]{:S(2)}) collective-permute-start(f32[256,128]{1,0:T(8,128)S(1)} %get-tuple-element.62.refs_8_), channel_id=1, source_target_pairs={{0,2},{2,32},{32,34},{34,0},{1,3},{3,33},{33,35},{35,1},{4,6},{6,3... | collective-permute-start | bytes 393224 | tf_op jit(solution)/shard_map/ppermute | solution.py:24
  108.7 8.4 %collective-permute-start.11 = (f32[256,64]{1,0:T(8,128)S(1)}, f32[256,64]{1,0:T(8,128)S(1)}, u32[]{:S(2)}, u32[]{:S(2)}) collective-permute-start(f32[256,64]{1,0:T(8,128)S(1)} %get-tuple-element.63.refs_9_), channel_id=1, source_target_pairs={{0,34},{2,0},{32,2},{34,32},{1,35},{3,1},{33,3},{35,33},{4,38},{6,... | collective-permute-start | bytes 196616 | tf_op jit(solution)/shard_map/ppermute | solution.py:24
Sparse Core Ops, SparseCore 0:
  19.4 73.4 all-gather.2

commit v5 on v4

--- a/solution.py
+++ b/solution.py
@@ -155,7 +155,7 @@
             pltpu.VMEM((ys, rank // 2, lanes), BF16),
             pltpu.SemaphoreType.DMA((chunks + 1,)),
         ],
-        compiler_params=params(51),
+        compiler_params=params(49),
         cost_estimate=pl.CostEstimate(
             flops=2 * 8 * part * chunks * lanes * (units + rank),
             bytes_accessed=(8 * part + units + rank) * chunks * lanes * 2,
@@ -314,12 +314,16 @@
 
     swapped = exchange(split_weights(frozen, ys, block), "core")
     chunks = swapped.shape[1]
-    down_rows = down.T.reshape(4, rank // 4, block).transpose(1, 0, 2).reshape(rank // 4, 4 * block)
-    near_down = shift(down_rows, "xl", 1)
-    both_down = jnp.where(
-        xl == 0,
-        jnp.concatenate([down_rows, near_down], axis=0),
-        jnp.concatenate([near_down, down_rows], axis=0),
+    near = shift(down.T, "xl", 1)
+    both_down = jnp.concatenate(
+        [
+            jnp.where(xl == half_at, down.T, near)
+            .reshape(4, rank // 4, block)
+            .transpose(1, 0, 2)
+            .reshape(rank // 4, 4 * block)
+            for half_at in range(2)
+        ],
+        axis=0,
     )
     sent = jnp.concatenate(
         [swapped.transpose(1, 0, 2, 3).reshape(chunks * 2 * n, 4 * block), both_down], axis=0

time: 181 us -> 181 us (level)
    unnamed x26 -> x28, local copies, waits for them, and re-layouts: 3.9 us -> 3.9 us
where the time goes in v5:
time: 181 us; the launch traced here: 179 us
  blocking collectives  50.5 us (28%)
  starting transfers between devices  48.9 us (27%)
  waiting for transfers between devices  33 us (18%)
  Pallas kernels  17.1 us (9%)
  between operations  14.5 us (8%)
  local copies, waits for them, and re-layouts  7.17 us (4%)
  other arithmetic  7.07 us (4%)
    all_to_all x2, blocking collectives, exchange(): return lax.all_to_all(array, axes, split_axis=0, concat_axis=0, tiled=True)  50.5 us
    ppermute x13, starting transfers between devices, shift(): lax.ppermute(array, axes, [(i, (i + step) % size) for i in range(size)])  39.7 us
    ppermute x13, waiting for transfers between devices, shift(): lax.ppermute(array, axes, [(i, (i + step) % size) for i in range(size)])  22.2 us
    all_to_all x2, starting transfers between devices, exchange(): return lax.all_to_all(array, axes, split_axis=0, concat_axis=0, tiled=True)  9.19 us
    pallas_call x1, Pallas kernels, products(): pl.pallas_call(functools.partial(products_kernel, block=block, rank=rank,...  8.18 us
    all_to_all x2, waiting for transfers between devices, exchange(): return lax.all_to_all(array, axes, split_axis=0, concat_axis=0, tiled=True)  7.02 us
    unnamed x28, local copies, waits for them, and re-layouts  3.9 us
    all_gather x1, waiting for transfers between devices, shards(): gathered = lax.all_gather(sent[None], 'y', axis=0, tiled=True)  3.69 us
  transfers between devices with their start and end apart: 16, of which 8 were waited for; matrix products, arithmetic and copies ran while one was open for 4% of the time, Pallas kernels for 3%

profile of v5, /device:TPU:6, one launch (start us, length us, event | category | flops | bytes accessed | tf_op | source)
XLA Modules:
  0.0 178.6 jit_solution(2668496814701789427)
XLA Ops:
  7.2 0.0 copy-start
  7.2 2.9 %collective-permute-start.7 = (bf16[64,512]{1,0:T(8,128)(2,1)}, bf16[64,512]{1,0:T(8,128)(2,1)S(1)}, u32[]{:S(2)}, u32[]{:S(2)}) collective-permute-start(bf16[64,512]{1,0:T(8,128)(2,1)} %bitcast.64), channel_id=1, source_target_pairs={{0,2},{2,0},{1,3},{3,1},{4,6},{6,4},{5,7},{7,5},{8,10},{10,8},{9,1... | collective-permute-start | bytes 196616 | tf_op jit(solution)/shard_map/ppermute | solution.py:24
  10.1 1.0 copy-done.4
  11.1 1.1 split_weights.1
  12.2 3.5 %all-to-all-start.1 = ((bf16[2,4,16,2048]{3,2,1,0:T(8,128)(2,1)}), bf16[2,4,16,2048]{3,2,1,0:T(8,128)(2,1)S(1)}, u32[]{:S(2)}, u32[]{:S(2)}) async-start(bf16[2,4,16,2048]{3,2,1,0:T(8,128)(2,1)} %bitcast.10), calls=%async_computation.1 | async-start | bytes 1048576 | tf_op jit(solution)/shard_map/all_to_all | solution.py:28
  15.7 0.0 all-gather.3.cloned.1.call-start
  15.8 1.7 all-to-all-done.1
  17.5 0.0 collective-permute-done.7
  17.6 0.9 pad_maximum_fusion
  18.5 0.0 all-gather.3.cloned.1.call-update
  18.5 0.0 copy-start.3
  18.5 2.2 %copy-done.3 = bf16[128,16384]{1,0:T(8,128)(2,1)S(1)} copy-done((bf16[128,16384]{1,0:T(8,128)(2,1)S(1)}, bf16[128,16384]{1,0:T(8,128)(2,1)}, u32[]{:S(2)}) %copy-start.3) | copy-done | bytes 4194328
  20.7 0.0 copy-start.11
  20.7 3.6 %split_rows.1 = (bf16[2,2,64,2048]{3,2,1,0:T(8,128)(2,1)S(1)}, bf16[2,2,64,2048]{3,2,1,0:T(8,128)(2,1)S(1)}, bf16[2,2,64,2048]{3,2,1,0:T(8,128)(2,1)}, bf16[2,2,64,2048]{3,2,1,0:T(8,128)(2,1)}) custom-call(s32[1]{0:T(128)} %bitcast.1.core_ref, bf16[128,16384]{1,0:T(8,128)(2,1)S(1)} %copy-done.3), custom_call_target="tpu_custom_call" | custom-call | bytes 8388608 | tf_op jit(solution)/shard_map/split_rows/pallas_call | solution.py:52
  24.3 2.0 %collective-permute-start = (bf16[4,64,2048]{2,1,0:T(8,128)(2,1)}, bf16[4,64,2048]{2,1,0:T(8,128)(2,1)S(1)}, u32[]{:S(2)}, u32[]{:S(2)}) collective-permute-start(bf16[4,64,2048]{2,1,0:T(8,128)(2,1)} %bitcast.3), channel_id=1, source_target_pairs={{0,1},{1,0},{2,3},{3,2},{4,5},{5,4},{6,7},{7,6},{8,9},{9,8},{10,11... | collective-permute-start | bytes 3145736 | tf_op jit(solution)/shard_map/ppermute | solution.py:24
  26.4 7.0 %collective-permute-start.3 = (bf16[4,64,2048]{2,1,0:T(8,128)(2,1)S(1)}, bf16[4,64,2048]{2,1,0:T(8,128)(2,1)}, u32[]{:S(2)}, u32[]{:S(2)}) collective-permute-start(bf16[4,64,2048]{2,1,0:T(8,128)(2,1)S(1)} %bitcast.48), channel_id=1, source_target_pairs={{0,2},{2,32},{32,34},{34,0},{1,3},{3,33},{33,35},{35,1},{4,6},{6,3... | collective-permute-start | bytes 3145736 | tf_op jit(solution)/shard_map/ppermute | solution.py:24
  33.3 2.0 %collective-permute-start.1 = (bf16[4,64,2048]{2,1,0:T(8,128)(2,1)}, bf16[4,64,2048]{2,1,0:T(8,128)(2,1)}, u32[]{:S(2)}, u32[]{:S(2)}) collective-permute-start(bf16[4,64,2048]{2,1,0:T(8,128)(2,1)} %bitcast.4), channel_id=1, source_target_pairs={{0,1},{1,0},{2,3},{3,2},{4,5},{5,4},{6,7},{7,6},{8,9},{9,8},{10,11... | collective-permute-start | bytes 3145736 | tf_op jit(solution)/shard_map/ppermute | solution.py:24
  35.3 1.9 %collective-permute-start.4 = (bf16[4,64,2048]{2,1,0:T(8,128)(2,1)S(1)}, bf16[4,64,2048]{2,1,0:T(8,128)(2,1)}, u32[]{:S(2)}, u32[]{:S(2)}) collective-permute-start(bf16[4,64,2048]{2,1,0:T(8,128)(2,1)S(1)} %bitcast.51), channel_id=1, source_target_pairs={{0,34},{2,0},{32,2},{34,32},{1,35},{3,1},{33,3},{35,33},{4,38},{6,... | collective-permute-start | bytes 3145736 | tf_op jit(solution)/shard_map/ppermute | solution.py:24
  37.3 0.6 fusion.25
  37.9 0.6 fusion.24
  38.5 0.2 convert_reduce_fusion.2
  38.7 0.4 select_reduce_fusion
  39.1 1.3 fusion.21
  40.4 0.2 convert_reduce_fusion.1
  40.6 0.1 add_add_fusion.1
  40.7 2.4 %compare_select_fusion.1 = s32[256,1]{0,1:T(1,128)S(1)} fusion(s32[256,1]{0,1:T(1,128)S(1)} %bitcast.68, s32[256,1]{0,1:T(1,128)S(1)} %bitcast.67, s32[]{:T(128)} %bitcast.23, s32[]{:T(128)} %bitcast.24, s32[]{:T(128)} %bitcast.26, s32[]{:T(128)} %bitcast.25), kind=kLoop, calls=%fused_computation.29 | loop fusion | flops 2048 | bytes 3088 | tf_op jit(solution)/shard_map/jit(_take)/gather | solution.py:295
  43.1 0.1 and_select_fusion.7
  43.1 0.0 collective-permute-done.refs_1_
  43.1 0.0 collective-permute-done.1.refs_7_
  43.2 0.2 convolution_convert_fusion.1
  43.3 0.7 all_to_all.17
  44.0 5.7 %all-to-all-start = ((bf16[32,4,256]{2,1,0:T(4,128)(2,1)}), bf16[32,4,256]{2,1,0:T(4,128)(2,1)S(1)}, u32[]{:S(2)}, u32[]{:S(2)}) async-start(bf16[32,4,256]{2,1,0:T(4,128)(2,1)} %all_to_all.17), calls=%async_computation | async-start | bytes 131072 | tf_op jit(solution)/shard_map/all_to_all | solution.py:28
  49.7 3.3 %collective-permute-start.6 = (bf16[4,64,2048]{2,1,0:T(8,128)(2,1)S(1)}, bf16[4,64,2048]{2,1,0:T(8,128)(2,1)}, u32[]{:S(2)}, u32[]{:S(2)}) collective-permute-start(bf16[4,64,2048]{2,1,0:T(8,128)(2,1)S(1)} %collective-permute-done.refs_1_), channel_id=1, source_target_pairs={{0,2},{2,32},{32,34},{34,0},{1,3},{3,33},{33,35},{35,1},{4,6},{6,3... | collective-permute-start | bytes 3145736 | tf_op jit(solution)/shard_map/ppermute | solution.py:24
  53.0 2.6 %collective-permute-start.5 = (bf16[4,64,2048]{2,1,0:T(8,128)(2,1)}, bf16[4,64,2048]{2,1,0:T(8,128)(2,1)}, u32[]{:S(2)}, u32[]{:S(2)}) collective-permute-start(bf16[4,64,2048]{2,1,0:T(8,128)(2,1)} %collective-permute-done.1.refs_7_), channel_id=1, source_target_pairs={{0,34},{2,0},{32,2},{34,32},{1,35},{3,1},{33,3},{35,33},{4,38},{6,... | collective-permute-start | bytes 3145736 | tf_op jit(solution)/shard_map/ppermute | solution.py:24
  55.5 0.6 fusion.17
  56.1 5.3 %all-to-all-done = bf16[32,4,256]{2,1,0:T(4,128)(2,1)S(1)} async-done(((bf16[32,4,256]{2,1,0:T(4,128)(2,1)}), bf16[32,4,256]{2,1,0:T(4,128)(2,1)S(1)}, u32[]{:S(2)}, u32[]{:S(2)}) %all-to-all-start) | async-done | bytes 65568 | tf_op jit(solution)/shard_map/all_to_all | solution.py:28
  61.5 0.2 convolution_convert_fusion
  61.7 1.9 %collective-permute-start.2 = (bf16[128,256]{1,0:T(8,128)(2,1)S(1)}, bf16[128,256]{1,0:T(8,128)(2,1)S(1)}, u32[]{:S(2)}, u32[]{:S(2)}) collective-permute-start(bf16[128,256]{1,0:T(8,128)(2,1)S(1)} %convolution_convert_fusion), channel_id=1, source_target_pairs={{0,1},{1,0},{2,3},{3,2},{4,5},{5,4},{6,7},{7,6},{8,9},{9,8},{10,11... | collective-permute-start | bytes 196616 | tf_op jit(solution)/shard_map/ppermute | solution.py:24
  63.7 1.2 collective-permute-done.2
  64.9 0.0 collective-permute-done.3.refs_4_
  64.9 0.0 collective-permute-done.4.refs_2_
  64.9 6.3 %collective-permute-start.9 = (bf16[128,256]{1,0:T(8,128)(2,1)S(1)}, bf16[128,256]{1,0:T(8,128)(2,1)S(1)}, u32[]{:S(2)}, u32[]{:S(2)}) collective-permute-start(bf16[128,256]{1,0:T(8,128)(2,1)S(1)} %get-tuple-element.57.a_ref), channel_id=1, source_target_pairs={{0,2},{2,32},{32,34},{34,0},{1,3},{3,33},{33,35},{35,1},{4,6},{6,3... | collective-permute-start | bytes 196616 | tf_op jit(solution)/shard_map/ppermute | solution.py:24
  71.3 1.9 %collective-permute-start.8 = (bf16[128,256]{1,0:T(8,128)(2,1)S(1)}, bf16[128,256]{1,0:T(8,128)(2,1)S(1)}, u32[]{:S(2)}, u32[]{:S(2)}) collective-permute-start(bf16[128,256]{1,0:T(8,128)(2,1)S(1)} %get-tuple-element.60.b_ref), channel_id=1, source_target_pairs={{0,34},{2,0},{32,2},{34,32},{1,35},{3,1},{33,3},{35,33},{4,38},{6,... | collective-permute-start | bytes 196616 | tf_op jit(solution)/shard_map/ppermute | solution.py:24
  73.2 0.8 and_convert_fusion.pick_ref
  74.0 6.1 %collective-permute-done.9.prev_a_ref = bf16[128,256]{1,0:T(8,128)(2,1)S(1)} collective-permute-done((bf16[128,256]{1,0:T(8,128)(2,1)S(1)}, bf16[128,256]{1,0:T(8,128)(2,1)S(1)}, u32[]{:S(2)}, u32[]{:S(2)}) %collective-permute-start.9) | collective-permute-done | bytes 65568 | tf_op jit(solution)/shard_map/ppermute | solution.py:24
  80.1 7.7 %collective-permute-done.8.next_b_ref = bf16[128,256]{1,0:T(8,128)(2,1)S(1)} collective-permute-done((bf16[128,256]{1,0:T(8,128)(2,1)S(1)}, bf16[128,256]{1,0:T(8,128)(2,1)S(1)}, u32[]{:S(2)}, u32[]{:S(2)}) %collective-permute-start.8) | collective-permute-done | bytes 65568 | tf_op jit(solution)/shard_map/ppermute | solution.py:24
  87.8 0.6 copy-done.5
  88.4 3.7 %all-gather.3.cloned.1.call-done = bf16[1280,2048]{1,0:T(8,128)(2,1)} async-done(((bf16[160,2048]{1,0:T(8,128)(2,1)}), bf16[1280,2048]{1,0:T(8,128)(2,1)}) %all-gather.3.cloned.1.call-update) | async-done | bytes 5242896 | tf_op jit(solution)/shard_map/all_gather | solution.py:331
  92.1 0.0 collective-permute-done.6.refs_5_
  92.1 0.0 collective-permute-done.5.refs_3_
  92.2 8.2 %products.1.mine_ref = f32[512,384]{1,0:T(8,128)S(1)} custom-call(bf16[4,64,2048]{2,1,0:T(8,128)(2,1)S(1)} %bitcast.49, bf16[4,64,2048]{2,1,0:T(8,128)(2,1)S(1)} %collective-permute-done.refs_1_, bf16[4,64,2048]{2,1,0:T(8,128)(2,1)} %collective-permute-done.4.refs_2_, bf16[4,64,2048]{2,1,0:T(8,128)(2,1)} %collective-permute-done.5.refs_3_, ...), custom_call_target="tpu_custom_call" | custom-call | flops 2684354560 | bytes 13631488 | tf_op jit(solution)/shard_map/products/pallas_call | solution.py:148
  100.4 2.1 %collective-permute-start.10 = (f32[512,384]{1,0:T(8,128)S(1)}, f32[512,384]{1,0:T(8,128)S(1)}, u32[]{:S(2)}, u32[]{:S(2)}) collective-permute-start(f32[512,384]{1,0:T(8,128)S(1)} %products.1.mine_ref), channel_id=1, source_target_pairs={{0,1},{1,0},{2,3},{3,2},{4,5},{5,4},{6,7},{7,6},{8,9},{9,8},{10,11... | collective-permute-start | bytes 2359304 | tf_op jit(solution)/shard_map/ppermute | solution.py:24
  102.4 2.3 %collective-permute-done.10.his_ref = f32[512,384]{1,0:T(8,128)S(1)} collective-permute-done((f32[512,384]{1,0:T(8,128)S(1)}, f32[512,384]{1,0:T(8,128)S(1)}, u32[]{:S(2)}, u32[]{:S(2)}) %collective-permute-start.10) | collective-permute-done | bytes 786464 | tf_op jit(solution)/shard_map/ppermute | solution.py:24
  104.7 0.9 gate_stage.1
  105.5 2.5 %collective-permute-start.12 = (f32[256,128]{1,0:T(8,128)S(1)}, f32[256,128]{1,0:T(8,128)S(1)}, u32[]{:S(2)}, u32[]{:S(2)}) collective-permute-start(f32[256,128]{1,0:T(8,128)S(1)} %get-tuple-element.62.refs_8_), channel_id=1, source_target_pairs={{0,2},{2,32},{32,34},{34,0},{1,3},{3,33},{33,35},{35,1},{4,6},{6,3... | collective-permute-start | bytes 393224 | tf_op jit(solution)/shard_map/ppermute | solution.py:24
  108.0 3.4 %collective-permute-start.11 = (f32[256,64]{1,0:T(8,128)S(1)}, f32[256,64]{1,0:T(8,128)S(1)}, u32[]{:S(2)}, u32[]{:S(2)}) collective-permute-start(f32[256,64]{1,0:T(8,128)S(1)} %get-tuple-element.63.refs_9_), channel_id=1, source_target_pairs={{0,34},{2,0},{32,2},{34,32},{1,35},{3,1},{33,3},{35,33},{4,38},{6,... | collective-permute-start | bytes 196616 | tf_op jit(solution)/shard_map/ppermute | solution.py:24
  111.4 5.0 %collective-permute-done.11.refs_10_ = f32[256,64]{1,0:T(8,128)S(1)} collective-permute-done((f32[256,64]{1,0:T(8,128)S(1)}, f32[256,64]{1,0:T(8,128)S(1)}, u32[]{:S(2)}, u32[]{:S(2)}) %collective-permute-start.11) | collective-permute-done | bytes 65568 | tf_op jit(solution)/shard_map/ppermute | solution.py:24
  116.4 0.0 collective-permute-done.12.refs_11_
  116.4 3.4 %down_terms.1 = bf16[8,8,8,768]{3,2,1,0:T(8,128)(2,1)S(1)} custom-call(s32[1]{0:T(128)} %bitcast.xl_ref, bf16[4,64,2048]{2,1,0:T(8,128)(2,1)S(1)} %bitcast.50, bf16[4,64,2048]{2,1,0:T(8,128)(2,1)S(1)} %collective-permute-done.refs_1_, bf16[4,64,2048]{2,1,0:T(8,128)(2,1)} %collective-permute-done.4.refs_2_, ...), custom_call_target="tpu_custom_call" | custom-call | flops 268435456 | bytes 4718592 | tf_op jit(solution)/shard_map/down_terms/pallas_call | solution.py:246
  119.8 34.6 %all_to_all.27 = bf16[64,8,768]{2,1,0:T(8,128)(2,1)S(1)} all-to-all(bf16[64,8,768]{2,1,0:T(8,128)(2,1)S(1)} %bitcast.54), channel_id=1, replica_groups=mesh['z'=8,'xh'=2,'y'=8,'xl'=2,'core'=2] {'z','y'}, dimensions={0} | all-to-all | bytes 1572864 | tf_op jit(solution)/shard_map/all_to_all | solution.py:28
  154.3 0.1 reduce_sum.51
  154.5 15.9 %all_to_all.28 = bf16[16,8,768]{2,1,0:T(8,128)(2,1)S(1)} all-to-all(bf16[16,8,768]{2,1,0:T(8,128)(2,1)S(1)} %tile.2), channel_id=1, replica_groups=mesh['z'=8,'xh'=2,'y'=8,'xl'=2,'core'=2] {'z','xh'}, dimensions={0} | all-to-all | bytes 393216 | tf_op jit(solution)/shard_map/all_to_all | solution.py:28
  170.4 0.6 slice.66
  171.1 0.7 slice_bitcast_fusion
  (38 shorter events, 0.2 us)
Async XLA Ops:
  7.2 36.0 %copy-start = (bf16[128,256]{1,0:T(8,128)(2,1)S(1)}, bf16[128,256]{1,0:T(8,128)(2,1)}, u32[]{:S(2)}) copy-start(bf16[128,256]{1,0:T(8,128)(2,1)} %param.13) | copy-start | bytes 196612
  7.2 10.3 %collective-permute-start.7 = (bf16[64,512]{1,0:T(8,128)(2,1)}, bf16[64,512]{1,0:T(8,128)(2,1)S(1)}, u32[]{:S(2)}, u32[]{:S(2)}) collective-permute-start(bf16[64,512]{1,0:T(8,128)(2,1)} %bitcast.64), channel_id=1, source_target_pairs={{0,2},{2,0},{1,3},{3,1},{4,6},{6,4},{5,7},{7,5},{8,10},{10,8},{9,1... | collective-permute-start | bytes 196616 | tf_op jit(solution)/shard_map/ppermute | solution.py:24
  10.1 1.0 copy-start.4
  11.1 6.4 %copy-start.8 = (bf16[512,64]{0,1:T(8,128)(2,1)S(1)}, bf16[512,64]{0,1:T(8,128)(2,1)}, u32[]{:S(2)}) copy-start(bf16[512,64]{0,1:T(8,128)(2,1)} %param.16) | copy-start | bytes 196612
  12.2 5.2 %all-to-all-start.1 = ((bf16[2,4,16,2048]{3,2,1,0:T(8,128)(2,1)}), bf16[2,4,16,2048]{3,2,1,0:T(8,128)(2,1)S(1)}, u32[]{:S(2)}, u32[]{:S(2)}) async-start(bf16[2,4,16,2048]{3,2,1,0:T(8,128)(2,1)} %bitcast.10), calls=%async_computation.1 | async-start | bytes 1048576 | tf_op jit(solution)/shard_map/all_to_all | solution.py:28
  15.7 76.4 %all-gather.3.cloned.1.call-start = ((), (), s32[]{:S(2)}) async-start(), calls=%async_computation.4 | async-start | bytes 5898240 | tf_op jit(solution)/shard_map/all_gather | solution.py:331
  18.5 2.2 %copy-start.3 = (bf16[128,16384]{1,0:T(8,128)(2,1)S(1)}, bf16[128,16384]{1,0:T(8,128)(2,1)}, u32[]{:S(2)}) copy-start(bf16[128,16384]{1,0:T(8,128)(2,1)} %x_ref.1) | copy-start | bytes 12582916
  20.7 16.6 %copy-start.9 = (s32[1,4096]{1,0:T(1,128)S(1)}, s32[1,4096]{1,0:T(1,128)}, u32[]{:S(2)}) copy-start(s32[1,4096]{1,0:T(1,128)} %param.19) | copy-start | bytes 49156
  20.7 16.6 %copy-start.12 = (s32[2]{0:T(128)S(1)}, s32[2]{0:T(128)}, u32[]{:S(2)}) copy-start(s32[2]{0:T(128)} %param.18) | copy-start | bytes 28
  20.7 17.2 %copy-start.10 = (s32[4]{0:T(128)S(1)}, s32[4]{0:T(128)}, u32[]{:S(2)}) copy-start(s32[4]{0:T(128)} %param.15) | copy-start | bytes 52
  20.7 18.4 %copy-start.13 = (pred[128]{0:T(512)(128)(4,1)S(1)}, pred[128]{0:T(512)(128)(4,1)}, u32[]{:S(2)}) copy-start(pred[128]{0:T(512)(128)(4,1)} %constant.312) | copy-start | bytes 388
  20.7 19.9 %copy-start.11 = (s32[2,128]{1,0:T(2,128)S(1)}, s32[2,128]{1,0:T(2,128)}, u32[]{:S(2)}) copy-start(s32[2,128]{1,0:T(2,128)} %constant.293.clone.1) | copy-start | bytes 3076
  24.3 67.8 %copy-start.1 = (bf16[2,2,64,2048]{3,2,1,0:T(8,128)(2,1)}, bf16[2,2,64,2048]{3,2,1,0:T(8,128)(2,1)S(1)}, u32[]{:S(2)}) copy-start(bf16[2,2,64,2048]{3,2,1,0:T(8,128)(2,1)S(1)} %get-tuple-element.50) | copy-start | bytes 3145732
  24.3 18.8 %collective-permute-start = (bf16[4,64,2048]{2,1,0:T(8,128)(2,1)}, bf16[4,64,2048]{2,1,0:T(8,128)(2,1)S(1)}, u32[]{:S(2)}, u32[]{:S(2)}) collective-permute-start(bf16[4,64,2048]{2,1,0:T(8,128)(2,1)} %bitcast.3), channel_id=1, source_target_pairs={{0,1},{1,0},{2,3},{3,2},{4,5},{5,4},{6,7},{7,6},{8,9},{9,8},{10,11... | collective-permute-start | bytes 3145736 | tf_op jit(solution)/shard_map/ppermute | solution.py:24
  26.4 38.5 %collective-permute-start.3 = (bf16[4,64,2048]{2,1,0:T(8,128)(2,1)S(1)}, bf16[4,64,2048]{2,1,0:T(8,128)(2,1)}, u32[]{:S(2)}, u32[]{:S(2)}) collective-permute-start(bf16[4,64,2048]{2,1,0:T(8,128)(2,1)S(1)} %bitcast.48), channel_id=1, source_target_pairs={{0,2},{2,32},{32,34},{34,0},{1,3},{3,33},{33,35},{35,1},{4,6},{6,3... | collective-permute-start | bytes 3145736 | tf_op jit(solution)/shard_map/ppermute | solution.py:24
  33.3 9.8 %collective-permute-start.1 = (bf16[4,64,2048]{2,1,0:T(8,128)(2,1)}, bf16[4,64,2048]{2,1,0:T(8,128)(2,1)}, u32[]{:S(2)}, u32[]{:S(2)}) collective-permute-start(bf16[4,64,2048]{2,1,0:T(8,128)(2,1)} %bitcast.4), channel_id=1, source_target_pairs={{0,1},{1,0},{2,3},{3,2},{4,5},{5,4},{6,7},{7,6},{8,9},{9,8},{10,11... | collective-permute-start | bytes 3145736 | tf_op jit(solution)/shard_map/ppermute | solution.py:24
  35.3 29.6 %collective-permute-start.4 = (bf16[4,64,2048]{2,1,0:T(8,128)(2,1)S(1)}, bf16[4,64,2048]{2,1,0:T(8,128)(2,1)}, u32[]{:S(2)}, u32[]{:S(2)}) collective-permute-start(bf16[4,64,2048]{2,1,0:T(8,128)(2,1)S(1)} %bitcast.51), channel_id=1, source_target_pairs={{0,34},{2,0},{32,2},{34,32},{1,35},{3,1},{33,3},{35,33},{4,38},{6,... | collective-permute-start | bytes 3145736 | tf_op jit(solution)/shard_map/ppermute | solution.py:24
  44.0 17.5 %all-to-all-start = ((bf16[32,4,256]{2,1,0:T(4,128)(2,1)}), bf16[32,4,256]{2,1,0:T(4,128)(2,1)S(1)}, u32[]{:S(2)}, u32[]{:S(2)}) async-start(bf16[32,4,256]{2,1,0:T(4,128)(2,1)} %all_to_all.17), calls=%async_computation | async-start | bytes 131072 | tf_op jit(solution)/shard_map/all_to_all | solution.py:28
  49.7 42.5 %collective-permute-start.6 = (bf16[4,64,2048]{2,1,0:T(8,128)(2,1)S(1)}, bf16[4,64,2048]{2,1,0:T(8,128)(2,1)}, u32[]{:S(2)}, u32[]{:S(2)}) collective-permute-start(bf16[4,64,2048]{2,1,0:T(8,128)(2,1)S(1)} %collective-permute-done.refs_1_), channel_id=1, source_target_pairs={{0,2},{2,32},{32,34},{34,0},{1,3},{3,33},{33,35},{35,1},{4,6},{6,3... | collective-permute-start | bytes 3145736 | tf_op jit(solution)/shard_map/ppermute | solution.py:24
  53.0 39.2 %collective-permute-start.5 = (bf16[4,64,2048]{2,1,0:T(8,128)(2,1)}, bf16[4,64,2048]{2,1,0:T(8,128)(2,1)}, u32[]{:S(2)}, u32[]{:S(2)}) collective-permute-start(bf16[4,64,2048]{2,1,0:T(8,128)(2,1)} %collective-permute-done.1.refs_7_), channel_id=1, source_target_pairs={{0,34},{2,0},{32,2},{34,32},{1,35},{3,1},{33,3},{35,33},{4,38},{6,... | collective-permute-start | bytes 3145736 | tf_op jit(solution)/shard_map/ppermute | solution.py:24
  61.7 3.1 %collective-permute-start.2 = (bf16[128,256]{1,0:T(8,128)(2,1)S(1)}, bf16[128,256]{1,0:T(8,128)(2,1)S(1)}, u32[]{:S(2)}, u32[]{:S(2)}) collective-permute-start(bf16[128,256]{1,0:T(8,128)(2,1)S(1)} %convolution_convert_fusion), channel_id=1, source_target_pairs={{0,1},{1,0},{2,3},{3,2},{4,5},{5,4},{6,7},{7,6},{8,9},{9,8},{10,11... | collective-permute-start | bytes 196616 | tf_op jit(solution)/shard_map/ppermute | solution.py:24
  64.9 15.2 %collective-permute-start.9 = (bf16[128,256]{1,0:T(8,128)(2,1)S(1)}, bf16[128,256]{1,0:T(8,128)(2,1)S(1)}, u32[]{:S(2)}, u32[]{:S(2)}) collective-permute-start(bf16[128,256]{1,0:T(8,128)(2,1)S(1)} %get-tuple-element.57.a_ref), channel_id=1, source_target_pairs={{0,2},{2,32},{32,34},{34,0},{1,3},{3,33},{33,35},{35,1},{4,6},{6,3... | collective-permute-start | bytes 196616 | tf_op jit(solution)/shard_map/ppermute | solution.py:24
  71.3 16.5 %collective-permute-start.8 = (bf16[128,256]{1,0:T(8,128)(2,1)S(1)}, bf16[128,256]{1,0:T(8,128)(2,1)S(1)}, u32[]{:S(2)}, u32[]{:S(2)}) collective-permute-start(bf16[128,256]{1,0:T(8,128)(2,1)S(1)} %get-tuple-element.60.b_ref), channel_id=1, source_target_pairs={{0,34},{2,0},{32,2},{34,32},{1,35},{3,1},{33,3},{35,33},{4,38},{6,... | collective-permute-start | bytes 196616 | tf_op jit(solution)/shard_map/ppermute | solution.py:24
  87.8 0.6 copy-start.5
  92.1 12.5 %copy-start.6 = (bf16[128,256]{1,0:T(8,128)(2,1)S(1)}, bf16[128,256]{1,0:T(8,128)(2,1)}, u32[]{:S(2)}) copy-start(bf16[128,256]{1,0:T(8,128)(2,1)} %copy-done.5) | copy-start | bytes 196612
  92.1 12.5 %copy-start.7 = (bf16[64,256]{1,0:T(8,128)(2,1)S(1)}, bf16[64,256]{1,0:T(8,128)(2,1)}, u32[]{:S(2)}) copy-start(bf16[64,256]{1,0:T(8,128)(2,1)} %up_ref.1) | copy-start | bytes 98308
  100.3 16.0 %copy-start.2 = (bf16[2,2,64,2048]{3,2,1,0:T(8,128)(2,1)S(1)}, bf16[2,2,64,2048]{3,2,1,0:T(8,128)(2,1)}, u32[]{:S(2)}) copy-start(bf16[2,2,64,2048]{3,2,1,0:T(8,128)(2,1)} %copy-done.1) | copy-start | bytes 3145732
  100.4 4.3 %collective-permute-start.10 = (f32[512,384]{1,0:T(8,128)S(1)}, f32[512,384]{1,0:T(8,128)S(1)}, u32[]{:S(2)}, u32[]{:S(2)}) collective-permute-start(f32[512,384]{1,0:T(8,128)S(1)} %products.1.mine_ref), channel_id=1, source_target_pairs={{0,1},{1,0},{2,3},{3,2},{4,5},{5,4},{6,7},{7,6},{8,9},{9,8},{10,11... | collective-permute-start | bytes 2359304 | tf_op jit(solution)/shard_map/ppermute | solution.py:24
  105.5 10.8 %collective-permute-start.12 = (f32[256,128]{1,0:T(8,128)S(1)}, f32[256,128]{1,0:T(8,128)S(1)}, u32[]{:S(2)}, u32[]{:S(2)}) collective-permute-start(f32[256,128]{1,0:T(8,128)S(1)} %get-tuple-element.62.refs_8_), channel_id=1, source_target_pairs={{0,2},{2,32},{32,34},{34,0},{1,3},{3,33},{33,35},{35,1},{4,6},{6,3... | collective-permute-start | bytes 393224 | tf_op jit(solution)/shard_map/ppermute | solution.py:24
  108.0 8.4 %collective-permute-start.11 = (f32[256,64]{1,0:T(8,128)S(1)}, f32[256,64]{1,0:T(8,128)S(1)}, u32[]{:S(2)}, u32[]{:S(2)}) collective-permute-start(f32[256,64]{1,0:T(8,128)S(1)} %get-tuple-element.63.refs_9_), channel_id=1, source_target_pairs={{0,34},{2,0},{32,2},{34,32},{1,35},{3,1},{33,3},{35,33},{4,38},{6,... | collective-permute-start | bytes 196616 | tf_op jit(solution)/shard_map/ppermute | solution.py:24
Sparse Core Ops, SparseCore 0:
  18.6 73.4 all-gather.2

commit v6 on v5

--- a/solution.py
+++ b/solution.py
@@ -65,32 +65,38 @@
     return [part.reshape(2 * (ys // 4), half, 4 * block) for part in parts]
 
 
-def split_weights_kernel(w_ref, out_ref, *, block):
-    spans, _, units, _ = w_ref.shape
-    rows = jnp.concatenate(
-        [w_ref[s, j].astype(F32) for j in range(2) for s in range(spans)], axis=0
-    ).astype(BF16)
-    for parity in range(2):
-        for xl in range(2):
-            for y in range(4):
-                at = ((y * 2 + xl) * 2 + parity) * block
-                out_ref[parity, xl, 0, :, y * block : (y + 1) * block] = rows[:, at : at + block]
-
-
-def split_weights(w, ys, block):
+def split_weights_kernel(core_ref, w_ref, mine_ref, other_ref, *, block):
+    spans = w_ref.shape[0]
+    first = core_ref[0] == 0
+    rows = jnp.concatenate([w_ref[s, j].astype(F32) for j in range(2) for s in range(spans)], axis=0)
+    for xl in range(2):
+        for y in range(4):
+            at = (y * 2 + xl) * 2 * block
+            even, odd = rows[:, at : at + block], rows[:, at + block : at + 2 * block]
+            lanes = slice(y * block, (y + 1) * block)
+            mine_ref[xl, 0, :, lanes] = jnp.where(first, even, odd).astype(BF16)
+            other_ref[xl, 0, :, lanes] = jnp.where(first, odd, even).astype(BF16)
+
+
+def split_weights(w, core, ys, block):
     spans, _, units, width = w.shape
     n = 2 * spans * units
-    out = pl.pallas_call(
+    spec = pl.BlockSpec((2, 1, n, 4 * block), lambda y, c: (0, y, 0, 0))
+    shape = jax.ShapeDtypeStruct((2, ys // 4, n, 4 * block), BF16)
+    parts = pl.pallas_call(
         functools.partial(split_weights_kernel, block=block),
-        grid=(ys // 4,),
-        in_specs=[pl.BlockSpec((spans, 2, units, 16 * block), lambda y: (0, 0, 0, y))],
-        out_specs=pl.BlockSpec((2, 2, 1, n, 4 * block), lambda y: (0, 0, y, 0, 0)),
-        out_shape=jax.ShapeDtypeStruct((2, 2, ys // 4, n, 4 * block), BF16),
+        grid_spec=pltpu.PrefetchScalarGridSpec(
+            num_scalar_prefetch=1,
+            grid=(ys // 4,),
+            in_specs=[pl.BlockSpec((spans, 2, units, 16 * block), lambda y, c: (0, 0, 0, y))],
+            out_specs=[spec, spec],
+        ),
+        out_shape=[shape, shape],
         compiler_params=params(24),
         cost_estimate=pl.CostEstimate(flops=0, bytes_accessed=w.size * 4, transcendentals=0),
         name="split_weights",
-    )(w)
-    return out.reshape(2, 2 * (ys // 4), n, 4 * block)
+    )(core, w)
+    return [part.reshape(2 * (ys // 4), n, 4 * block) for part in parts]
 
 
 def products_kernel(*refs, block, rank, n):
@@ -312,7 +318,9 @@
     core_id = core.astype(jnp.int32).reshape(1)
     xl_id = xl.astype(jnp.int32).reshape(1)
 
-    swapped = exchange(split_weights(frozen, ys, block), "core")
+    mine, other = split_weights(frozen, core_id, ys, block)
+    other = shift(other, "core", 1)
+    swapped = jnp.where(core == 0, jnp.stack([mine, other]), jnp.stack([other, mine]))
     chunks = swapped.shape[1]
     near = shift(down.T, "xl", 1)
     both_down = jnp.concatenate(

time: 181 us -> 178 us (0.983)
  starting transfers between devices: 48.9 us -> 46.9 us
    all_to_all x2 -> x1, starting transfers between devices: 9.19 us -> 5.32 us  [exchange(): return lax.all_to_all(array, axes, split_axis=0, concat_axis=0, tiled=True)]
    ppermute x13 -> x14, starting transfers between devices: 39.7 us -> 41.6 us  [shift(): lax.ppermute(array, axes, [(i, (i + step) % size) for i in range(size)])]
    all_to_all x2 -> x1, waiting for transfers between devices: 7.02 us -> 5.69 us  [exchange(): return lax.all_to_all(array, axes, split_axis=0, concat_axis=0, tiled=True)]
    ppermute x13 -> x14, waiting for transfers between devices: 22.2 us -> 23.2 us  [shift(): lax.ppermute(array, axes, [(i, (i + step) % size) for i in range(size)])]
    unnamed x28 -> x26, local copies, waits for them, and re-layouts: 3.9 us -> 3.89 us
  transfers between devices with their start and end apart: 16 -> 16, of which waited for: 8 -> 9; matrix products, arithmetic and copies ran while one was open for 4% -> 5% of each run, Pallas kernels for 3% -> 2%
where the time goes in v6:
time: 178 us; the launch traced here: 176 us
  blocking collectives  50.5 us (28%)
  starting transfers between devices  46.9 us (26%)
  waiting for transfers between devices  32.2 us (18%)
  Pallas kernels  16.5 us (9%)
  between operations  14.5 us (8%)
  other arithmetic  7.77 us (4%)
  local copies, waits for them, and re-layouts  7.2 us (4%)
    all_to_all x2, blocking collectives, exchange(): return lax.all_to_all(array, axes, split_axis=0, concat_axis=0, tiled=True)  50.5 us
    ppermute x14, starting transfers between devices, shift(): lax.ppermute(array, axes, [(i, (i + step) % size) for i in range(size)])  41.6 us
    ppermute x14, waiting for transfers between devices, shift(): lax.ppermute(array, axes, [(i, (i + step) % size) for i in range(size)])  23.2 us
    pallas_call x1, Pallas kernels, products(): pl.pallas_call(functools.partial(products_kernel, block=block, rank=rank,...  8.18 us
    all_to_all x1, waiting for transfers between devices, exchange(): return lax.all_to_all(array, axes, split_axis=0, concat_axis=0, tiled=True)  5.69 us
    all_to_all x1, starting transfers between devices, exchange(): return lax.all_to_all(array, axes, split_axis=0, concat_axis=0, tiled=True)  5.32 us
    unnamed x26, local copies, waits for them, and re-layouts  3.89 us
    pallas_call x1, Pallas kernels, split_rows(): pl.pallas_call(functools.partial(split_rows_kernel, block=block), grid_sp...  3.57 us
  transfers between devices with their start and end apart: 16, of which 9 were waited for; matrix products, arithmetic and copies ran while one was open for 5% of the time, Pallas kernels for 2%

profile of v6, /device:TPU:6, one launch (start us, length us, event | category | flops | bytes accessed | tf_op | source)
XLA Modules:
  0.0 175.9 jit_solution(15114867416779053920)
XLA Ops:
  7.2 0.0 copy-start
  7.2 0.0 all-gather.3.cloned.1.call-start
  7.2 2.7 %collective-permute-start.8 = (bf16[64,512]{1,0:T(8,128)(2,1)}, bf16[64,512]{1,0:T(8,128)(2,1)S(1)}, u32[]{:S(2)}, u32[]{:S(2)}) collective-permute-start(bf16[64,512]{1,0:T(8,128)(2,1)} %bitcast.69), channel_id=1, source_target_pairs={{0,2},{2,0},{1,3},{3,1},{4,6},{6,4},{5,7},{7,5},{8,10},{10,8},{9,1... | collective-permute-start | bytes 196616 | tf_op jit(solution)/shard_map/ppermute | solution.py:24
  10.0 1.0 copy-done.4
  11.0 0.5 split_weights.1
  11.5 1.9 %collective-permute-start.7 = (bf16[4,16,2048]{2,1,0:T(8,128)(2,1)S(1)}, bf16[4,16,2048]{2,1,0:T(8,128)(2,1)S(1)}, u32[]{:S(2)}, u32[]{:S(2)}) collective-permute-start(bf16[4,16,2048]{2,1,0:T(8,128)(2,1)S(1)} %bitcast.59), channel_id=1, source_target_pairs={{0,1},{1,0},{2,3},{3,2},{4,5},{5,4},{6,7},{7,6},{8,9},{9,8},{10,11... | collective-permute-start | bytes 786440 | tf_op jit(solution)/shard_map/ppermute | solution.py:24
  13.4 0.1 collective-permute-done.8
  13.6 0.9 broadcast_select_fusion.1
  14.5 0.5 collective-permute-done.7
  14.9 0.1 fusion
  15.1 0.9 pad_maximum_fusion
  16.0 0.0 all-gather.3.cloned.1.call-update
  16.0 0.0 copy-start.3
  16.0 2.2 %copy-done.3 = bf16[128,16384]{1,0:T(8,128)(2,1)S(1)} copy-done((bf16[128,16384]{1,0:T(8,128)(2,1)S(1)}, bf16[128,16384]{1,0:T(8,128)(2,1)}, u32[]{:S(2)}) %copy-start.3) | copy-done | bytes 4194328
  18.2 0.0 copy-start.10
  18.2 3.6 %split_rows.1 = (bf16[2,2,64,2048]{3,2,1,0:T(8,128)(2,1)S(1)}, bf16[2,2,64,2048]{3,2,1,0:T(8,128)(2,1)S(1)}, bf16[2,2,64,2048]{3,2,1,0:T(8,128)(2,1)}, bf16[2,2,64,2048]{3,2,1,0:T(8,128)(2,1)}) custom-call(s32[1]{0:T(128)} %bitcast.1.core_ref, bf16[128,16384]{1,0:T(8,128)(2,1)S(1)} %copy-done.3), custom_call_target="tpu_custom_call" | custom-call | bytes 8388608 | tf_op jit(solution)/shard_map/split_rows/pallas_call | solution.py:52
  21.8 2.0 %collective-permute-start = (bf16[4,64,2048]{2,1,0:T(8,128)(2,1)}, bf16[4,64,2048]{2,1,0:T(8,128)(2,1)S(1)}, u32[]{:S(2)}, u32[]{:S(2)}) collective-permute-start(bf16[4,64,2048]{2,1,0:T(8,128)(2,1)} %bitcast.3), channel_id=1, source_target_pairs={{0,1},{1,0},{2,3},{3,2},{4,5},{5,4},{6,7},{7,6},{8,9},{9,8},{10,11... | collective-permute-start | bytes 3145736 | tf_op jit(solution)/shard_map/ppermute | solution.py:24
  23.8 7.2 %collective-permute-start.3 = (bf16[4,64,2048]{2,1,0:T(8,128)(2,1)S(1)}, bf16[4,64,2048]{2,1,0:T(8,128)(2,1)}, u32[]{:S(2)}, u32[]{:S(2)}) collective-permute-start(bf16[4,64,2048]{2,1,0:T(8,128)(2,1)S(1)} %bitcast.51), channel_id=1, source_target_pairs={{0,2},{2,32},{32,34},{34,0},{1,3},{3,33},{33,35},{35,1},{4,6},{6,3... | collective-permute-start | bytes 3145736 | tf_op jit(solution)/shard_map/ppermute | solution.py:24
  31.0 2.1 %collective-permute-start.1 = (bf16[4,64,2048]{2,1,0:T(8,128)(2,1)}, bf16[4,64,2048]{2,1,0:T(8,128)(2,1)}, u32[]{:S(2)}, u32[]{:S(2)}) collective-permute-start(bf16[4,64,2048]{2,1,0:T(8,128)(2,1)} %bitcast.4), channel_id=1, source_target_pairs={{0,1},{1,0},{2,3},{3,2},{4,5},{5,4},{6,7},{7,6},{8,9},{9,8},{10,11... | collective-permute-start | bytes 3145736 | tf_op jit(solution)/shard_map/ppermute | solution.py:24
  33.2 1.9 %collective-permute-start.4 = (bf16[4,64,2048]{2,1,0:T(8,128)(2,1)S(1)}, bf16[4,64,2048]{2,1,0:T(8,128)(2,1)}, u32[]{:S(2)}, u32[]{:S(2)}) collective-permute-start(bf16[4,64,2048]{2,1,0:T(8,128)(2,1)S(1)} %bitcast.54), channel_id=1, source_target_pairs={{0,34},{2,0},{32,2},{34,32},{1,35},{3,1},{33,3},{35,33},{4,38},{6,... | collective-permute-start | bytes 3145736 | tf_op jit(solution)/shard_map/ppermute | solution.py:24
  35.1 0.6 fusion.26
  35.7 0.7 fusion.25
  36.4 0.2 convert_reduce_fusion.2
  36.6 0.4 select_reduce_fusion
  37.0 1.2 fusion.22
  38.2 0.2 convert_reduce_fusion.1
  38.4 0.1 add_add_fusion.1
  38.4 2.5 %compare_select_fusion.1 = s32[256,1]{0,1:T(1,128)S(1)} fusion(s32[256,1]{0,1:T(1,128)S(1)} %bitcast.73, s32[256,1]{0,1:T(1,128)S(1)} %bitcast.72, s32[]{:T(128)} %bitcast.25, s32[]{:T(128)} %bitcast.26, s32[]{:T(128)} %bitcast.28, s32[]{:T(128)} %bitcast.27), kind=kLoop, calls=%fused_computation.31 | loop fusion | flops 2048 | bytes 3088 | tf_op jit(solution)/shard_map/jit(_take)/gather | solution.py:301
  40.9 0.1 and_select_fusion.7
  41.0 0.0 collective-permute-done.refs_1_
  41.0 0.0 collective-permute-done.1.refs_7_
  41.0 0.2 convolution_convert_fusion.1
  41.2 0.7 all_to_all.14
  41.8 5.3 %all-to-all-start = ((bf16[32,4,256]{2,1,0:T(4,128)(2,1)}), bf16[32,4,256]{2,1,0:T(4,128)(2,1)S(1)}, u32[]{:S(2)}, u32[]{:S(2)}) async-start(bf16[32,4,256]{2,1,0:T(4,128)(2,1)} %all_to_all.14), calls=%async_computation | async-start | bytes 131072 | tf_op jit(solution)/shard_map/all_to_all | solution.py:28
  47.2 3.7 %collective-permute-start.6 = (bf16[4,64,2048]{2,1,0:T(8,128)(2,1)S(1)}, bf16[4,64,2048]{2,1,0:T(8,128)(2,1)}, u32[]{:S(2)}, u32[]{:S(2)}) collective-permute-start(bf16[4,64,2048]{2,1,0:T(8,128)(2,1)S(1)} %collective-permute-done.refs_1_), channel_id=1, source_target_pairs={{0,2},{2,32},{32,34},{34,0},{1,3},{3,33},{33,35},{35,1},{4,6},{6,3... | collective-permute-start | bytes 3145736 | tf_op jit(solution)/shard_map/ppermute | solution.py:24
  50.9 2.2 %collective-permute-start.5 = (bf16[4,64,2048]{2,1,0:T(8,128)(2,1)}, bf16[4,64,2048]{2,1,0:T(8,128)(2,1)}, u32[]{:S(2)}, u32[]{:S(2)}) collective-permute-start(bf16[4,64,2048]{2,1,0:T(8,128)(2,1)} %collective-permute-done.1.refs_7_), channel_id=1, source_target_pairs={{0,34},{2,0},{32,2},{34,32},{1,35},{3,1},{33,3},{35,33},{4,38},{6,... | collective-permute-start | bytes 3145736 | tf_op jit(solution)/shard_map/ppermute | solution.py:24
  53.0 0.5 fusion.18
  53.5 5.7 %all-to-all-done = bf16[32,4,256]{2,1,0:T(4,128)(2,1)S(1)} async-done(((bf16[32,4,256]{2,1,0:T(4,128)(2,1)}), bf16[32,4,256]{2,1,0:T(4,128)(2,1)S(1)}, u32[]{:S(2)}, u32[]{:S(2)}) %all-to-all-start) | async-done | bytes 65568 | tf_op jit(solution)/shard_map/all_to_all | solution.py:28
  59.3 0.2 convolution_convert_fusion
  59.5 1.9 %collective-permute-start.2 = (bf16[128,256]{1,0:T(8,128)(2,1)S(1)}, bf16[128,256]{1,0:T(8,128)(2,1)S(1)}, u32[]{:S(2)}, u32[]{:S(2)}) collective-permute-start(bf16[128,256]{1,0:T(8,128)(2,1)S(1)} %convolution_convert_fusion), channel_id=1, source_target_pairs={{0,1},{1,0},{2,3},{3,2},{4,5},{5,4},{6,7},{7,6},{8,9},{9,8},{10,11... | collective-permute-start | bytes 196616 | tf_op jit(solution)/shard_map/ppermute | solution.py:24
  61.4 1.2 collective-permute-done.2
  62.6 0.0 collective-permute-done.3.refs_4_
  62.7 0.0 collective-permute-done.4.refs_2_
  62.7 6.0 %collective-permute-start.10 = (bf16[128,256]{1,0:T(8,128)(2,1)S(1)}, bf16[128,256]{1,0:T(8,128)(2,1)S(1)}, u32[]{:S(2)}, u32[]{:S(2)}) collective-permute-start(bf16[128,256]{1,0:T(8,128)(2,1)S(1)} %get-tuple-element.61.a_ref), channel_id=1, source_target_pairs={{0,2},{2,32},{32,34},{34,0},{1,3},{3,33},{33,35},{35,1},{4,6},{6,3... | collective-permute-start | bytes 196616 | tf_op jit(solution)/shard_map/ppermute | solution.py:24
  68.7 1.9 %collective-permute-start.9 = (bf16[128,256]{1,0:T(8,128)(2,1)S(1)}, bf16[128,256]{1,0:T(8,128)(2,1)S(1)}, u32[]{:S(2)}, u32[]{:S(2)}) collective-permute-start(bf16[128,256]{1,0:T(8,128)(2,1)S(1)} %get-tuple-element.64.b_ref), channel_id=1, source_target_pairs={{0,34},{2,0},{32,2},{34,32},{1,35},{3,1},{33,3},{35,33},{4,38},{6,... | collective-permute-start | bytes 196616 | tf_op jit(solution)/shard_map/ppermute | solution.py:24
  70.6 0.7 and_convert_fusion.pick_ref
  71.4 6.6 %collective-permute-done.10.prev_a_ref = bf16[128,256]{1,0:T(8,128)(2,1)S(1)} collective-permute-done((bf16[128,256]{1,0:T(8,128)(2,1)S(1)}, bf16[128,256]{1,0:T(8,128)(2,1)S(1)}, u32[]{:S(2)}, u32[]{:S(2)}) %collective-permute-start.10) | collective-permute-done | bytes 65568 | tf_op jit(solution)/shard_map/ppermute | solution.py:24
  78.0 7.5 %collective-permute-done.9.next_b_ref = bf16[128,256]{1,0:T(8,128)(2,1)S(1)} collective-permute-done((bf16[128,256]{1,0:T(8,128)(2,1)S(1)}, bf16[128,256]{1,0:T(8,128)(2,1)S(1)}, u32[]{:S(2)}, u32[]{:S(2)}) %collective-permute-start.9) | collective-permute-done | bytes 65568 | tf_op jit(solution)/shard_map/ppermute | solution.py:24
  85.5 0.6 copy-done.5
  86.1 3.4 %all-gather.3.cloned.1.call-done = bf16[1280,2048]{1,0:T(8,128)(2,1)} async-done(((bf16[160,2048]{1,0:T(8,128)(2,1)}), bf16[1280,2048]{1,0:T(8,128)(2,1)}) %all-gather.3.cloned.1.call-update) | async-done | bytes 5242896 | tf_op jit(solution)/shard_map/all_gather | solution.py:339
  89.5 0.0 collective-permute-done.6.refs_5_
  89.5 8.2 %products.1.mine_ref = f32[512,384]{1,0:T(8,128)S(1)} custom-call(bf16[4,64,2048]{2,1,0:T(8,128)(2,1)S(1)} %bitcast.52, bf16[4,64,2048]{2,1,0:T(8,128)(2,1)S(1)} %collective-permute-done.refs_1_, bf16[4,64,2048]{2,1,0:T(8,128)(2,1)} %collective-permute-done.4.refs_2_, bf16[4,64,2048]{2,1,0:T(8,128)(2,1)} %collective-permute-done.5.refs_3_, ...), custom_call_target="tpu_custom_call" | custom-call | flops 2684354560 | bytes 13631488 | tf_op jit(solution)/shard_map/products/pallas_call | solution.py:154
  97.7 2.1 %collective-permute-start.11 = (f32[512,384]{1,0:T(8,128)S(1)}, f32[512,384]{1,0:T(8,128)S(1)}, u32[]{:S(2)}, u32[]{:S(2)}) collective-permute-start(f32[512,384]{1,0:T(8,128)S(1)} %products.1.mine_ref), channel_id=1, source_target_pairs={{0,1},{1,0},{2,3},{3,2},{4,5},{5,4},{6,7},{7,6},{8,9},{9,8},{10,11... | collective-permute-start | bytes 2359304 | tf_op jit(solution)/shard_map/ppermute | solution.py:24
  99.8 2.3 %collective-permute-done.11.his_ref = f32[512,384]{1,0:T(8,128)S(1)} collective-permute-done((f32[512,384]{1,0:T(8,128)S(1)}, f32[512,384]{1,0:T(8,128)S(1)}, u32[]{:S(2)}, u32[]{:S(2)}) %collective-permute-start.11) | collective-permute-done | bytes 786464 | tf_op jit(solution)/shard_map/ppermute | solution.py:24
  102.0 0.9 gate_stage.1
  102.9 2.4 %collective-permute-start.13 = (f32[256,128]{1,0:T(8,128)S(1)}, f32[256,128]{1,0:T(8,128)S(1)}, u32[]{:S(2)}, u32[]{:S(2)}) collective-permute-start(f32[256,128]{1,0:T(8,128)S(1)} %get-tuple-element.66.refs_8_), channel_id=1, source_target_pairs={{0,2},{2,32},{32,34},{34,0},{1,3},{3,33},{33,35},{35,1},{4,6},{6,3... | collective-permute-start | bytes 393224 | tf_op jit(solution)/shard_map/ppermute | solution.py:24
  105.3 3.4 %collective-permute-start.12 = (f32[256,64]{1,0:T(8,128)S(1)}, f32[256,64]{1,0:T(8,128)S(1)}, u32[]{:S(2)}, u32[]{:S(2)}) collective-permute-start(f32[256,64]{1,0:T(8,128)S(1)} %get-tuple-element.67.refs_9_), channel_id=1, source_target_pairs={{0,34},{2,0},{32,2},{34,32},{1,35},{3,1},{33,3},{35,33},{4,38},{6,... | collective-permute-start | bytes 196616 | tf_op jit(solution)/shard_map/ppermute | solution.py:24
  108.8 5.0 %collective-permute-done.12.refs_10_ = f32[256,64]{1,0:T(8,128)S(1)} collective-permute-done((f32[256,64]{1,0:T(8,128)S(1)}, f32[256,64]{1,0:T(8,128)S(1)}, u32[]{:S(2)}, u32[]{:S(2)}) %collective-permute-start.12) | collective-permute-done | bytes 65568 | tf_op jit(solution)/shard_map/ppermute | solution.py:24
  113.7 3.4 %down_terms.1 = bf16[8,8,8,768]{3,2,1,0:T(8,128)(2,1)S(1)} custom-call(s32[1]{0:T(128)} %bitcast.xl_ref, bf16[4,64,2048]{2,1,0:T(8,128)(2,1)S(1)} %bitcast.53, bf16[4,64,2048]{2,1,0:T(8,128)(2,1)S(1)} %collective-permute-done.refs_1_, bf16[4,64,2048]{2,1,0:T(8,128)(2,1)} %collective-permute-done.4.refs_2_, ...), custom_call_target="tpu_custom_call" | custom-call | flops 268435456 | bytes 4718592 | tf_op jit(solution)/shard_map/down_terms/pallas_call | solution.py:252
  117.1 34.6 %all_to_all.22 = bf16[64,8,768]{2,1,0:T(8,128)(2,1)S(1)} all-to-all(bf16[64,8,768]{2,1,0:T(8,128)(2,1)S(1)} %bitcast.57), channel_id=1, replica_groups=mesh['z'=8,'xh'=2,'y'=8,'xl'=2,'core'=2] {'z','y'}, dimensions={0} | all-to-all | bytes 1572864 | tf_op jit(solution)/shard_map/all_to_all | solution.py:28
  151.7 0.1 reduce_sum.51
  151.8 15.9 %all_to_all.23 = bf16[16,8,768]{2,1,0:T(8,128)(2,1)S(1)} all-to-all(bf16[16,8,768]{2,1,0:T(8,128)(2,1)S(1)} %tile.2), channel_id=1, replica_groups=mesh['z'=8,'xh'=2,'y'=8,'xl'=2,'core'=2] {'z','xh'}, dimensions={0} | all-to-all | bytes 393216 | tf_op jit(solution)/shard_map/all_to_all | solution.py:28
  167.8 0.6 slice.66
  168.4 0.7 slice_bitcast_fusion
  (37 shorter events, 0.2 us)
Async XLA Ops:
  7.2 33.9 %copy-start = (bf16[128,256]{1,0:T(8,128)(2,1)S(1)}, bf16[128,256]{1,0:T(8,128)(2,1)}, u32[]{:S(2)}) copy-start(bf16[128,256]{1,0:T(8,128)(2,1)} %param.13) | copy-start | bytes 196612
  7.2 82.3 %all-gather.3.cloned.1.call-start = ((), (), s32[]{:S(2)}) async-start(), calls=%async_computation.3 | async-start | bytes 5898240 | tf_op jit(solution)/shard_map/all_gather | solution.py:339
  7.2 6.4 %collective-permute-start.8 = (bf16[64,512]{1,0:T(8,128)(2,1)}, bf16[64,512]{1,0:T(8,128)(2,1)S(1)}, u32[]{:S(2)}, u32[]{:S(2)}) collective-permute-start(bf16[64,512]{1,0:T(8,128)(2,1)} %bitcast.69), channel_id=1, source_target_pairs={{0,2},{2,0},{1,3},{3,1},{4,6},{6,4},{5,7},{7,5},{8,10},{10,8},{9,1... | collective-permute-start | bytes 196616 | tf_op jit(solution)/shard_map/ppermute | solution.py:24
  10.0 1.0 copy-start.4
  11.5 3.4 %collective-permute-start.7 = (bf16[4,16,2048]{2,1,0:T(8,128)(2,1)S(1)}, bf16[4,16,2048]{2,1,0:T(8,128)(2,1)S(1)}, u32[]{:S(2)}, u32[]{:S(2)}) collective-permute-start(bf16[4,16,2048]{2,1,0:T(8,128)(2,1)S(1)} %bitcast.59), channel_id=1, source_target_pairs={{0,1},{1,0},{2,3},{3,2},{4,5},{5,4},{6,7},{7,6},{8,9},{9,8},{10,11... | collective-permute-start | bytes 786440 | tf_op jit(solution)/shard_map/ppermute | solution.py:24
  16.0 2.2 %copy-start.3 = (bf16[128,16384]{1,0:T(8,128)(2,1)S(1)}, bf16[128,16384]{1,0:T(8,128)(2,1)}, u32[]{:S(2)}) copy-start(bf16[128,16384]{1,0:T(8,128)(2,1)} %x_ref.1) | copy-start | bytes 12582916
  18.2 16.9 %copy-start.8 = (s32[1,4096]{1,0:T(1,128)S(1)}, s32[1,4096]{1,0:T(1,128)}, u32[]{:S(2)}) copy-start(s32[1,4096]{1,0:T(1,128)} %param.19) | copy-start | bytes 49156
  18.2 17.0 %copy-start.11 = (s32[2]{0:T(128)S(1)}, s32[2]{0:T(128)}, u32[]{:S(2)}) copy-start(s32[2]{0:T(128)} %param.18) | copy-start | bytes 28
  18.2 17.6 %copy-start.9 = (s32[4]{0:T(128)S(1)}, s32[4]{0:T(128)}, u32[]{:S(2)}) copy-start(s32[4]{0:T(128)} %param.15) | copy-start | bytes 52
  18.2 18.8 %copy-start.12 = (pred[128]{0:T(512)(128)(4,1)S(1)}, pred[128]{0:T(512)(128)(4,1)}, u32[]{:S(2)}) copy-start(pred[128]{0:T(512)(128)(4,1)} %constant.312) | copy-start | bytes 388
  18.2 20.2 %copy-start.10 = (s32[2,128]{1,0:T(2,128)S(1)}, s32[2,128]{1,0:T(2,128)}, u32[]{:S(2)}) copy-start(s32[2,128]{1,0:T(2,128)} %constant.293.clone.1) | copy-start | bytes 3076
  21.8 67.7 %copy-start.1 = (bf16[2,2,64,2048]{3,2,1,0:T(8,128)(2,1)}, bf16[2,2,64,2048]{3,2,1,0:T(8,128)(2,1)S(1)}, u32[]{:S(2)}) copy-start(bf16[2,2,64,2048]{3,2,1,0:T(8,128)(2,1)S(1)} %get-tuple-element.52) | copy-start | bytes 3145732
  21.8 19.2 %collective-permute-start = (bf16[4,64,2048]{2,1,0:T(8,128)(2,1)}, bf16[4,64,2048]{2,1,0:T(8,128)(2,1)S(1)}, u32[]{:S(2)}, u32[]{:S(2)}) collective-permute-start(bf16[4,64,2048]{2,1,0:T(8,128)(2,1)} %bitcast.3), channel_id=1, source_target_pairs={{0,1},{1,0},{2,3},{3,2},{4,5},{5,4},{6,7},{7,6},{8,9},{9,8},{10,11... | collective-permute-start | bytes 3145736 | tf_op jit(solution)/shard_map/ppermute | solution.py:24
  23.8 38.8 %collective-permute-start.3 = (bf16[4,64,2048]{2,1,0:T(8,128)(2,1)S(1)}, bf16[4,64,2048]{2,1,0:T(8,128)(2,1)}, u32[]{:S(2)}, u32[]{:S(2)}) collective-permute-start(bf16[4,64,2048]{2,1,0:T(8,128)(2,1)S(1)} %bitcast.51), channel_id=1, source_target_pairs={{0,2},{2,32},{32,34},{34,0},{1,3},{3,33},{33,35},{35,1},{4,6},{6,3... | collective-permute-start | bytes 3145736 | tf_op jit(solution)/shard_map/ppermute | solution.py:24
  31.0 10.0 %collective-permute-start.1 = (bf16[4,64,2048]{2,1,0:T(8,128)(2,1)}, bf16[4,64,2048]{2,1,0:T(8,128)(2,1)}, u32[]{:S(2)}, u32[]{:S(2)}) collective-permute-start(bf16[4,64,2048]{2,1,0:T(8,128)(2,1)} %bitcast.4), channel_id=1, source_target_pairs={{0,1},{1,0},{2,3},{3,2},{4,5},{5,4},{6,7},{7,6},{8,9},{9,8},{10,11... | collective-permute-start | bytes 3145736 | tf_op jit(solution)/shard_map/ppermute | solution.py:24
  33.2 29.5 %collective-permute-start.4 = (bf16[4,64,2048]{2,1,0:T(8,128)(2,1)S(1)}, bf16[4,64,2048]{2,1,0:T(8,128)(2,1)}, u32[]{:S(2)}, u32[]{:S(2)}) collective-permute-start(bf16[4,64,2048]{2,1,0:T(8,128)(2,1)S(1)} %bitcast.54), channel_id=1, source_target_pairs={{0,34},{2,0},{32,2},{34,32},{1,35},{3,1},{33,3},{35,33},{4,38},{6,... | collective-permute-start | bytes 3145736 | tf_op jit(solution)/shard_map/ppermute | solution.py:24
  41.8 17.4 %all-to-all-start = ((bf16[32,4,256]{2,1,0:T(4,128)(2,1)}), bf16[32,4,256]{2,1,0:T(4,128)(2,1)S(1)}, u32[]{:S(2)}, u32[]{:S(2)}) async-start(bf16[32,4,256]{2,1,0:T(4,128)(2,1)} %all_to_all.14), calls=%async_computation | async-start | bytes 131072 | tf_op jit(solution)/shard_map/all_to_all | solution.py:28
  47.2 42.3 %collective-permute-start.6 = (bf16[4,64,2048]{2,1,0:T(8,128)(2,1)S(1)}, bf16[4,64,2048]{2,1,0:T(8,128)(2,1)}, u32[]{:S(2)}, u32[]{:S(2)}) collective-permute-start(bf16[4,64,2048]{2,1,0:T(8,128)(2,1)S(1)} %collective-permute-done.refs_1_), channel_id=1, source_target_pairs={{0,2},{2,32},{32,34},{34,0},{1,3},{3,33},{33,35},{35,1},{4,6},{6,3... | collective-permute-start | bytes 3145736 | tf_op jit(solution)/shard_map/ppermute | solution.py:24
  50.9 38.7 %collective-permute-start.5 = (bf16[4,64,2048]{2,1,0:T(8,128)(2,1)}, bf16[4,64,2048]{2,1,0:T(8,128)(2,1)}, u32[]{:S(2)}, u32[]{:S(2)}) collective-permute-start(bf16[4,64,2048]{2,1,0:T(8,128)(2,1)} %collective-permute-done.1.refs_7_), channel_id=1, source_target_pairs={{0,34},{2,0},{32,2},{34,32},{1,35},{3,1},{33,3},{35,33},{4,38},{6,... | collective-permute-start | bytes 3145736 | tf_op jit(solution)/shard_map/ppermute | solution.py:24
  59.5 3.1 %collective-permute-start.2 = (bf16[128,256]{1,0:T(8,128)(2,1)S(1)}, bf16[128,256]{1,0:T(8,128)(2,1)S(1)}, u32[]{:S(2)}, u32[]{:S(2)}) collective-permute-start(bf16[128,256]{1,0:T(8,128)(2,1)S(1)} %convolution_convert_fusion), channel_id=1, source_target_pairs={{0,1},{1,0},{2,3},{3,2},{4,5},{5,4},{6,7},{7,6},{8,9},{9,8},{10,11... | collective-permute-start | bytes 196616 | tf_op jit(solution)/shard_map/ppermute | solution.py:24
  62.7 15.3 %collective-permute-start.10 = (bf16[128,256]{1,0:T(8,128)(2,1)S(1)}, bf16[128,256]{1,0:T(8,128)(2,1)S(1)}, u32[]{:S(2)}, u32[]{:S(2)}) collective-permute-start(bf16[128,256]{1,0:T(8,128)(2,1)S(1)} %get-tuple-element.61.a_ref), channel_id=1, source_target_pairs={{0,2},{2,32},{32,34},{34,0},{1,3},{3,33},{33,35},{35,1},{4,6},{6,3... | collective-permute-start | bytes 196616 | tf_op jit(solution)/shard_map/ppermute | solution.py:24
  68.7 16.8 %collective-permute-start.9 = (bf16[128,256]{1,0:T(8,128)(2,1)S(1)}, bf16[128,256]{1,0:T(8,128)(2,1)S(1)}, u32[]{:S(2)}, u32[]{:S(2)}) collective-permute-start(bf16[128,256]{1,0:T(8,128)(2,1)S(1)} %get-tuple-element.64.b_ref), channel_id=1, source_target_pairs={{0,34},{2,0},{32,2},{34,32},{1,35},{3,1},{33,3},{35,33},{4,38},{6,... | collective-permute-start | bytes 196616 | tf_op jit(solution)/shard_map/ppermute | solution.py:24
  85.5 0.6 copy-start.5
  89.5 12.5 %copy-start.6 = (bf16[128,256]{1,0:T(8,128)(2,1)S(1)}, bf16[128,256]{1,0:T(8,128)(2,1)}, u32[]{:S(2)}) copy-start(bf16[128,256]{1,0:T(8,128)(2,1)} %copy-done.5) | copy-start | bytes 196612
  89.5 12.5 %copy-start.7 = (bf16[64,256]{1,0:T(8,128)(2,1)S(1)}, bf16[64,256]{1,0:T(8,128)(2,1)}, u32[]{:S(2)}) copy-start(bf16[64,256]{1,0:T(8,128)(2,1)} %up_ref.1) | copy-start | bytes 98308
  97.7 16.0 %copy-start.2 = (bf16[2,2,64,2048]{3,2,1,0:T(8,128)(2,1)S(1)}, bf16[2,2,64,2048]{3,2,1,0:T(8,128)(2,1)}, u32[]{:S(2)}) copy-start(bf16[2,2,64,2048]{3,2,1,0:T(8,128)(2,1)} %copy-done.1) | copy-start | bytes 3145732
  97.7 4.3 %collective-permute-start.11 = (f32[512,384]{1,0:T(8,128)S(1)}, f32[512,384]{1,0:T(8,128)S(1)}, u32[]{:S(2)}, u32[]{:S(2)}) collective-permute-start(f32[512,384]{1,0:T(8,128)S(1)} %products.1.mine_ref), channel_id=1, source_target_pairs={{0,1},{1,0},{2,3},{3,2},{4,5},{5,4},{6,7},{7,6},{8,9},{9,8},{10,11... | collective-permute-start | bytes 2359304 | tf_op jit(solution)/shard_map/ppermute | solution.py:24
  102.9 10.8 %collective-permute-start.13 = (f32[256,128]{1,0:T(8,128)S(1)}, f32[256,128]{1,0:T(8,128)S(1)}, u32[]{:S(2)}, u32[]{:S(2)}) collective-permute-start(f32[256,128]{1,0:T(8,128)S(1)} %get-tuple-element.66.refs_8_), channel_id=1, source_target_pairs={{0,2},{2,32},{32,34},{34,0},{1,3},{3,33},{33,35},{35,1},{4,6},{6,3... | collective-permute-start | bytes 393224 | tf_op jit(solution)/shard_map/ppermute | solution.py:24
  105.3 8.4 %collective-permute-start.12 = (f32[256,64]{1,0:T(8,128)S(1)}, f32[256,64]{1,0:T(8,128)S(1)}, u32[]{:S(2)}, u32[]{:S(2)}) collective-permute-start(f32[256,64]{1,0:T(8,128)S(1)} %get-tuple-element.67.refs_9_), channel_id=1, source_target_pairs={{0,34},{2,0},{32,2},{34,32},{1,35},{3,1},{33,3},{35,33},{4,38},{6,... | collective-permute-start | bytes 196616 | tf_op jit(solution)/shard_map/ppermute | solution.py:24
Sparse Core Ops, SparseCore 0:
  16.1 73.3 all-gather.2
